TPU v7x, 32 devices: a whole 2x2x4 slice. The times are simulated.
32 devices in a mesh: dp: 2 (over y), expert: 16 (over z, x, core).
Axes of the slice: x: 2, y: 2, z: 4, core: 2. Of those that a mesh axis runs over, the one named last changes fastest.
Arguments:
- inputs: bfloat16 [2, 32, 128, 1536], P(None, ('dp', 'expert')), may hold values from -6 to 6
- cotangent: bfloat16 [2, 32, 128, 1536], P(None, ('dp', 'expert')), may hold values from -6 to 6
- routes: int32 [2, 32, 128, 4], P(None, ('dp', 'expert')), may hold values from 0 to 15, all different within a row
- attention_gain: bfloat16 [1536], P(('dp', 'expert')), may hold values from 0.25 to 1.75
- query_weight: bfloat16 [1536, 1536], P(('dp', 'expert')), may hold values from -0.15625 to 0.15625
- key_matrix: bfloat16 [1536, 256], P(('dp', 'expert')), may hold values from -0.15625 to 0.15625
- value_matrix: bfloat16 [1536, 256], P(('dp', 'expert')), may hold values from -0.15625 to 0.15625
- output_weight: bfloat16 [1536, 1536], P(None, ('dp', 'expert')), may hold values from -0.625 to 0.625
- mixture_gain: bfloat16 [1536], P(('dp', 'expert')), may hold values from 0.25 to 1.75
- router_weight: bfloat16 [1536, 16], P(('dp', 'expert')), may hold values from -0.078125 to 0.078125
- gate_weight: bfloat16 [16, 1536, 768], P('expert', 'dp'), may hold values from -0.15625 to 0.15625
- up_weight: bfloat16 [16, 1536, 768], P('expert', 'dp'), may hold values from -0.15625 to 0.15625
- down_weight: bfloat16 [16, 768, 1536], P('expert', 'dp'), may hold values from -0.875 to 0.875
Outputs:
- outputs: bfloat16 [2, 32, 128, 1536], P(None, ('dp', 'expert'))
- input_grad: float32 [2, 32, 128, 1536], P(None, ('dp', 'expert'))
- attention_gain_grad: float32 [1536], P(('dp', 'expert'))
- query_grad: float32 [1536, 1536], P(('dp', 'expert'))
- key_grad: float32 [1536, 256], P(('dp', 'expert'))
- value_grad: float32 [1536, 256], P(('dp', 'expert'))
- output_grad: float32 [1536, 1536], P(None, ('dp', 'expert'))
- mixture_gain_grad: float32 [1536], P(('dp', 'expert'))
- router_grad: float32 [1536, 16], P(('dp', 'expert'))
- gate_grad: float32 [16, 1536, 768], P('expert', 'dp')
- up_grad: float32 [16, 1536, 768], P('expert', 'dp')
- down_grad: float32 [16, 768, 1536], P('expert', 'dp')
Inputs may be any that keep to these rules, and one draw needn't show every extreme that they name: `routes`: each token names 4 different experts, the first of highest priority.
All inputs are finite; a program needn't handle non-finite values.
Results may differ from a plain program's by a relative error of at most 0.018.
Values may be sent and summed in bfloat16 or wider, within the bound.
No kernel may reach another device: no remote copies, remote signals or barrier semaphores. Data moves between devices by JAX's collectives and lax.ppermute only.
A program may use at most 192 MiB of HBM per device.

v0:
```python
import math

import jax
import jax.numpy as jnp
from jax import lax
from jax.sharding import PartitionSpec as P

MODEL_WIDTH = 1536
QUERY_HEADS = 12
KEY_VALUE_HEADS = 2
HEAD_SIZE = 128


epsilon = 1e-06
rope_base = 10000.0
masked_score = -1e30


def rms_scale(values):
    return lax.rsqrt(jnp.mean(values * values, axis=-1, keepdims=True) + epsilon)


def rope_tables(sequence_length, head_width):
    halfway = head_width // 2
    frequency = rope_base ** (-(jnp.arange(halfway, dtype=jnp.float32) * 2.0 / head_width))
    angles = jnp.arange(sequence_length, dtype=jnp.float32)[:, None] * frequency[None, :]
    cosine_table = jnp.concatenate([jnp.cos(angles), jnp.cos(angles)], axis=-1)
    sine_table = jnp.concatenate([jnp.sin(angles), jnp.sin(angles)], axis=-1)
    return (cosine_table, sine_table)


def apply_rotation(values, cosine_table, sine_table):
    halfway = values.shape[-1] // 2
    turned = jnp.concatenate([-values[..., halfway:], values[..., :halfway]], axis=-1)
    return values * cosine_table + turned * sine_table


def rotate_back(values, cosine_table, sine_table):
    halfway = values.shape[-1] // 2
    shifted = values * sine_table
    turned = jnp.concatenate([shifted[..., halfway:], -shifted[..., :halfway]], axis=-1)
    return values * cosine_table + turned


def norm_back(upstream, scaled, scale_rows, gain_values):
    weighted = upstream * gain_values
    grad_values = scale_rows * (
        weighted - scaled * jnp.mean(weighted * scaled, axis=-1, keepdims=True)
    )
    return (grad_values, jnp.sum(upstream * scaled, axis=0))


def route_tables(route_rows, experts, capacity, topk_count):
    expert_ids = route_rows.reshape(-1)
    onehot_table = (expert_ids[:, None] == jnp.arange(experts, dtype=jnp.int32)[None, :]).astype(
        jnp.int32
    )
    position = jnp.sum(jnp.cumsum(onehot_table, axis=0) * onehot_table, axis=1) - 1
    kept_pairs = position < capacity
    slot_raw = jnp.where(kept_pairs, expert_ids * capacity + position, experts * capacity)
    token_ids = jnp.arange(expert_ids.shape[0], dtype=jnp.int32) // topk_count
    slot_token = (
        jnp.zeros((experts * capacity,), jnp.int32).at[slot_raw].set(token_ids, mode="drop")
    )
    slot_valid = jnp.zeros((experts * capacity,), jnp.int32).at[slot_raw].set(1, mode="drop")
    return (slot_token, slot_valid, slot_raw, kept_pairs.astype(jnp.int32))


def on_device(
    inputs,
    cotangent,
    routes,
    attention_gain,
    query_weight,
    key_matrix,
    value_matrix,
    output_weight,
    mixture_gain,
    router_weight,
    gate_weight,
    up_weight,
    down_weight,
):
    micro_count = inputs.shape[0]
    sequence_length = inputs.shape[2]
    topk_count = routes.shape[3]
    local_experts = gate_weight.shape[0]
    expert_devices = lax.axis_size("expert")
    experts = local_experts * expert_devices
    capacity = (5 * sequence_length * topk_count + 4 * experts - 1) // (4 * experts)
    group_feature_width = QUERY_HEADS // KEY_VALUE_HEADS
    score_scale = 1.0 / math.sqrt(HEAD_SIZE)
    cosine_table, sine_table = rope_tables(sequence_length, HEAD_SIZE)
    cosine_expanded = cosine_table[:, None, :]
    sine_expanded = sine_table[:, None, :]
    causal = jnp.arange(sequence_length)[:, None] >= jnp.arange(sequence_length)[None, :]
    expert_ids = jnp.arange(experts, dtype=jnp.int32)
    gain_first_total = jnp.zeros((MODEL_WIDTH,), jnp.float32)
    query_total = jnp.zeros((MODEL_WIDTH, QUERY_HEADS * HEAD_SIZE), jnp.float32)
    key_weight_gradient = jnp.zeros((MODEL_WIDTH, KEY_VALUE_HEADS * HEAD_SIZE), jnp.float32)
    value_weight_gradient = jnp.zeros((MODEL_WIDTH, KEY_VALUE_HEADS * HEAD_SIZE), jnp.float32)
    output_total = jnp.zeros((QUERY_HEADS * HEAD_SIZE, MODEL_WIDTH), jnp.float32)
    gain_second_total = jnp.zeros((MODEL_WIDTH,), jnp.float32)
    router_total = jnp.zeros((MODEL_WIDTH, experts), jnp.float32)
    gate_total = jnp.zeros((local_experts, MODEL_WIDTH, gate_weight.shape[2]), jnp.float32)
    up_total = jnp.zeros((local_experts, MODEL_WIDTH, up_weight.shape[2]), jnp.float32)
    down_total = jnp.zeros(
        (local_experts, down_weight.shape[1] * lax.axis_size("dp"), MODEL_WIDTH), jnp.float32
    )
    output_rows = []
    input_rows = []
    for micro_step in range(micro_count):
        dense_full = (
            lax.all_gather(attention_gain, ("dp", "expert"), axis=0, tiled=True),
            lax.all_gather(query_weight, ("dp", "expert"), axis=0, tiled=True),
            lax.all_gather(key_matrix, ("dp", "expert"), axis=0, tiled=True),
            lax.all_gather(value_matrix, ("dp", "expert"), axis=0, tiled=True),
            lax.all_gather(output_weight, ("dp", "expert"), axis=1, tiled=True),
            lax.all_gather(mixture_gain, ("dp", "expert"), axis=0, tiled=True),
            lax.all_gather(router_weight, ("dp", "expert"), axis=0, tiled=True),
        )
        expert_full = (
            lax.all_gather(gate_weight, "dp", axis=1, tiled=True),
            lax.all_gather(up_weight, "dp", axis=1, tiled=True),
            lax.all_gather(down_weight, "dp", axis=1, tiled=True),
        )
        gain_first, query_full, key_full, value_full, output_full, gain_second, router_full = (
            dense_full
        )
        gate_full, up_full, down_full = expert_full
        tokens = inputs[micro_step, 0].astype(jnp.float32)
        first_scale = rms_scale(tokens)
        first_hat = tokens * first_scale
        normed_one = (first_hat * gain_first.astype(jnp.float32)).astype(jnp.bfloat16)
        query_pre = jnp.dot(normed_one, query_full, preferred_element_type=jnp.float32)
        key_before_rotation = jnp.dot(normed_one, key_full, preferred_element_type=jnp.float32)
        value_low = (
            jnp.dot(normed_one, value_full, preferred_element_type=jnp.float32)
            .astype(jnp.bfloat16)
            .reshape(sequence_length, KEY_VALUE_HEADS, HEAD_SIZE)
        )
        query_rotated = apply_rotation(
            query_pre.reshape(sequence_length, QUERY_HEADS, HEAD_SIZE),
            cosine_expanded,
            sine_expanded,
        ).astype(jnp.bfloat16)
        key_rotated = apply_rotation(
            key_before_rotation.reshape(sequence_length, KEY_VALUE_HEADS, HEAD_SIZE),
            cosine_expanded,
            sine_expanded,
        ).astype(jnp.bfloat16)
        grouped_query = query_rotated.reshape(
            sequence_length, KEY_VALUE_HEADS, group_feature_width, HEAD_SIZE
        )
        scores = (
            jnp.einsum(
                "lcgd,mcd->cglm", grouped_query, key_rotated, preferred_element_type=jnp.float32
            )
            * score_scale
        )
        scores = jnp.where(causal, scores, masked_score)
        score_top = jnp.max(scores, axis=-1, keepdims=True)
        exponent = jnp.exp(scores - score_top)
        score_total = jnp.sum(exponent, axis=-1, keepdims=True)
        log_total = score_top + jnp.log(score_total)
        softmax_low = (exponent / score_total).astype(jnp.bfloat16)
        mixed_heads = jnp.einsum(
            "cglm,mcd->lcgd", softmax_low, value_low, preferred_element_type=jnp.float32
        )
        mixed_heads = mixed_heads.reshape(sequence_length, QUERY_HEADS * HEAD_SIZE).astype(
            jnp.bfloat16
        )
        hidden = tokens + jnp.dot(mixed_heads, output_full, preferred_element_type=jnp.float32)
        second_scale = rms_scale(hidden)
        second_hat = hidden * second_scale
        normed_two = (second_hat * gain_second.astype(jnp.float32)).astype(jnp.bfloat16)
        logits = jnp.dot(normed_two, router_full, preferred_element_type=jnp.float32)
        route_rows = routes[micro_step, 0]
        chosen = (route_rows[:, :, None] == expert_ids[None, None, :]).astype(jnp.float32)
        gate_values = jax.nn.softmax(jnp.sum(chosen * logits[:, None, :], axis=-1), axis=-1)
        slot_token, slot_valid, slot_raw, kept_pairs = route_tables(
            route_rows, experts, capacity, topk_count
        )
        pair_slot = jnp.minimum(slot_raw, experts * capacity - 1)
        pair_keep = kept_pairs.reshape(sequence_length, topk_count).astype(jnp.float32)
        send_rows = normed_two[slot_token] * slot_valid[:, None].astype(jnp.bfloat16)
        send_rows = send_rows.reshape(expert_devices, local_experts, capacity, MODEL_WIDTH)
        received = lax.all_to_all(send_rows, "expert", split_axis=0, concat_axis=0, tiled=True)
        gate_pre = jnp.einsum(
            "sxnd,xdf->sxnf", received, gate_full, preferred_element_type=jnp.float32
        )
        up_pre = jnp.einsum("sxnd,xdf->sxnf", received, up_full, preferred_element_type=jnp.float32)
        activated = (jax.nn.silu(gate_pre) * up_pre).astype(jnp.bfloat16)
        produced = jnp.einsum(
            "sxnf,xfd->sxnd", activated, down_full, preferred_element_type=jnp.float32
        ).astype(jnp.bfloat16)
        produced, received, gate_pre, up_pre, activated = (
            produced,
            received,
            gate_pre,
            up_pre,
            activated,
        )
        returned = lax.all_to_all(
            produced, "expert", split_axis=0, concat_axis=0, tiled=True
        ).reshape(experts * capacity, MODEL_WIDTH)
        pair_rows = (
            returned[pair_slot]
            .astype(jnp.float32)
            .reshape(sequence_length, topk_count, MODEL_WIDTH)
        )
        pair_weight = gate_values * pair_keep
        outputs_now = hidden + jnp.sum(pair_weight[:, :, None] * pair_rows, axis=1)
        output_rows.append(outputs_now.astype(jnp.bfloat16))
        back_dense = (
            lax.all_gather(attention_gain, ("dp", "expert"), axis=0, tiled=True),
            lax.all_gather(query_weight, ("dp", "expert"), axis=0, tiled=True),
            lax.all_gather(key_matrix, ("dp", "expert"), axis=0, tiled=True),
            lax.all_gather(value_matrix, ("dp", "expert"), axis=0, tiled=True),
            lax.all_gather(output_weight, ("dp", "expert"), axis=1, tiled=True),
            lax.all_gather(mixture_gain, ("dp", "expert"), axis=0, tiled=True),
            lax.all_gather(router_weight, ("dp", "expert"), axis=0, tiled=True),
        )
        back_expert = (
            lax.all_gather(gate_weight, "dp", axis=1, tiled=True),
            lax.all_gather(up_weight, "dp", axis=1, tiled=True),
            lax.all_gather(down_weight, "dp", axis=1, tiled=True),
        )
        (
            gain_first_back,
            query_back,
            key_back,
            value_back,
            output_back,
            gain_second_back,
            router_back,
        ) = back_dense
        gate_back, up_back, down_back = back_expert
        upstream = cotangent[micro_step, 0].astype(jnp.float32)
        pair_grad = pair_keep * jnp.sum(pair_rows * upstream[:, None, :], axis=-1)
        slot_gate = (
            jnp.zeros((experts * capacity,), jnp.float32)
            .at[slot_raw]
            .set(gate_values.reshape(-1), mode="drop")
        )
        slot_grad = (upstream[slot_token] * slot_gate[:, None]).astype(jnp.bfloat16)
        slot_grad = slot_grad.reshape(expert_devices, local_experts, capacity, MODEL_WIDTH)
        grad_received = lax.all_to_all(slot_grad, "expert", split_axis=0, concat_axis=0, tiled=True)
        down_total = down_total + jnp.einsum(
            "sxnf,sxnd->xfd", activated, grad_received, preferred_element_type=jnp.float32
        )
        grad_activated = jnp.einsum(
            "sxnd,xfd->sxnf", grad_received, down_back, preferred_element_type=jnp.float32
        )
        sigmoid_gate = jax.nn.sigmoid(gate_pre)
        grad_gate_pre = (
            grad_activated * up_pre * sigmoid_gate * (1.0 + gate_pre * (1.0 - sigmoid_gate))
        ).astype(jnp.bfloat16)
        grad_up_pre = (grad_activated * gate_pre * sigmoid_gate).astype(jnp.bfloat16)
        gate_total = gate_total + jnp.einsum(
            "sxnd,sxnf->xdf", received, grad_gate_pre, preferred_element_type=jnp.float32
        )
        up_total = up_total + jnp.einsum(
            "sxnd,sxnf->xdf", received, grad_up_pre, preferred_element_type=jnp.float32
        )
        grad_rows = jnp.einsum(
            "sxnf,xdf->sxnd", grad_gate_pre, gate_back, preferred_element_type=jnp.float32
        )
        grad_rows = grad_rows + jnp.einsum(
            "sxnf,xdf->sxnd", grad_up_pre, up_back, preferred_element_type=jnp.float32
        )
        grad_returned = lax.all_to_all(
            grad_rows.astype(jnp.bfloat16), "expert", split_axis=0, concat_axis=0, tiled=True
        ).reshape(experts * capacity, MODEL_WIDTH)
        grad_pairs = (
            grad_returned[pair_slot]
            .astype(jnp.float32)
            .reshape(sequence_length, topk_count, MODEL_WIDTH)
        )
        grad_normed = jnp.sum(grad_pairs * pair_keep[:, :, None], axis=1)
        grad_picked = gate_values * (
            pair_grad - jnp.sum(gate_values * pair_grad, axis=-1, keepdims=True)
        )
        grad_logits = jnp.sum(chosen * grad_picked[:, :, None], axis=1).astype(jnp.bfloat16)
        router_total = router_total + jnp.einsum(
            "ld,le->de", normed_two, grad_logits, preferred_element_type=jnp.float32
        )
        grad_normed = grad_normed + jnp.einsum(
            "le,de->ld", grad_logits, router_back, preferred_element_type=jnp.float32
        )
        grad_hidden_norm, gain_second_part = norm_back(
            grad_normed, second_hat, second_scale, gain_second_back.astype(jnp.float32)
        )
        gain_second_total = gain_second_total + gain_second_part
        grad_hidden = upstream + grad_hidden_norm
        grad_branch = grad_hidden.astype(jnp.bfloat16)
        output_total = output_total + jnp.einsum(
            "le,ld->ed", mixed_heads, grad_branch, preferred_element_type=jnp.float32
        )
        mixed_heads_gradient = jnp.einsum(
            "ld,ed->le", grad_branch, output_back, preferred_element_type=jnp.float32
        )
        mixed_heads_gradient = mixed_heads_gradient.astype(jnp.bfloat16).reshape(
            sequence_length, KEY_VALUE_HEADS, group_feature_width, HEAD_SIZE
        )
        scores_again = (
            jnp.einsum(
                "lcgd,mcd->cglm", grouped_query, key_rotated, preferred_element_type=jnp.float32
            )
            * score_scale
        )
        scores_again = jnp.where(causal, scores_again, masked_score)
        softmax_again = jnp.exp(scores_again - log_total)
        value_gradient = jnp.einsum(
            "cglm,lcgd->mcd",
            softmax_again.astype(jnp.bfloat16),
            mixed_heads_gradient,
            preferred_element_type=jnp.float32,
        )
        value_gradient = value_gradient.astype(jnp.bfloat16).reshape(
            sequence_length, KEY_VALUE_HEADS * HEAD_SIZE
        )
        grad_softmax = jnp.einsum(
            "lcgd,mcd->cglm", mixed_heads_gradient, value_low, preferred_element_type=jnp.float32
        )
        grad_scores = softmax_again * (
            grad_softmax - jnp.sum(softmax_again * grad_softmax, axis=-1, keepdims=True)
        )
        grad_scores = grad_scores.astype(jnp.bfloat16)
        grad_query = (
            jnp.einsum(
                "cglm,mcd->lcgd", grad_scores, key_rotated, preferred_element_type=jnp.float32
            )
            * score_scale
        )
        grad_key = (
            jnp.einsum(
                "cglm,lcgd->mcd", grad_scores, grouped_query, preferred_element_type=jnp.float32
            )
            * score_scale
        )
        grad_query_pre = (
            rotate_back(
                grad_query.reshape(sequence_length, QUERY_HEADS, HEAD_SIZE),
                cosine_expanded,
                sine_expanded,
            )
            .astype(jnp.bfloat16)
            .reshape(sequence_length, QUERY_HEADS * HEAD_SIZE)
        )
        grad_key_pre = (
            rotate_back(grad_key, cosine_expanded, sine_expanded)
            .astype(jnp.bfloat16)
            .reshape(sequence_length, KEY_VALUE_HEADS * HEAD_SIZE)
        )
        query_total = query_total + jnp.einsum(
            "ld,le->de", normed_one, grad_query_pre, preferred_element_type=jnp.float32
        )
        key_weight_gradient = key_weight_gradient + jnp.einsum(
            "ld,le->de", normed_one, grad_key_pre, preferred_element_type=jnp.float32
        )
        value_weight_gradient = value_weight_gradient + jnp.einsum(
            "ld,le->de", normed_one, value_gradient, preferred_element_type=jnp.float32
        )
        grad_normed_one = jnp.einsum(
            "le,de->ld", grad_query_pre, query_back, preferred_element_type=jnp.float32
        )
        grad_normed_one = grad_normed_one + jnp.einsum(
            "le,de->ld", grad_key_pre, key_back, preferred_element_type=jnp.float32
        )
        grad_normed_one = grad_normed_one + jnp.einsum(
            "le,de->ld", value_gradient, value_back, preferred_element_type=jnp.float32
        )
        grad_tokens_norm, gain_first_part = norm_back(
            grad_normed_one, first_hat, first_scale, gain_first_back.astype(jnp.float32)
        )
        gain_first_total = gain_first_total + gain_first_part
        input_rows.append(grad_hidden + grad_tokens_norm)
    dense_shards = (
        lax.psum_scatter(gain_first_total, ("dp", "expert"), scatter_dimension=0, tiled=True),
        lax.psum_scatter(query_total, ("dp", "expert"), scatter_dimension=0, tiled=True),
        lax.psum_scatter(key_weight_gradient, ("dp", "expert"), scatter_dimension=0, tiled=True),
        lax.psum_scatter(value_weight_gradient, ("dp", "expert"), scatter_dimension=0, tiled=True),
        lax.psum_scatter(output_total, ("dp", "expert"), scatter_dimension=1, tiled=True),
        lax.psum_scatter(gain_second_total, ("dp", "expert"), scatter_dimension=0, tiled=True),
        lax.psum_scatter(router_total, ("dp", "expert"), scatter_dimension=0, tiled=True),
    )
    expert_shards = (
        lax.psum_scatter(
            gate_total.astype(jnp.bfloat16), "dp", scatter_dimension=1, tiled=True
        ).astype(jnp.float32),
        lax.psum_scatter(
            up_total.astype(jnp.bfloat16), "dp", scatter_dimension=1, tiled=True
        ).astype(jnp.float32),
        lax.psum_scatter(
            down_total.astype(jnp.bfloat16), "dp", scatter_dimension=1, tiled=True
        ).astype(jnp.float32),
    )
    outputs = jnp.stack(output_rows, axis=0)[:, None]
    input_grad = jnp.stack(input_rows, axis=0)[:, None]
    return (
        outputs,
        input_grad,
        dense_shards[0],
        dense_shards[1],
        dense_shards[2],
        dense_shards[3],
        dense_shards[4],
        dense_shards[5],
        dense_shards[6],
        expert_shards[0],
        expert_shards[1],
        expert_shards[2],
    )


def solution(mesh):
    in_specs = (
        P(None, ("dp", "expert"), None, None),
        P(None, ("dp", "expert"), None, None),
        P(None, ("dp", "expert"), None, None),
        P(("dp", "expert")),
        P(("dp", "expert"), None),
        P(("dp", "expert"), None),
        P(("dp", "expert"), None),
        P(None, ("dp", "expert")),
        P(("dp", "expert")),
        P(("dp", "expert"), None),
        P("expert", "dp", None),
        P("expert", "dp", None),
        P("expert", "dp", None),
    )
    out_specs = (
        P(None, ("dp", "expert"), None, None),
        P(None, ("dp", "expert"), None, None),
        P(("dp", "expert")),
        P(("dp", "expert"), None),
        P(("dp", "expert"), None),
        P(("dp", "expert"), None),
        P(None, ("dp", "expert")),
        P(("dp", "expert")),
        P(("dp", "expert"), None),
        P("expert", "dp", None),
        P("expert", "dp", None),
        P("expert", "dp", None),
    )
    return jax.shard_map(
        on_device, mesh=mesh, in_specs=in_specs, out_specs=out_specs, check_vma=False
    )
```

profile of v0, /device:TPU:0, one launch (start us, length us, event | category | flops | bytes accessed | tf_op | source)
XLA Modules:
  0.0 1364.4 jit_solution(14641771589693783231)
XLA Ops:
  11.1 46.7 %all_gather.22 = bf16[1536,256]{1,0:T(8,128)(2,1)S(1)} all-gather(bf16[48,256]{1,0:T(8,128)(2,1)} %param.18), channel_id=1, replica_groups=mesh['dp'=2,'expert'=16] {'dp','expert'}, dimensions={0}, use_global_device_ids=true | all-gather | bytes 811008 | tf_op jit(solution)/shard_map/all_gather | solution.py:116
  58.6 37.6 %all-reduce.5 = (bf16[1536]{0:T(1024)(128)(2,1)S(1)}, bf16[1536]{0:T(1024)(128)(2,1)S(1)}) all-reduce(bf16[1536]{0:T(1024)(128)(2,1)S(1)} %dynamic-update-slice, bf16[1536]{0:T(1024)(128)(2,1)S(1)} %dynamic-update-slice.1), channel_id=1, replica_groups=mesh['dp'=2,'expert'=16] {'dp','expert'}, use_global_device_ids=true, to_apply=%add | all-reduce | flops 3072 | bytes 12288
  97.7 43.2 %all_gather.21 = bf16[1536,256]{1,0:T(8,128)(2,1)S(1)} all-gather(bf16[48,256]{1,0:T(8,128)(2,1)S(1)} %copy-done.83), channel_id=1, replica_groups=mesh['dp'=2,'expert'=16] {'dp','expert'}, dimensions={0}, use_global_device_ids=true | all-gather | bytes 811008 | tf_op jit(solution)/shard_map/all_gather | solution.py:117
  151.7 6.8 copy.185
  178.7 4.4 all-to-all-start
  193.3 62.7 %all-gather = bf16[32,48,16]{1,2,0:T(8,128)(2,1)S(1)} all-gather(bf16[1,48,16]{1,2,0:T(8,128)(2,1)} %bitcast.676), channel_id=1, replica_groups=mesh['dp'=2,'expert'=16] {'dp','expert'}, dimensions={0}, use_global_device_ids=true | all-gather | bytes 50688 | tf_op jit(solution)/shard_map/all_gather | solution.py:120
  275.0 4.4 all-to-all-start.4
  280.0 5.2 fusion.28
  285.3 5.2 fusion.20
  290.5 28.1 %all-gather.15.cloned.1.call-done = bf16[1,768,1536]{2,1,0:T(8,128)(2,1)} async-done(((bf16[1,384,1536]{2,1,0:T(8,128)(2,1)}), bf16[1,768,1536]{2,1,0:T(8,128)(2,1)}) %all-gather.15.cloned.1.call-update) | async-done | bytes 2359312 | tf_op jit(solution)/shard_map/all_gather | solution.py:125
  318.6 6.9 fusion.42
  330.8 10.3 all-to-all-start.5
  341.2 4.9 fusion.6
  346.1 33.9 %all-to-all-done.5 = bf16[16,1,40,1536]{3,2,1,0:T(8,128)(2,1)} async-done(((bf16[16,1,40,1536]{3,2,1,0:T(8,128)(2,1)}), bf16[16,1,40,1536]{3,2,1,0:T(8,128)(2,1)}, u32[]{:S(2)}, u32[]{:S(2)}) %all-to-all-start.5) | async-done | bytes 1966112 | tf_op jit(solution)/shard_map/all_to_all | solution.py:272
  380.1 10.7 all-to-all-start.1
  427.1 5.1 multiply_reduce_fusion.12
  432.2 6.2 gather_fusion.5
  438.4 4.3 reshape.998
  442.7 5.0 multiply_reduce_fusion.3
  447.7 6.2 gather_fusion.1
  453.9 4.3 reshape.994
  458.2 5.0 multiply_reduce_fusion.2
  472.5 6.2 all-to-all-start.2
  489.8 27.8 %all-to-all-done.2 = bf16[16,1,40,1536]{3,2,1,0:T(8,128)(2,1)} async-done(((bf16[16,1,40,1536]{3,2,1,0:T(8,128)(2,1)}), bf16[16,1,40,1536]{3,2,1,0:T(8,128)(2,1)}, u32[]{:S(2)}, u32[]{:S(2)}) %all-to-all-start.2) | async-done | bytes 1966112 | tf_op jit(solution)/shard_map/all_to_all | solution.py:188
  517.6 10.7 all-to-all-start.6
  528.4 5.4 fusion.26
  533.8 4.5 fusion.18
  538.3 28.9 %all-to-all-done.6 = bf16[16,1,40,1536]{3,2,1,0:T(8,128)(2,1)} async-done(((bf16[16,1,40,1536]{3,2,1,0:T(8,128)(2,1)}), bf16[16,1,40,1536]{3,2,1,0:T(8,128)(2,1)}, u32[]{:S(2)}, u32[]{:S(2)}) %all-to-all-start.6) | async-done | bytes 1966112 | tf_op jit(solution)/shard_map/all_to_all | solution.py:248
  567.3 7.2 fusion.34
  578.4 10.9 all-to-all-start.3
  589.3 6.0 fusion.61
  595.6 32.5 %all-to-all-done.3 = bf16[16,1,40,1536]{3,2,1,0:T(8,128)(2,1)} async-done(((bf16[16,1,40,1536]{3,2,1,0:T(8,128)(2,1)}), bf16[16,1,40,1536]{3,2,1,0:T(8,128)(2,1)}, u32[]{:S(2)}, u32[]{:S(2)}) %all-to-all-start.3) | async-done | bytes 1966112 | tf_op jit(solution)/shard_map/all_to_all | solution.py:204
  628.1 6.6 gather_fusion.3
  639.0 5.0 multiply_reduce_fusion
  645.6 6.4 fusion.3
  656.8 5.2 fusion.4
  669.8 10.7 all-to-all-start.7
  687.2 5.2 fusion.5
  692.6 28.8 %all-to-all-done.7 = bf16[16,1,40,1536]{3,2,1,0:T(8,128)(2,1)S(1)} async-done(((bf16[16,1,40,1536]{3,2,1,0:T(8,128)(2,1)}), bf16[16,1,40,1536]{3,2,1,0:T(8,128)(2,1)S(1)}, u32[]{:S(2)}, u32[]{:S(2)}) %all-to-all-start.7) | async-done | bytes 1966112 | tf_op jit(solution)/shard_map/all_to_all | solution.py:272
  724.5 4.3 reshape.1000
  759.2 5.2 convolution_add_fusion.1
  768.1 5.1 convolution_add_fusion
  789.9 46.2 %all-reduce.4 = (f32[1536]{0:T(1024)}, f32[1536]{0:T(1024)}) all-reduce(f32[1536]{0:T(1024)} %add.389, f32[1536]{0:T(1024)} %add.396), channel_id=2, replica_groups=mesh['dp'=2,'expert'=16] {'dp','expert'}, use_global_device_ids=true, to_apply=%region_44.45.clone | all-reduce | flops 3072 | bytes 24576
  850.8 17.4 %reduce-scatter.23.cloned.1.call-done = bf16[1,384,1536]{2,1,0:T(8,128)(2,1)} async-done(((bf16[1,768,1536]{2,1,0:T(8,128)(2,1)}), bf16[1,384,1536]{2,1,0:T(8,128)(2,1)}) %reduce-scatter.23.cloned.1.call-update) | async-done | bytes 1179664 | tf_op jit(solution)/shard_map/reduce_scatter | solution.py:395
  871.2 100.5 %reduce-scatter.13.cloned.1.call-done = f32[48,256]{1,0:T(8,128)} async-done(((f32[1536,256]{1,0:T(8,128)}), f32[48,256]{1,0:T(8,128)}) %reduce-scatter.13.cloned.1.call-update) | async-done | bytes 49168 | tf_op jit(solution)/shard_map/reduce_scatter | solution.py:382
  971.7 102.7 %reduce-scatter.15.cloned.1.call-done = f32[48,256]{1,0:T(8,128)} async-done(((f32[1536,256]{1,0:T(8,128)}), f32[48,256]{1,0:T(8,128)}) %reduce-scatter.15.cloned.1.call-update) | async-done | bytes 49168 | tf_op jit(solution)/shard_map/reduce_scatter | solution.py:383
  1074.4 142.0 %reduce-scatter.11.cloned.1.call-done = f32[48,1536]{1,0:T(8,128)} async-done(((f32[1536,1536]{1,0:T(8,128)}), f32[48,1536]{1,0:T(8,128)}) %reduce-scatter.11.cloned.1.call-update) | async-done | bytes 294928 | tf_op jit(solution)/shard_map/reduce_scatter | solution.py:381
  1216.4 141.0 %reduce-scatter.17.cloned.1.call-done = f32[1536,48]{0,1:T(8,128)} async-done(((f32[1536,1536]{0,1:T(8,128)}), f32[1536,48]{0,1:T(8,128)}) %reduce-scatter.17.cloned.1.call-update) | async-done | bytes 294928 | tf_op jit(solution)/shard_map/reduce_scatter | solution.py:384
  (473 shorter events, 228.5 us)
Async XLA Ops:
  7.2 144.6 %all-gather.7.cloned.1.call-start = ((), (), s32[]{:S(2)}) async-start(), calls=%async_computation.16 | async-start | bytes 4866048 | tf_op jit(solution)/shard_map/all_gather | solution.py:115
  7.9 50.2 %copy-start.109 = (bf16[48]{0:T(256)(128)(2,1)S(1)}, bf16[48]{0:T(256)(128)(2,1)}, u32[]{:S(2)}) copy-start(bf16[48]{0:T(256)(128)(2,1)} %param.16) | copy-start | bytes 292
  7.9 50.5 %copy-start.110 = (bf16[48]{0:T(256)(128)(2,1)S(1)}, bf16[48]{0:T(256)(128)(2,1)}, u32[]{:S(2)}) copy-start(bf16[48]{0:T(256)(128)(2,1)} %param.21) | copy-start | bytes 292
  7.9 88.3 %copy-start = (bf16[2,1,128,1536]{3,2,1,0:T(8,128)(2,1)S(1)}, bf16[2,1,128,1536]{3,2,1,0:T(8,128)(2,1)}, u32[]{:S(2)}) copy-start(bf16[2,1,128,1536]{3,2,1,0:T(8,128)(2,1)} %param.13) | copy-start | bytes 2359300
  7.9 159.6 %all-gather.9.cloned.1.call-start = ((), (), s32[]{:S(2)}) async-start(), calls=%async_computation.17 | async-start | bytes 4866048 | tf_op jit(solution)/shard_map/all_gather | solution.py:118
  8.7 271.3 %all-gather.11.cloned.1.call-start = ((), (), s32[]{:S(2)}) async-start(), calls=%async_computation.18 | async-start | bytes 3538944 | tf_op jit(solution)/shard_map/all_gather | solution.py:123
  9.5 155.7 %copy-start.60 = (pred[128,128]{0,1:T(8,128)(4,1)}, pred[128,128]{0,1:T(8,128)(4,1)S(1)}, u32[]{:S(2)}) copy-start(pred[128,128]{0,1:T(8,128)(4,1)S(1)} %iota_compare_fusion) | copy-start | bytes 49156
  11.1 133.4 %copy-start.100 = (s32[512]{0:T(512)}, s32[512]{0:T(512)S(1)}, u32[]{:S(2)}) copy-start(s32[512]{0:T(512)S(1)} %add_select_fusion) | copy-start | bytes 6148
  57.8 39.2 %copy-start.8 = (bf16[1536,256]{1,0:T(8,128)(2,1)}, bf16[1536,256]{1,0:T(8,128)(2,1)S(1)}, u32[]{:S(2)}) copy-start(bf16[1536,256]{1,0:T(8,128)(2,1)S(1)} %all_gather.22) | copy-start | bytes 2359300
  96.2 319.7 %copy-start.37 = (f32[1536]{0:T(1024)}, f32[1536]{0:T(1024)S(1)}, u32[]{:S(2)}) copy-start(f32[1536]{0:T(1024)S(1)} %convert_element_type.447) | copy-start | bytes 18436
  96.5 62.0 %copy-start.70 = (f32[128]{0:T(128)}, f32[128]{0:T(128)S(1)}, u32[]{:S(2)}) copy-start(f32[128]{0:T(128)S(1)} %get-tuple-element.182) | copy-start | bytes 1540
  96.5 66.0 %copy-start.79 = (f32[128]{0:T(128)}, f32[128]{0:T(128)S(1)}, u32[]{:S(2)}) copy-start(f32[128]{0:T(128)S(1)} %get-tuple-element.181) | copy-start | bytes 1540
  142.1 24.4 %copy-start.54 = (bf16[128,2,128]{2,1,0:T(2,128)(2,1)}, bf16[128,2,128]{2,1,0:T(2,128)(2,1)S(1)}, u32[]{:S(2)}) copy-start(bf16[128,2,128]{2,1,0:T(2,128)(2,1)S(1)} %reshape.960) | copy-start | bytes 196612
  143.9 6.5 copy-start.85
  144.5 14.0 %copy-start.101 = (s32[512,1]{0,1:T(1,128)}, s32[512,1]{0,1:T(1,128)S(1)}, u32[]{:S(2)}) copy-start(s32[512,1]{0,1:T(1,128)S(1)} %compare_select_fusion.3) | copy-start | bytes 6148
  147.0 25.0 %copy-start.68 = (s32[1024]{0:T(1024)}, s32[1024]{0:T(1024)S(1)}, u32[]{:S(2)}) copy-start(s32[1024]{0:T(1024)S(1)} %pad_clamp_fusion.3) | copy-start | bytes 12292
  151.0 13.1 copy-start.31
  151.0 13.1 copy-start.39
  151.7 13.5 copy-start.50
  178.7 96.3 %all-to-all-start = ((bf16[16,1,40,1536]{3,2,1,0:T(8,128)(2,1)}), bf16[16,1,40,1536]{3,2,1,0:T(8,128)(2,1)}, u32[]{:S(2)}, u32[]{:S(2)}) async-start(bf16[16,1,40,1536]{3,2,1,0:T(8,128)(2,1)} %broadcast_multiply_fusion.1), calls=%async_computation | async-start | bytes 3932160 | tf_op jit(solution)/shard_map/all_to_all | solution.py:188
  183.1 102.2 %all-gather.13.cloned.1.call-start = ((), (), s32[]{:S(2)}) async-start(), calls=%async_computation.19 | async-start | bytes 3538944 | tf_op jit(solution)/shard_map/all_gather | solution.py:124
  275.0 43.6 %all-to-all-start.4 = ((bf16[16,1,40,1536]{3,2,1,0:T(8,128)(2,1)}), bf16[16,1,40,1536]{3,2,1,0:T(8,128)(2,1)}, u32[]{:S(2)}, u32[]{:S(2)}) async-start(bf16[16,1,40,1536]{3,2,1,0:T(8,128)(2,1)} %multiply_convert_fusion.1), calls=%async_computation.4 | async-start | bytes 3932160 | tf_op jit(solution)/shard_map/all_to_all | solution.py:248
  279.4 39.2 %all-gather.15.cloned.1.call-start = ((), (), s32[]{:S(2)}) async-start(), calls=%async_computation.20 | async-start | bytes 3538944 | tf_op jit(solution)/shard_map/all_gather | solution.py:125
  318.6 6.9 copy-start.104
  330.8 49.2 %all-to-all-start.5 = ((bf16[16,1,40,1536]{3,2,1,0:T(8,128)(2,1)}), bf16[16,1,40,1536]{3,2,1,0:T(8,128)(2,1)}, u32[]{:S(2)}, u32[]{:S(2)}) async-start(bf16[16,1,40,1536]{3,2,1,0:T(8,128)(2,1)} %fusion.8), calls=%async_computation.5 | async-start | bytes 3932160 | tf_op jit(solution)/shard_map/all_to_all | solution.py:272
  380.1 67.7 %all-to-all-start.1 = ((bf16[16,1,40,1536]{3,2,1,0:T(8,128)(2,1)}), bf16[16,1,40,1536]{3,2,1,0:T(8,128)(2,1)}, u32[]{:S(2)}, u32[]{:S(2)}) async-start(bf16[16,1,40,1536]{3,2,1,0:T(8,128)(2,1)} %fusion.6), calls=%async_computation.1 | async-start | bytes 3932160 | tf_op jit(solution)/shard_map/all_to_all | solution.py:204
  432.2 31.2 %copy-start.97 = (f32[128]{0:T(128)}, f32[128]{0:T(128)S(1)}, u32[]{:S(2)}) copy-start(f32[128]{0:T(128)S(1)} %add_rsqrt_fusion) | copy-start | bytes 1540
  472.5 45.1 %all-to-all-start.2 = ((bf16[16,1,40,1536]{3,2,1,0:T(8,128)(2,1)}), bf16[16,1,40,1536]{3,2,1,0:T(8,128)(2,1)}, u32[]{:S(2)}, u32[]{:S(2)}) async-start(bf16[16,1,40,1536]{3,2,1,0:T(8,128)(2,1)} %broadcast_multiply_fusion), calls=%async_computation.2 | async-start | bytes 3932160 | tf_op jit(solution)/shard_map/all_to_all | solution.py:188
  482.9 7.0 copy-start.45
  517.6 49.6 %all-to-all-start.6 = ((bf16[16,1,40,1536]{3,2,1,0:T(8,128)(2,1)}), bf16[16,1,40,1536]{3,2,1,0:T(8,128)(2,1)}, u32[]{:S(2)}, u32[]{:S(2)}) async-start(bf16[16,1,40,1536]{3,2,1,0:T(8,128)(2,1)} %multiply_convert_fusion), calls=%async_computation.6 | async-start | bytes 3932160 | tf_op jit(solution)/shard_map/all_to_all | solution.py:248
  567.3 8.1 copy-start.108
  578.4 10.9 copy-start.93
  578.4 49.8 %all-to-all-start.3 = ((bf16[16,1,40,1536]{3,2,1,0:T(8,128)(2,1)}), bf16[16,1,40,1536]{3,2,1,0:T(8,128)(2,1)}, u32[]{:S(2)}, u32[]{:S(2)}) async-start(bf16[16,1,40,1536]{3,2,1,0:T(8,128)(2,1)} %fusion.7), calls=%async_computation.3 | async-start | bytes 3932160 | tf_op jit(solution)/shard_map/all_to_all | solution.py:204
  589.2 254.5 %reduce-scatter.25.cloned.1.call-start = ((), (), s32[]{:S(2)}) async-start(), calls=%async_computation.28 | async-start | bytes 811008
  589.3 38.8 %copy-start.91 = (s32[1024]{0:T(1024)}, s32[1024]{0:T(1024)S(1)}, u32[]{:S(2)}) copy-start(s32[1024]{0:T(1024)S(1)} %pad_clamp_fusion) | copy-start | bytes 12292
  644.2 7.8 copy-start.66
  645.5 199.6 %reduce-scatter.19.cloned.1.call-start = ((), (), s32[]{:S(2)}) async-start(), calls=%async_computation.25 | async-start | bytes 3538944 | tf_op jit(solution)/shard_map/reduce_scatter | solution.py:389
  652.0 196.0 %reduce-scatter.21.cloned.1.call-start = ((), (), s32[]{:S(2)}) async-start(), calls=%async_computation.26 | async-start | bytes 3538944 | tf_op jit(solution)/shard_map/reduce_scatter | solution.py:392
  669.8 51.6 %all-to-all-start.7 = ((bf16[16,1,40,1536]{3,2,1,0:T(8,128)(2,1)}), bf16[16,1,40,1536]{3,2,1,0:T(8,128)(2,1)S(1)}, u32[]{:S(2)}, u32[]{:S(2)}) async-start(bf16[16,1,40,1536]{3,2,1,0:T(8,128)(2,1)} %fusion.9), calls=%async_computation.7 | async-start | bytes 3932160 | tf_op jit(solution)/shard_map/all_to_all | solution.py:272
  680.5 187.7 %reduce-scatter.23.cloned.1.call-start = ((), (), s32[]{:S(2)}) async-start(), calls=%async_computation.27 | async-start | bytes 3538944 | tf_op jit(solution)/shard_map/reduce_scatter | solution.py:395
  681.3 62.3 %copy-start.61 = (f32[2,6,128]{2,1,0:T(8,128)}, f32[2,6,128]{2,1,0:T(8,128)S(1)}, u32[]{:S(2)}) copy-start(f32[2,6,128]{2,1,0:T(8,128)S(1)} %log_add_fusion.1) | copy-start | bytes 18436
  692.4 279.4 %reduce-scatter.13.cloned.1.call-start = ((), (), s32[]{:S(2)}) async-start(), calls=%async_computation.22 | async-start | bytes 1622016 | tf_op jit(solution)/shard_map/reduce_scatter | solution.py:382
  728.8 8.2 slice-start
  747.5 326.9 %reduce-scatter.15.cloned.1.call-start = ((), (), s32[]{:S(2)}) async-start(), calls=%async_computation.23 | async-start | bytes 1622016 | tf_op jit(solution)/shard_map/reduce_scatter | solution.py:383
  754.9 461.5 %reduce-scatter.11.cloned.1.call-start = ((), (), s32[]{:S(2)}) async-start(), calls=%async_computation.21 | async-start | bytes 9732096 | tf_op jit(solution)/shard_map/reduce_scatter | solution.py:381
  764.4 593.0 %reduce-scatter.17.cloned.1.call-start = ((), (), s32[]{:S(2)}) async-start(), calls=%async_computation.24 | async-start | bytes 9732096 | tf_op jit(solution)/shard_map/reduce_scatter | solution.py:384
  786.5 53.5 %copy-start.34 = (bf16[1,128,1536]{2,1,0:T(8,128)(2,1)S(1)}, bf16[1,128,1536]{2,1,0:T(8,128)(2,1)}, u32[]{:S(2)}) copy-start(bf16[1,128,1536]{2,1,0:T(8,128)(2,1)} %get-tuple-element.114) | copy-start | bytes 1179652
  836.1 6.0 copy-start.29
  (94 other events, 245.4 us)
Sparse Core Ops, SparseCore 0:
  10.9 68.6 all-gather.6
  82.4 63.8 all-gather.8
  147.8 35.7 all-gather.10
  185.2 37.1 all-gather.12
  281.5 37.0 all-gather.14
  645.6 110.7 reduce-scatter.24
  759.2 33.7 reduce-scatter.18
  796.0 35.3 reduce-scatter.20
  833.6 34.5 reduce-scatter.22
  874.7 96.9 reduce-scatter.12
  978.4 95.9 reduce-scatter.14
  1081.8 134.5 reduce-scatter.10
  1222.9 134.4 reduce-scatter.16
where the time goes:
time: 1370 us; the launch traced here: 1360 us
  waiting for transfers between devices  687 us (50%)
  blocking collectives  236 us (17%)
  matrix products  149 us (11%)
  local copies, waits for them, and re-layouts  124 us (9%)
  other arithmetic  81.8 us (6%)
  starting transfers between devices  70 us (5%)
  between operations  16.2 us (1%)
    reduce_scatter x1, waiting for transfers between devices, on_device(): lax.psum_scatter(query_total, ('dp', 'expert'), scatter_dimension=0, tile...  142 us
    reduce_scatter x1, waiting for transfers between devices, on_device(): lax.psum_scatter(output_total, ('dp', 'expert'), scatter_dimension=1, til...  141 us
    reduce_scatter x1, waiting for transfers between devices, on_device(): lax.psum_scatter(value_weight_gradient, ('dp', 'expert'), scatter_dimensi...  103 us
    reduce_scatter x1, waiting for transfers between devices, on_device(): lax.psum_scatter(key_weight_gradient, ('dp', 'expert'), scatter_dimension...  101 us
    unnamed x2, blocking collectives  83.8 us
    all_to_all x2, waiting for transfers between devices, on_device(): lax.all_to_all(grad_rows.astype(jnp.bfloat16), 'expert', split_axis=0, co...  62.7 us
    all_gather x1, blocking collectives, on_device(): lax.all_gather(router_weight, ('dp', 'expert'), axis=0, tiled=True)  62.7 us
    all_gather x1, blocking collectives, on_device(): lax.all_gather(key_matrix, ('dp', 'expert'), axis=0, tiled=True)  46.7 us
  transfers between devices with their start and end apart: 21, of which 11 were waited for; matrix products, arithmetic and copies ran while one was open for 20% of the time, Pallas kernels for 0%

commit v1 on v0

v1 whole, which is shorter than its diff:
```python
import functools
import math

import jax
import jax.numpy as jnp
import numpy as np
from jax import lax
from jax.experimental import pallas as pl
from jax.experimental.pallas import tpu as pltpu
from jax.sharding import PartitionSpec as P

WIDTH = 1536
QUERY_HEADS = 12
KEY_VALUE_HEADS = 2
HEAD = 128
GROUP = QUERY_HEADS // KEY_VALUE_HEADS
Q_COLS = QUERY_HEADS * HEAD
KV_COLS = KEY_VALUE_HEADS * HEAD
MISC = Q_COLS + 2 * KV_COLS
EXTRA = 16
LANES = 128
EPSILON = 1e-06
ROPE_BASE = 10000.0
MASKED = -1e30
SCALE = 1.0 / math.sqrt(HEAD)

f32 = jnp.float32
bf16 = jnp.bfloat16


def dot(a, b, ca=1, cb=0):
    return lax.dot_general(a, b, (((ca,), (cb,)), ((), ())), preferred_element_type=f32)


def vmem(n):
    return [pl.BlockSpec(memory_space=pltpu.VMEM)] * n


def smem():
    return pl.BlockSpec(memory_space=pltpu.SMEM)


def call(body, outs, ins, args, name, flops, scratch=()):
    size = sum(math.prod(a.shape) * a.dtype.itemsize for a in args)
    size += sum(math.prod(o.shape) * o.dtype.itemsize for o in outs)
    return pl.pallas_call(
        body,
        out_shape=outs,
        in_specs=ins,
        out_specs=vmem(len(outs)),
        scratch_shapes=list(scratch),
        compiler_params=pltpu.CompilerParams(vmem_limit_bytes=60 * 1024 * 1024),
        cost_estimate=pl.CostEstimate(flops=flops, bytes_accessed=size, transcendentals=0),
        name=name,
    )(*args)


def sds(shape, dtype):
    return jax.ShapeDtypeStruct(shape, dtype)


def rope_tables(length):
    half = HEAD // 2
    frequency = ROPE_BASE ** (-(np.arange(half, dtype=np.float64) * 2.0 / HEAD))
    angles = np.arange(length, dtype=np.float64)[:, None] * frequency[None, :]
    cos, sin = np.cos(angles), np.sin(angles)
    cosine = np.concatenate([cos, cos], axis=1).astype(np.float32)
    signed = np.concatenate([-sin, sin], axis=1).astype(np.float32)
    return cosine, signed


def place(where_ref, scratch, piece_refs, first=0):
    at = first
    for ref in piece_refs:
        blocks, rows, _ = ref.shape
        for j in range(blocks):
            start = pl.multiple_of(where_ref[at] * rows, 16 if rows % 16 == 0 else 8)
            scratch[pl.ds(start, rows), :] = ref[j]
            at += 1


def scale_of(z):
    return lax.rsqrt(jnp.mean(z * z, axis=-1, keepdims=True) + EPSILON)


def heads_of(ref, b, length, c):
    return jnp.concatenate(
        [ref[b * length : (b + 1) * length, h * HEAD : (h + 1) * HEAD] for h in range(c * GROUP, (c + 1) * GROUP)],
        axis=0,
    )


def causal_mask(length):
    row = lax.broadcasted_iota(jnp.int32, (length, length), 0)
    column = lax.broadcasted_iota(jnp.int32, (length, length), 1)
    return jnp.concatenate([row >= column] * GROUP, axis=0)


def softmax_of(q, k, keep):
    s = jnp.where(keep, dot(q, k, 1, 1) * SCALE, MASKED)
    e = jnp.exp(s - jnp.max(s, axis=-1, keepdims=True))
    return e / jnp.sum(e, axis=-1, keepdims=True)


def attend_body(seqs, experts, n_pieces, where_ref, x_ref, cos_ref, sin_ref, *refs):
    pieces = refs[:n_pieces]
    w_ref, gain_ref, n1_ref, q_ref, k_ref, v_ref, mixed_ref = refs[n_pieces:]
    length = x_ref.shape[0] // seqs
    place(where_ref, w_ref, pieces)
    gains = jnp.transpose(w_ref[:, MISC : MISC + LANES].astype(f32))[experts : experts + 8]
    gain_ref[...] = gains
    x = x_ref[...].astype(f32)
    n1 = (x * scale_of(x) * gains[0:1]).astype(bf16)
    n1_ref[...] = n1
    cos = jnp.concatenate([cos_ref[...]] * seqs, axis=0)
    sin = jnp.concatenate([sin_ref[...]] * seqs, axis=0)

    def rotated(u):
        return (u * cos + pltpu.roll(u, HEAD // 2, 1) * sin).astype(bf16)

    kv = dot(n1, w_ref[:, Q_COLS:MISC])
    v_ref[...] = kv[:, KV_COLS:].astype(bf16)
    for c in range(KEY_VALUE_HEADS):
        k_ref[:, c * HEAD : (c + 1) * HEAD] = rotated(kv[:, c * HEAD : (c + 1) * HEAD])
    keep = causal_mask(length)
    for c in range(KEY_VALUE_HEADS):
        cols = GROUP * HEAD
        q = dot(n1, w_ref[:, c * cols : (c + 1) * cols])
        for h in range(GROUP):
            at = c * cols + h * HEAD
            q_ref[:, at : at + HEAD] = rotated(q[:, h * HEAD : (h + 1) * HEAD])
        for b in range(seqs):
            rows = slice(b * length, (b + 1) * length)
            k = k_ref[rows, c * HEAD : (c + 1) * HEAD]
            v = v_ref[rows, c * HEAD : (c + 1) * HEAD]
            p = softmax_of(heads_of(q_ref, b, length, c), k, keep).astype(bf16)
            o = dot(p, v).astype(bf16)
            for h in range(GROUP):
                at = c * cols + h * HEAD
                mixed_ref[rows, at : at + HEAD] = o[h * length : (h + 1) * length]


def project_body(experts, n_pieces, where_ref, x_ref, mixed_ref, gain_ref, misc_ref, routes_ref, *refs):
    pieces = refs[:n_pieces]
    o_ref, hidden_ref, send_ref, gate_ref = refs[n_pieces:]
    place(where_ref, o_ref, pieces)
    tokens = x_ref.shape[0]
    h = x_ref[...].astype(f32) + dot(mixed_ref[...], o_ref[...], 1, 1)
    hidden_ref[...] = h
    n2 = (h * scale_of(h) * gain_ref[1:2]).astype(bf16)
    send_ref[0:tokens] = n2
    z = dot(n2, misc_ref[...])
    lane = lax.broadcasted_iota(jnp.int32, (tokens, LANES), 1)
    chosen = lane == routes_ref[:, 0:1]
    for j in range(1, routes_ref.shape[1]):
        chosen = chosen | (lane == routes_ref[:, j : j + 1])
    top = jnp.max(jnp.where(chosen, z, MASKED), axis=-1, keepdims=True)
    e = jnp.where(chosen, jnp.exp(jnp.where(chosen, z - top, 0.0)), 0.0)
    gate = e / jnp.sum(e, axis=-1, keepdims=True)
    gate_ref[...] = gate
    high = gate.astype(bf16).astype(f32)
    tables = [jnp.transpose(t) for t in (high, gate - high, chosen.astype(f32))]
    blank = jnp.zeros((EXTRA, tokens), f32)
    parts = []
    for first in range(0, experts, EXTRA):
        parts += [t[first : first + EXTRA] for t in tables]
    parts += [blank] * (WIDTH // tokens - len(parts))
    send_ref[tokens:] = jnp.concatenate(parts, axis=1).astype(bf16)


def expert_body(layout, capacity, slots, tokens, seqs, which_ref, *refs):
    arrays, n_in = layout
    count = len(arrays)
    ins = refs[:n_in]
    gate_ref, up_ref, down_ref = refs[n_in : n_in + 3]
    outs = refs[n_in + 3 :]
    out_refs, dx_refs = outs[:count], outs[count : 2 * count]
    xs_ref, dy_ref, act_ref, du_ref, dw_ref, gs_ref, gcol_ref = outs[2 * count :]
    length = tokens // seqs
    me = which_ref[0]
    row_in = lax.rem(me, EXTRA)
    row = lax.broadcasted_iota(jnp.int32, (EXTRA, tokens), 0)
    mine = row == row_in
    block = lax.div(me, EXTRA)

    def table(extra, k):
        t = jnp.zeros((EXTRA, tokens), f32)
        for b in range(WIDTH // (3 * tokens)):
            at = (3 * b + k) * tokens
            t = jnp.where(block == b, extra[:, at : at + tokens].astype(f32), t)
        return jnp.sum(jnp.where(mine, t, 0.0), axis=0, keepdims=True)

    def read(pieces, first, rows):
        got = []
        for index, start, size, offset in pieces:
            lo, hi = max(first, start), min(first + rows, start + size)
            if lo < hi:
                got.append(ins[index][offset + lo - start : offset + hi - start])
        return got[0] if len(got) == 1 else jnp.concatenate(got, axis=0)

    tri_a = lax.broadcasted_iota(jnp.int32, (length, length), 0)
    tri_b = lax.broadcasted_iota(jnp.int32, (length, length), 1)
    before = (tri_a < tri_b).astype(bf16)
    slot = lax.broadcasted_iota(jnp.int32, (slots, tokens), 0).astype(f32)
    gates, masks = [], []
    for n2_pieces, _ in arrays:
        extra = read(n2_pieces, tokens, EXTRA)
        gates.append(table(extra, 0) + table(extra, 1))
        masks.append(table(extra, 2))
    picks = []
    for i, (n2_pieces, g_pieces) in enumerate(arrays):
        at = []
        for b in range(seqs):
            m = masks[i][:, b * length : (b + 1) * length]
            earlier = dot(jnp.broadcast_to(m, (16, length)).astype(bf16), before)[0:1]
            keep = (m > 0.5) & (earlier < capacity)
            at.append(jnp.where(keep, earlier + b * (slots // seqs), -1.0))
        pick = (slot == jnp.concatenate(at, axis=1)).astype(f32)
        gcol_ref[i * slots : (i + 1) * slots, :] = jnp.broadcast_to(
            jnp.sum(pick * gates[i], axis=1, keepdims=True), (slots, LANES)
        )
        pick = pick.astype(bf16)
        picks.append(pick)
        rows = slice(i * slots, (i + 1) * slots)
        xs_ref[rows, :] = dot(pick, read(n2_pieces, 0, tokens)).astype(bf16)
        gs_ref[rows, :] = dot(pick, read(g_pieces, 0, tokens)).astype(bf16)
    xs = xs_ref[...]
    u = dot(xs, gate_ref[...])
    w = dot(xs, up_ref[...])
    s = 1.0 / (1.0 + jnp.exp(-u))
    act = (u * s * w).astype(bf16)
    act_ref[...] = act
    y = dot(act, down_ref[...]).astype(bf16).astype(f32)
    gcol = gcol_ref[:, 0:1]
    gs = gs_ref[...].astype(f32)
    dy = (gcol * gs).astype(bf16)
    dy_ref[...] = dy
    dg = jnp.sum(gs * y, axis=1, keepdims=True)
    weighted = (gcol * y).astype(bf16)
    dact = dot(dy, down_ref[...], 1, 1)
    du = (dact * w * s * (1.0 + u * (1.0 - s))).astype(bf16)
    dw = (dact * (u * s)).astype(bf16)
    du_ref[...] = du
    dw_ref[...] = dw
    dx = (dot(du, gate_ref[...], 1, 1) + dot(dw, up_ref[...], 1, 1)).astype(bf16)
    for i in range(count):
        rows = slice(i * slots, (i + 1) * slots)
        out_refs[i][...] = dot(picks[i], weighted[rows], 0, 0).astype(bf16)
        dx_refs[i][0:tokens] = dot(picks[i], dx[rows], 0, 0).astype(bf16)
        back = jnp.sum(picks[i].astype(f32) * dg[rows], axis=0, keepdims=True)
        high = back.astype(bf16).astype(f32)
        blank = jnp.zeros((EXTRA, tokens), f32)
        parts = []
        for b in range(WIDTH // (3 * tokens)):
            here = mine & (block == b)
            parts += [jnp.where(here, high, 0.0), jnp.where(here, back - high, 0.0), blank]
        dx_refs[i][tokens:] = jnp.concatenate(parts, axis=1).astype(bf16)


def weights_body(n, half, adds, which_ref, *refs):
    lists = [refs[k * n : (k + 1) * n] for k in range(5)]
    xs, dys, acts, dus, dws = lists
    more = refs[5 * n : 5 * n + 3 * adds]
    gate_out, up_out, down_out = refs[5 * n + 3 * adds :]
    wide, narrow = half
    x_at = pl.multiple_of(which_ref[0] * wide, LANES)
    a_at = pl.multiple_of(which_ref[0] * narrow, LANES)
    totals = [None, None, None]
    for i in range(n):
        x = xs[i][:, pl.ds(x_at, wide)]
        a = acts[i][:, pl.ds(a_at, narrow)]
        for k, (left, right) in enumerate(((x, dus[i]), (x, dws[i]), (a, dys[i]))):
            now = dot(left, right[...], 0, 0)
            totals[k] = now if totals[k] is None else totals[k] + now
    for k, out in enumerate((gate_out, up_out, down_out)):
        total = totals[k]
        for j in range(adds):
            total = total + more[3 * j + k][...].astype(f32)
        out[...] = total.astype(out.dtype)


def norm_back(up, hat, scale, gain):
    w = up * gain
    return scale * (w - hat * jnp.mean(w * hat, axis=-1, keepdims=True)), jnp.sum(up * hat, axis=0, keepdims=True)


def hidden_back_body(experts, a_ref, b_ref, c_ref, d_ref, g_ref, hidden_ref, gain_ref, gate_ref, misc_ref, o_ref, mixed_ref, *outs):
    dh_ref, dmixed_ref, og_ref, rg_ref, gg_ref = outs
    tokens = g_ref.shape[0]
    got = a_ref[...].astype(f32) + b_ref[...].astype(f32) + c_ref[...].astype(f32) + d_ref[...].astype(f32)
    extra = got[tokens:]
    rows = []
    for first in range(experts // EXTRA):
        at = 3 * first * tokens
        rows.append(extra[:, at : at + tokens] + extra[:, at + tokens : at + 2 * tokens])
    rows.append(jnp.zeros((LANES - experts, tokens), f32))
    dg = jnp.transpose(jnp.concatenate(rows, axis=0))
    gate = gate_ref[...]
    dl = gate * (dg - jnp.sum(gate * dg, axis=-1, keepdims=True))
    dz = dl.astype(bf16)
    dn = got[0:tokens] + dot(dz, misc_ref[...], 1, 1)
    h = hidden_ref[...]
    scale = scale_of(h)
    hat = h * scale
    gain = gain_ref[1:2]
    n2 = (hat * gain).astype(bf16)
    rg_ref[...] = dot(n2, dz, 0, 0)
    back, grad = norm_back(dn, hat, scale, gain)
    gg_ref[...] = jnp.broadcast_to(grad, gg_ref.shape)
    dh = g_ref[...].astype(f32) + back
    dh_ref[...] = dh
    da = dh.astype(bf16)
    dmixed_ref[...] = dot(da, o_ref[...]).astype(bf16)
    og_ref[...] = dot(da, mixed_ref[...], 0, 0).astype(bf16)


def attend_back_body(seqs, experts, x_ref, cos_ref, sin_ref, w_ref, gain_ref, n1_ref, q_ref, k_ref, v_ref, do_ref, dh_ref, rg_ref, gg_ref, dx_ref, wg_ref, dqkv_ref):
    length = x_ref.shape[0] // seqs
    cos = cos_ref[...]
    sin = sin_ref[...]
    keep = causal_mask(length)

    def back(u):
        return (u * cos - pltpu.roll(u, HEAD // 2, 1) * sin).astype(bf16)

    for b in range(seqs):
        rows = slice(b * length, (b + 1) * length)
        for c in range(KEY_VALUE_HEADS):
            cols = slice(c * HEAD, (c + 1) * HEAD)
            k = k_ref[rows, cols]
            v = v_ref[rows, cols]
            q = heads_of(q_ref, b, length, c)
            do = heads_of(do_ref, b, length, c)
            p = softmax_of(q, k, keep)
            dqkv_ref[rows, Q_COLS + KV_COLS + c * HEAD : Q_COLS + KV_COLS + (c + 1) * HEAD] = dot(
                p.astype(bf16), do, 0, 0
            ).astype(bf16)
            dp = dot(do, v, 1, 1)
            ds = (p * (dp - jnp.sum(p * dp, axis=-1, keepdims=True))).astype(bf16)
            dq = dot(ds, k) * SCALE
            for h in range(GROUP):
                at = (c * GROUP + h) * HEAD
                dqkv_ref[rows, at : at + HEAD] = back(dq[h * length : (h + 1) * length])
            dqkv_ref[rows, Q_COLS + c * HEAD : Q_COLS + (c + 1) * HEAD] = back(dot(ds, q, 0, 0) * SCALE)
    dqkv = dqkv_ref[...]
    wg_ref[:, 0:MISC] = dot(n1_ref[...], dqkv, 0, 0).astype(bf16)
    dn = dot(dqkv, w_ref[:, 0:MISC], 1, 1)
    x = x_ref[...].astype(f32)
    scale = scale_of(x)
    back_x, grad = norm_back(dn, x * scale, scale, gain_ref[0:1])
    dx_ref[...] = dh_ref[...] + back_x
    row = lax.broadcasted_iota(jnp.int32, (LANES, x.shape[1]), 0)
    gains = jnp.where(row == experts, grad, jnp.where(row == experts + 1, gg_ref[0:1], 0.0))
    wg_ref[:, MISC:] = (rg_ref[...] + jnp.transpose(gains)).astype(bf16)


def chip_ring(chips):
    if chips % 4 or chips < 8:
        return list(range(chips))
    high, low = 4, chips // 4
    order = [a * low for a in range(high)]
    for step, a in enumerate(reversed(range(high))):
        rest = list(range(1, low))
        order += [a * low + b for b in (rest if step % 2 == 0 else reversed(rest))]
    return order


class Ring:
    def __init__(self, devices):
        self.devices = devices
        self.chips = devices // 2
        self.half = self.chips // 2
        self.order = chip_ring(self.chips)
        n = self.chips
        self.up = [
            (2 * self.order[p] + lane, 2 * self.order[(p + 1) % n] + lane) for p in range(n) for lane in (0, 1)
        ]
        self.down = [(b, a) for a, b in self.up]
        self.swap = [(d, d ^ 1) for d in range(devices)]
        self.place = np.argsort(np.array(self.order)).astype(np.int32)
        self.offsets = [0] + [s * o for o in range(1, self.half) for s in (-1, 1)] + [self.half]

    def send_up(self, x):
        return lax.ppermute(x, "expert", self.up)

    def send_down(self, x):
        return lax.ppermute(x, "expert", self.down)

    def send_core(self, x):
        return lax.ppermute(x, "expert", self.swap)

    def device(self, offset, other):
        me = lax.axis_index("expert")
        at = (jnp.asarray(self.place)[me // 2] + offset) % self.chips
        return 2 * jnp.asarray(np.array(self.order, np.int32))[at] + lax.rem(me + other, 2)

    def gather(self, x, split=None):
        got = {0: [x]}
        up = down = x
        for s in range(1, self.half):
            up, down = self.send_up(up), self.send_down(down)
            got[-s], got[s] = [up], [down]
        if split is None:
            got[self.half] = [self.send_up(up)]
        else:
            got[self.half] = [self.send_up(up[:split]), self.send_down(down[split:])]
        return got

    def scatter(self, own, other, split):
        partner = {o: self.send_core(other[o]) for o in [self.half] + self.offsets[:-1][::-1]}

        def total(*terms):
            out = terms[0].astype(f32)
            for t in terms[1:]:
                out = out + t.astype(f32)
            return out.astype(bf16)

        h = self.half
        first = total(own[h], partner[h])
        up, down = self.send_up(first[:split]), self.send_down(first[split:])
        for s in range(h - 1, 0, -1):
            if s == h - 1:
                up = jnp.concatenate(
                    [total(own[s][:split], partner[s][:split], up), total(own[s][split:], partner[s][split:])]
                )
                down = jnp.concatenate(
                    [total(own[-s][:split], partner[-s][:split]), total(own[-s][split:], partner[-s][split:], down)]
                )
            else:
                up, down = total(own[s], partner[s], up), total(own[-s], partner[-s], down)
            up, down = self.send_up(up), self.send_down(down)
        return own[0], partner[0], up, down


def dp_pairs(shift):
    n = lax.axis_size("dp")
    return [(i, (i + shift) % n) for i in range(n)]


def from_dp(x, shift):
    return lax.ppermute(x, "dp", dp_pairs(shift))


def whole_from_dp(x):
    parts = lax.axis_size("dp")
    if parts != 2:
        return lax.all_gather(x, "dp", axis=0, tiled=True)
    other = from_dp(x, 1)
    low = lax.axis_index("dp") == 0
    return jnp.concatenate([jnp.where(low, x, other), jnp.where(low, other, x)], axis=0)


def on_device(
    inputs,
    cotangent,
    routes,
    attention_gain,
    query_weight,
    key_matrix,
    value_matrix,
    output_weight,
    mixture_gain,
    router_weight,
    gate_weight,
    up_weight,
    down_weight,
):
    seqs, _, length, _ = inputs.shape
    tokens = seqs * length
    topk = routes.shape[3]
    dp, experts = lax.axis_size("dp"), lax.axis_size("expert")
    assert gate_weight.shape[0] == 1 and experts % EXTRA == 0 and experts * 3 * tokens <= EXTRA * WIDTH * 2
    ring = Ring(experts)
    my_dp, me = lax.axis_index("dp"), lax.axis_index("expert")
    capacity = (5 * length * topk + 4 * experts - 1) // (4 * experts)
    slots = seqs * ((capacity + 7) // 8 * 8)
    x = inputs.reshape(tokens, WIDTH)
    g = cotangent.reshape(tokens, WIDTH)
    cos, sin = (jnp.asarray(t) for t in rope_tables(length))
    split = length

    rows = query_weight.shape[0]
    misc = jnp.concatenate(
        [
            router_weight,
            attention_gain[:, None],
            mixture_gain[:, None],
            jnp.zeros((rows, LANES - experts - 2), bf16),
        ],
        axis=1,
    )
    qkv_own = jnp.concatenate([query_weight, key_matrix, value_matrix, misc], axis=1)
    o_own = output_weight.T
    pieces_apart = dp == 2 and rows % 16 == 0
    if pieces_apart:
        pair = jnp.stack([qkv_own, from_dp(qkv_own, 1)])
        got = ring.gather(pair)
        qkv, where = [], []
        for o in ring.offsets:
            for other, piece in ((0, got[o][0]), (1, ring.send_core(got[o][0]))):
                qkv.append(piece)
                d = ring.device(o, other)
                where += [my_dp * experts + d, (1 - my_dp) * experts + d]
        qkv_where = jnp.stack(where).astype(jnp.int32)
        got = ring.gather(o_own)
        stack = jnp.stack([got[o][0] for o in ring.offsets])
        far = from_dp(stack, 1)
        o_full = [stack, ring.send_core(stack), far, ring.send_core(far)]
        o_where = jnp.stack(
            [
                y * experts + ring.device(o, other)
                for y in (my_dp, 1 - my_dp)
                for other in (0, 1)
                for o in ring.offsets
            ]
        ).astype(jnp.int32)
    else:
        both = lax.all_gather(jnp.concatenate([qkv_own, o_own], axis=1), ("dp", "expert"), axis=0, tiled=True)
        qkv, o_full = [both[None, :, : MISC + LANES]], [both[None, :, MISC + LANES :]]
        qkv_where = o_where = jnp.zeros((1,), jnp.int32)

    gate_full = whole_from_dp(gate_weight[0])
    up_full = whole_from_dp(up_weight[0])
    down_full = whole_from_dp(down_weight[0])

    g_all = ring.gather(g, split)
    g_far = {o: [ring.send_core(p) for p in g_all[o]] for o in ring.offsets}

    w_full, gains, n1, q, k, v, mixed = call(
        functools.partial(attend_body, seqs, experts, len(qkv)),
        [
            sds((WIDTH, MISC + LANES), bf16),
            sds((8, WIDTH), f32),
            sds((tokens, WIDTH), bf16),
            sds((tokens, Q_COLS), bf16),
            sds((tokens, KV_COLS), bf16),
            sds((tokens, KV_COLS), bf16),
            sds((tokens, Q_COLS), bf16),
        ],
        [smem()] + vmem(3 + len(qkv)),
        [qkv_where, x, cos, sin, *qkv],
        "attend",
        2 * tokens * WIDTH * MISC,
    )
    misc_full = w_full[:, MISC:]
    o_t, hidden, send, gate_values = call(
        functools.partial(project_body, experts, len(o_full)),
        [
            sds((WIDTH, Q_COLS), bf16),
            sds((tokens, WIDTH), f32),
            sds((tokens + EXTRA, WIDTH), bf16),
            sds((tokens, LANES), f32),
        ],
        [smem()] + vmem(5 + len(o_full)),
        [o_where, x, mixed, gains, misc_full, routes.reshape(tokens, topk), *o_full],
        "project",
        2 * tokens * WIDTH * Q_COLS,
    )

    n_all = ring.gather(send, split)
    n_far = {o: [ring.send_core(p) for p in n_all[o]] for o in ring.offsets}
    which = me.astype(jnp.int32)[None]
    out_own, out_far, dx_own, dx_far = {}, {}, {}, {}
    kept = [[], [], [], [], []]
    groups = [[0]] + [[-s, s] for s in range(1, ring.half)] + [[ring.half]]
    hidden_size = gate_full.shape[1]
    for group in groups:
        args, arrays = [], []
        for o in group:
            for n_side, g_side in ((n_all, g_all), (n_far, g_far)):
                described = []
                for pieces in (n_side[o], g_side[o]):
                    parts, start = [], 0
                    for p in pieces:
                        parts.append((len(args), start, p.shape[0], 0))
                        args.append(p)
                        start += p.shape[0]
                    described.append(parts)
                arrays.append(tuple(described))
        count = len(arrays)
        total = count * slots
        outs = call(
            functools.partial(expert_body, (arrays, len(args)), capacity, slots, tokens, seqs),
            [sds((tokens, WIDTH), bf16)] * count
            + [sds((tokens + EXTRA, WIDTH), bf16)] * count
            + [sds((total, WIDTH), bf16)] * 2
            + [sds((total, hidden_size), bf16)] * 3,
            [smem()] + vmem(len(args) + 3),
            [which, *args, gate_full, up_full, down_full],
            "experts",
            2 * total * WIDTH * hidden_size * 6,
            [pltpu.VMEM((total, WIDTH), bf16), pltpu.VMEM((total, LANES), f32)],
        )
        for i, o in enumerate(group):
            out_own[o], out_far[o] = outs[2 * i], outs[2 * i + 1]
            dx_own[o], dx_far[o] = outs[count + 2 * i], outs[count + 2 * i + 1]
        for k_, value in zip(kept, outs[2 * count :], strict=True):
            k_.append(value)
    dx_terms = ring.scatter(dx_own, dx_far, split)
    out_terms = ring.scatter(out_own, out_far, split)

    saved = [a for k_ in kept for a in k_]
    wide, narrow = WIDTH // dp, hidden_size // dp
    if wide % LANES == 0 and narrow % LANES == 0:

        def part(index, dtype, more):
            return call(
                functools.partial(weights_body, len(groups), (wide, narrow), len(more) // 3),
                [sds((wide, hidden_size), dtype)] * 2 + [sds((narrow, WIDTH), dtype)],
                [smem()] + vmem(len(saved) + len(more)),
                [index.astype(jnp.int32)[None], *saved, *more],
                "expert_weights",
                2 * experts * slots * wide * hidden_size * 3,
            )

        more = []
        for shift in range(1, dp):
            more += [from_dp(p, shift) for p in part(lax.rem(my_dp + shift, dp), bf16, [])]
        gate_grad, up_grad, down_grad = part(my_dp, f32, more)
    else:
        xs, dys, acts, dus, dws = (jnp.concatenate(k_) for k_ in kept)
        gate_grad, up_grad, down_grad = (
            lax.psum_scatter(dot(a, b, 0, 0).astype(bf16), "dp", scatter_dimension=0, tiled=True).astype(f32)
            for a, b in ((xs, dus), (xs, dws), (acts, dys))
        )

    dh, dmixed, o_part, router_part, gain_part = call(
        functools.partial(hidden_back_body, experts),
        [
            sds((tokens, WIDTH), f32),
            sds((tokens, Q_COLS), bf16),
            sds((WIDTH, Q_COLS), bf16),
            sds((WIDTH, LANES), f32),
            sds((8, WIDTH), f32),
        ],
        vmem(11),
        [*dx_terms, g, hidden, gains, gate_values, misc_full, o_t, mixed],
        "hidden_back",
        4 * tokens * WIDTH * Q_COLS,
    )
    input_grad, qkv_part, _ = call(
        functools.partial(attend_back_body, seqs, experts),
        [sds((tokens, WIDTH), f32), sds((WIDTH, MISC + LANES), bf16), sds((tokens, MISC), bf16)],
        vmem(13),
        [x, cos, sin, w_full, gains, n1, q, k, v, dmixed, dh, router_part, gain_part],
        "attend_back",
        4 * tokens * WIDTH * MISC,
    )

    def reduced(part):
        columns = part.shape[1]
        if dp != 2:
            return lax.psum_scatter(part, ("dp", "expert"), scatter_dimension=0, tiled=True).astype(f32)
        blocks = part.reshape(dp, ring.chips, 2, rows, columns)
        lane = lax.rem(me, 2)

        def of_lane(index):
            return lax.dynamic_index_in_dim(blocks, index, axis=2, keepdims=False)

        swapped = ring.send_core(of_lane(1 - lane))
        mine = of_lane(lane)

        def of_y(index):
            a = lax.dynamic_index_in_dim(mine, index, axis=0, keepdims=False).astype(f32)
            b = lax.dynamic_index_in_dim(swapped, index, axis=0, keepdims=False).astype(f32)
            return a + b

        far = from_dp(of_y(1 - my_dp).astype(bf16), 1)
        both = (of_y(my_dp) + far.astype(f32)).astype(bf16)

        def of_chip(offset):
            return lax.dynamic_index_in_dim(both, ring.device(offset, 0) // 2, axis=0, keepdims=False)

        up = ring.send_up(of_chip(ring.half))
        down = None
        for s in range(ring.half - 1, 0, -1):
            up = ring.send_up((up.astype(f32) + of_chip(s).astype(f32)).astype(bf16))
            term = of_chip(-s)
            down = ring.send_down(term if down is None else (down.astype(f32) + term.astype(f32)).astype(bf16))
        return up.astype(f32) + down.astype(f32) + of_chip(0).astype(f32)

    o_grad = reduced(o_part)
    qkv_grad = reduced(qkv_part)

    total = hidden
    for t in out_terms:
        total = total + t.astype(f32)
    outputs = total.astype(bf16).reshape(inputs.shape)
    return (
        outputs,
        input_grad.reshape(inputs.shape),
        qkv_grad[:, MISC + experts],
        qkv_grad[:, :Q_COLS],
        qkv_grad[:, Q_COLS : Q_COLS + KV_COLS],
        qkv_grad[:, Q_COLS + KV_COLS : MISC],
        o_grad.T,
        qkv_grad[:, MISC + experts + 1],
        qkv_grad[:, MISC : MISC + experts],
        gate_grad[None],
        up_grad[None],
        down_grad[None],
    )


def solution(mesh):
    both = ("dp", "expert")
    tokens = P(None, both, None, None)
    expert = P("expert", "dp", None)
    in_specs = (
        tokens,
        tokens,
        tokens,
        P(both),
        P(both, None),
        P(both, None),
        P(both, None),
        P(None, both),
        P(both),
        P(both, None),
        expert,
        expert,
        expert,
    )
    out_specs = (
        tokens,
        tokens,
        P(both),
        P(both, None),
        P(both, None),
        P(both, None),
        P(None, both),
        P(both),
        P(both, None),
        expert,
        expert,
        expert,
    )
    return jax.shard_map(on_device, mesh=mesh, in_specs=in_specs, out_specs=out_specs, check_vma=False)
```

time: 1370 us -> 683 us (0.50)
  waiting for transfers between devices: 687 us -> 356 us
  blocking collectives: 236 us -> 0 us
  matrix products: 149 us -> 0 us
  Pallas kernels: 0 us -> 142 us
  local copies, waits for them, and re-layouts: 124 us -> 27.3 us
  other arithmetic: 81.8 us -> 36.5 us
  starting transfers between devices: 70 us -> 96.9 us
    reduce_scatter x7 -> x0, waiting for transfers between devices: 504 us -> none  [the longest x1 142 us: on_device(): lax.psum_scatter(query_total, ('dp', 'expert'), scatter_dimension=0, tile...]
    ppermute x0 -> x116, waiting for transfers between devices: none -> 356 us  [the longest x32 167 us: send_up(): return lax.ppermute(x, 'expert', self.up)]
    all_gather x3 -> x0, blocking collectives: 153 us -> none  [the longest x1 62.7 us: on_device(): lax.all_gather(router_weight, ('dp', 'expert'), axis=0, tiled=True)]
    all_to_all x8 -> x0, waiting for transfers between devices: 152 us -> none  [the longest x2 62.7 us: on_device(): lax.all_to_all(grad_rows.astype(jnp.bfloat16), 'expert', split_axis=0, co...]
    dot_general x60 -> x0, matrix products: 149 us -> none  [the longest x2 14 us: on_device(): jnp.einsum('sxnd,xfd->sxnf', grad_received, down_back, preferred_element_...]
    pallas_call x0 -> x11, Pallas kernels: none -> 142 us  [call(): pl.pallas_call(body, out_shape=outs, in_specs=ins, out_specs=vmem(len(out...]
    ppermute x0 -> x116, starting transfers between devices: none -> 96.9 us  [the longest x32 52.4 us: send_up(): return lax.ppermute(x, 'expert', self.up)]
    unnamed x2 -> x0, blocking collectives: 83.8 us -> none
  transfers between devices with their start and end apart: 21 -> 116, of which waited for: 11 -> 47; matrix products, arithmetic and copies ran while one was open for 20% -> 8% of each run, Pallas kernels for 0% -> 21%
where the time goes in v1:
time: 683 us; the launch traced here: 673 us
  waiting for transfers between devices  356 us (52%)
  Pallas kernels  142 us (21%)
  starting transfers between devices  96.9 us (14%)
  other arithmetic  36.5 us (5%)
  local copies, waits for them, and re-layouts  27.3 us (4%)
  between operations  14 us (2%)
    ppermute x32, waiting for transfers between devices, send_up(): return lax.ppermute(x, 'expert', self.up)  167 us
    pallas_call x11, Pallas kernels, call(): pl.pallas_call(body, out_shape=outs, in_specs=ins, out_specs=vmem(len(out...  142 us
    ppermute x10, waiting for transfers between devices, from_dp(): return lax.ppermute(x, 'dp', dp_pairs(shift))  130 us
    ppermute x28, waiting for transfers between devices, send_down(): return lax.ppermute(x, 'expert', self.down)  54.7 us
    ppermute x32, starting transfers between devices, send_up(): return lax.ppermute(x, 'expert', self.up)  52.4 us
    ppermute x28, starting transfers between devices, send_down(): return lax.ppermute(x, 'expert', self.down)  23.7 us
    ppermute x10, starting transfers between devices, from_dp(): return lax.ppermute(x, 'dp', dp_pairs(shift))  13.8 us
  transfers between devices with their start and end apart: 116, of which 47 were waited for; matrix products, arithmetic and copies ran while one was open for 8% of the time, Pallas kernels for 21%

profile of v1, /device:TPU:0, one launch (start us, length us, event | category | flops | bytes accessed | tf_op | source)
XLA Modules:
  0.0 672.5 jit_solution(8198969050342004353)
XLA Ops:
  0.7 3.1 collective-permute-start.16
  15.4 12.3 %collective-permute-done.18 = bf16[48,1536]{1,0:T(8,128)(2,1)S(1)} collective-permute-done((bf16[48,1536]{1,0:T(8,128)(2,1)S(1)}, bf16[48,1536]{1,0:T(8,128)(2,1)S(1)}, u32[]{:S(2)}, u32[]{:S(2)}) %collective-permute-start.18) | collective-permute-done | bytes 147488 | tf_op jit(solution)/shard_map/ppermute | solution.py:384
  29.8 3.0 collective-permute-done.20
  34.8 3.3 collective-permute-done.22
  40.6 6.4 collective-permute-done.2.refs_2_
  52.4 9.3 %collective-permute-done.6.refs_6_ = bf16[2,48,2176]{2,1,0:T(8,128)(2,1)S(1)} collective-permute-done((bf16[2,48,2176]{2,1,0:T(8,128)(2,1)S(1)}, bf16[2,48,2176]{2,1,0:T(8,128)(2,1)S(1)}, u32[]{:S(2)}, u32[]{:S(2)}) %collective-permute-start.6) | collective-permute-done | bytes 417824 | tf_op jit(solution)/shard_map/ppermute | solution.py:384
  64.8 11.2 %collective-permute-done.29 = bf16[768,768]{1,0:T(8,128)(2,1)S(1)} collective-permute-done((bf16[768,768]{1,0:T(8,128)(2,1)S(1)}, bf16[768,768]{1,0:T(8,128)(2,1)S(1)}, u32[]{:S(2)}, u32[]{:S(2)}) %collective-permute-start.29) | collective-permute-done | bytes 1179680 | tf_op jit(solution)/shard_map/ppermute | solution.py:441
  77.9 18.6 %collective-permute-done.24.refs_2_ = bf16[8,48,1536]{2,1,0:T(8,128)(2,1)} collective-permute-done((bf16[8,48,1536]{2,1,0:T(8,128)(2,1)S(1)}, bf16[8,48,1536]{2,1,0:T(8,128)(2,1)}, u32[]{:S(2)}, u32[]{:S(2)}) %collective-permute-start.24) | collective-permute-done | bytes 1179680 | tf_op jit(solution)/shard_map/ppermute | solution.py:441
  101.5 8.6 %collective-permute-done.14.refs_14_ = bf16[2,48,2176]{2,1,0:T(8,128)(2,1)} collective-permute-done((bf16[2,48,2176]{2,1,0:T(8,128)(2,1)S(1)}, bf16[2,48,2176]{2,1,0:T(8,128)(2,1)}, u32[]{:S(2)}, u32[]{:S(2)}) %collective-permute-start.14) | collective-permute-done | bytes 417824 | tf_op jit(solution)/shard_map/ppermute | solution.py:384
  127.5 8.5 %attend.1 = (bf16[1536,2176]{1,0:T(8,128)(2,1)}, f32[8,1536]{1,0:T(8,128)}, bf16[256,1536]{1,0:T(8,128)(2,1)}, bf16[256,1536]{1,0:T(8,128)(2,1)}, bf16[256,256]{...) custom-call(s32[32]{0:T(128)} %stack.299.where_ref, bf16[256,1536]{1,0:T(8,128)(2,1)} %bitcast.171, ...), custom_call_target="tpu_custom_call" | custom-call | flops 1610612736 | bytes 16957568 | tf_op jit(solution)/shard_map/attend/pallas_call | solution.py:46
  137.8 6.4 project.1
  145.8 4.7 collective-permute-done.30
  153.8 12.0 %collective-permute-done.32.refs_0_ = bf16[272,1536]{1,0:T(8,128)(2,1)S(1)} collective-permute-done((bf16[272,1536]{1,0:T(8,128)(2,1)}, bf16[272,1536]{1,0:T(8,128)(2,1)S(1)}, u32[]{:S(2)}, u32[]{:S(2)}) %collective-permute-start.32) | collective-permute-done | bytes 835616 | tf_op jit(solution)/shard_map/ppermute | solution.py:384
  167.4 4.9 collective-permute-done.36.refs_4_
  173.6 9.1 %collective-permute-done.51.refs_1_ = bf16[256,1536]{1,0:T(8,128)(2,1)S(1)} collective-permute-done((bf16[256,1536]{1,0:T(8,128)(2,1)}, bf16[256,1536]{1,0:T(8,128)(2,1)S(1)}, u32[]{:S(2)}, u32[]{:S(2)}) %collective-permute-start.51) | collective-permute-done | bytes 786464 | tf_op jit(solution)/shard_map/ppermute | solution.py:384
  182.7 6.4 collective-permute-done.55.refs_5_
  192.2 8.4 %collective-permute-done.41.refs_0_ = bf16[272,1536]{1,0:T(8,128)(2,1)} collective-permute-done((bf16[272,1536]{1,0:T(8,128)(2,1)S(1)}, bf16[272,1536]{1,0:T(8,128)(2,1)}, u32[]{:S(2)}, u32[]{:S(2)}) %collective-permute-start.41) | collective-permute-done | bytes 835616 | tf_op jit(solution)/shard_map/ppermute | solution.py:384
  202.3 6.7 %collective-permute-done.61.refs_2_ = bf16[128,1536]{1,0:T(8,128)(2,1)S(1)} collective-permute-done((bf16[128,1536]{1,0:T(8,128)(2,1)S(1)}, bf16[128,1536]{1,0:T(8,128)(2,1)S(1)}, u32[]{:S(2)}, u32[]{:S(2)}) %collective-permute-start.61) | collective-permute-done | bytes 393248 | tf_op jit(solution)/shard_map/ppermute | solution.py:384
  209.3 4.7 collective-permute-done.62.refs_3_
  217.7 8.9 %collective-permute-done.50.refs_0_ = bf16[272,1536]{1,0:T(8,128)(2,1)} collective-permute-done((bf16[272,1536]{1,0:T(8,128)(2,1)}, bf16[272,1536]{1,0:T(8,128)(2,1)}, u32[]{:S(2)}, u32[]{:S(2)}) %collective-permute-start.50) | collective-permute-done | bytes 835616 | tf_op jit(solution)/shard_map/ppermute | solution.py:384
  231.9 3.5 collective-permute-done.54.refs_4_
  243.1 8.0 %collective-permute-done.60.refs_1_ = bf16[144,1536]{1,0:T(8,128)(2,1)S(1)} collective-permute-done((bf16[144,1536]{1,0:T(8,128)(2,1)S(1)}, bf16[144,1536]{1,0:T(8,128)(2,1)S(1)}, u32[]{:S(2)}, u32[]{:S(2)}) %collective-permute-start.60) | collective-permute-done | bytes 442400 | tf_op jit(solution)/shard_map/ppermute | solution.py:387
  251.1 11.0 %experts.5 = (bf16[256,1536]{1,0:T(8,128)(2,1)}, bf16[256,1536]{1,0:T(8,128)(2,1)}, bf16[272,1536]{1,0:T(8,128)(2,1)}, bf16[272,1536]{1,0:T(8,128)(2,1)}, bf16[1...) custom-call(s32[1]{0:T(128)} %bitcast.56.which_ref, ...), custom_call_target="tpu_custom_call" | custom-call | flops 2264924160 | bytes 15286276 | tf_op jit(solution)/shard_map/experts/pallas_call | solution.py:46
  263.6 16.4 %experts.8 = (bf16[256,1536]{1,0:T(8,128)(2,1)}, bf16[256,1536]{1,0:T(8,128)(2,1)}, bf16[256,1536]{1,0:T(8,128)(2,1)}, bf16[256,1536]{1,0:T(8,128)(2,1)}, bf16[2...) custom-call(s32[1]{0:T(128)} %bitcast.56.which_ref, ...), custom_call_target="tpu_custom_call" | custom-call | flops 4529848320 | bytes 23494660 | tf_op jit(solution)/shard_map/experts/pallas_call | solution.py:46
  280.5 16.4 %experts.6 = (bf16[256,1536]{1,0:T(8,128)(2,1)}, bf16[256,1536]{1,0:T(8,128)(2,1)}, bf16[256,1536]{1,0:T(8,128)(2,1)}, bf16[256,1536]{1,0:T(8,128)(2,1)}, bf16[2...) custom-call(s32[1]{0:T(128)} %bitcast.56.which_ref, ...), custom_call_target="tpu_custom_call" | custom-call | flops 4529848320 | bytes 23494660 | tf_op jit(solution)/shard_map/experts/pallas_call | solution.py:46
  296.9 10.9 %experts.9 = (bf16[256,1536]{1,0:T(8,128)(2,1)}, bf16[256,1536]{1,0:T(8,128)(2,1)}, bf16[272,1536]{1,0:T(8,128)(2,1)}, bf16[272,1536]{1,0:T(8,128)(2,1)}, bf16[1...) custom-call(s32[1]{0:T(128)} %bitcast.56.which_ref, ...), custom_call_target="tpu_custom_call" | custom-call | flops 2264924160 | bytes 15286276 | tf_op jit(solution)/shard_map/experts/pallas_call | solution.py:46
  309.3 16.6 %experts.7 = (bf16[256,1536]{1,0:T(8,128)(2,1)}, bf16[256,1536]{1,0:T(8,128)(2,1)}, bf16[256,1536]{1,0:T(8,128)(2,1)}, bf16[256,1536]{1,0:T(8,128)(2,1)}, bf16[2...) custom-call(s32[1]{0:T(128)} %bitcast.56.which_ref, ...), custom_call_target="tpu_custom_call" | custom-call | flops 4529848320 | bytes 23494660 | tf_op jit(solution)/shard_map/experts/pallas_call | solution.py:46
  327.4 3.5 collective-permute-done.90
  332.8 9.3 %collective-permute-done.84 = bf16[128,1536]{1,0:T(8,128)(2,1)S(1)} collective-permute-done((bf16[128,1536]{1,0:T(8,128)(2,1)S(1)}, bf16[128,1536]{1,0:T(8,128)(2,1)S(1)}, u32[]{:S(2)}, u32[]{:S(2)}) %collective-permute-start.84) | collective-permute-done | bytes 393248 | tf_op jit(solution)/shard_map/ppermute | solution.py:384
  343.5 10.0 %collective-permute-done.91 = bf16[144,1536]{1,0:T(8,128)(2,1)S(1)} collective-permute-done((bf16[144,1536]{1,0:T(8,128)(2,1)S(1)}, bf16[144,1536]{1,0:T(8,128)(2,1)S(1)}, u32[]{:S(2)}, u32[]{:S(2)}) %collective-permute-start.91) | collective-permute-done | bytes 442400 | tf_op jit(solution)/shard_map/ppermute | solution.py:387
  356.6 15.9 %collective-permute-done.85 = bf16[272,1536]{1,0:T(8,128)(2,1)S(1)} collective-permute-done((bf16[272,1536]{1,0:T(8,128)(2,1)S(1)}, bf16[272,1536]{1,0:T(8,128)(2,1)S(1)}, u32[]{:S(2)}, u32[]{:S(2)}) %collective-permute-start.85) | collective-permute-done | bytes 835616 | tf_op jit(solution)/shard_map/ppermute | solution.py:384
  376.0 17.9 %collective-permute-done.86 = bf16[272,1536]{1,0:T(8,128)(2,1)S(1)} collective-permute-done((bf16[272,1536]{1,0:T(8,128)(2,1)S(1)}, bf16[272,1536]{1,0:T(8,128)(2,1)S(1)}, u32[]{:S(2)}, u32[]{:S(2)}) %collective-permute-start.86) | collective-permute-done | bytes 835616 | tf_op jit(solution)/shard_map/ppermute | solution.py:384
  399.2 6.6 collective-permute-done.75
  411.0 13.6 %collective-permute-done.87.c_ref = bf16[272,1536]{1,0:T(8,128)(2,1)S(1)} collective-permute-done((bf16[272,1536]{1,0:T(8,128)(2,1)S(1)}, bf16[272,1536]{1,0:T(8,128)(2,1)S(1)}, u32[]{:S(2)}, u32[]{:S(2)}) %collective-permute-start.87) | collective-permute-done | bytes 835616 | tf_op jit(solution)/shard_map/ppermute | solution.py:384
  428.2 10.4 %hidden_back.1 = (f32[256,1536]{1,0:T(8,128)}, bf16[256,1536]{1,0:T(8,128)(2,1)}, bf16[1536,1536]{1,0:T(8,128)(2,1)}, f32[1536,128]{1,0:T(8,128)}, f32[8,1536]{1,0:T(8,128)}) custom-call(bf16[272,1536]{1,0:T(8,128)(2,1)} %get-tuple-element.118.a_ref, bf16[272,1536]{1,0:T(8,128)(2,1)} %copy-done.14, bf16[272,1536]{1,0:T(8,128)(2,1)} %copy-done.15, ...), custom_call_target="tpu_custom_call" | custom-call | flops 2415919104 | bytes 19693568 | tf_op jit(solution)/shard_map/hidden_back/pallas_call | solution.py:46
  438.6 15.4 %attend_back.1 = (f32[256,1536]{1,0:T(8,128)}, bf16[1536,2176]{1,0:T(8,128)(2,1)}, bf16[256,2048]{1,0:T(8,128)(2,1)}) custom-call(bf16[256,1536]{1,0:T(8,128)(2,1)} %bitcast.173, f32[128,128]{1,0:T(8,128)} %constant.672.clone.cos_ref, f32[128,128]{1,0:T(8,128)} %constant.673.clone.sin_ref, bf16[1536,2176]{1,0:T(8,128)(2,1)} %get-tuple-element.95.w_ref, ...), custom_call_target="tpu_custom_call" | custom-call | flops 3221225472 | bytes 21987328 | tf_op jit(solution)/shard_map/attend_back/pallas_call | solution.py:46
  454.1 4.0 dynamic-slice_bitcast_fusion
  459.9 3.4 dynamic-slice_bitcast_fusion.1
  466.6 11.5 %collective-permute-done.69 = bf16[256,1536]{1,0:T(8,128)(2,1)S(1)} collective-permute-done((bf16[256,1536]{1,0:T(8,128)(2,1)S(1)}, bf16[256,1536]{1,0:T(8,128)(2,1)S(1)}, u32[]{:S(2)}, u32[]{:S(2)}) %collective-permute-start.69) | collective-permute-done | bytes 786464 | tf_op jit(solution)/shard_map/ppermute | solution.py:384
  482.7 13.8 %expert_weights.2 = (bf16[768,768]{1,0:T(8,128)(2,1)}, bf16[768,768]{1,0:T(8,128)(2,1)}, bf16[384,1536]{1,0:T(8,128)(2,1)}) custom-call(s32[1]{0:T(128)} %bitcast.95.which_ref, bf16[160,1536]{1,0:T(8,128)(2,1)} %get-tuple-element.143.refs_0_, bf16[320,1536]{1,0:T(8,128)(2,1)} %get-tuple-element.144.refs_1_, bf16[320,1536]{1,0:T(8,128)(2,1)} %get-tuple-element.145.refs_2_, ...), custom_call_target="tpu_custom_call" | custom-call | flops 4529848320 | bytes 17301508 | tf_op jit(solution)/shard_map/expert_weights/pallas_call | solution.py:46
  507.6 18.1 %collective-permute-done.113.refs_25_ = bf16[768,768]{1,0:T(8,128)(2,1)S(1)} collective-permute-done((bf16[768,768]{1,0:T(8,128)(2,1)}, bf16[768,768]{1,0:T(8,128)(2,1)S(1)}, u32[]{:S(2)}, u32[]{:S(2)}) %collective-permute-start.113) | collective-permute-done | bytes 1179680 | tf_op jit(solution)/shard_map/ppermute | solution.py:441
  527.3 23.7 %collective-permute-done.114.refs_26_ = bf16[768,768]{1,0:T(8,128)(2,1)S(1)} collective-permute-done((bf16[768,768]{1,0:T(8,128)(2,1)}, bf16[768,768]{1,0:T(8,128)(2,1)S(1)}, u32[]{:S(2)}, u32[]{:S(2)}) %collective-permute-start.114) | collective-permute-done | bytes 1179680 | tf_op jit(solution)/shard_map/ppermute | solution.py:441
  557.4 18.9 %collective-permute-done.115.refs_27_ = bf16[384,1536]{1,0:T(8,128)(2,1)S(1)} collective-permute-done((bf16[384,1536]{1,0:T(8,128)(2,1)S(1)}, bf16[384,1536]{1,0:T(8,128)(2,1)S(1)}, u32[]{:S(2)}, u32[]{:S(2)}) %collective-permute-start.115) | collective-permute-done | bytes 1179680 | tf_op jit(solution)/shard_map/ppermute | solution.py:441
  577.8 16.1 %expert_weights.3 = (f32[768,768]{1,0:T(8,128)}, f32[768,768]{1,0:T(8,128)}, f32[384,1536]{1,0:T(8,128)}) custom-call(s32[1]{0:T(128)} %bitcast.94.which_ref, bf16[160,1536]{1,0:T(8,128)(2,1)} %get-tuple-element.143.refs_0_, bf16[320,1536]{1,0:T(8,128)(2,1)} %get-tuple-element.144.refs_1_, bf16[320,1536]{1,0:T(8,128)(2,1)} %get-tuple-element.145.refs_2_, ...), custom_call_target="tpu_custom_call" | custom-call | flops 4529848320 | bytes 24379396 | tf_op jit(solution)/shard_map/expert_weights/pallas_call | solution.py:46
  593.9 3.2 add_convert_fusion.5
  597.2 4.5 collective-permute-done.105
  606.2 29.6 %collective-permute-done.96 = bf16[8,48,2176]{2,1,0:T(8,128)(2,1)S(1)} collective-permute-done((bf16[8,48,2176]{2,1,0:T(8,128)(2,1)}, bf16[8,48,2176]{2,1,0:T(8,128)(2,1)S(1)}, u32[]{:S(2)}, u32[]{:S(2)}) %collective-permute-start.96) | collective-permute-done | bytes 1671200 | tf_op jit(solution)/shard_map/ppermute | solution.py:441
  641.4 4.7 collective-permute-done.97
  (415 shorter events, 165.2 us)
Async XLA Ops:
  3.7 45.1 %collective-permute-start.33 = (bf16[256,1536]{1,0:T(8,128)(2,1)}, bf16[256,1536]{1,0:T(8,128)(2,1)}, u32[]{:S(2)}, u32[]{:S(2)}) collective-permute-start(bf16[256,1536]{1,0:T(8,128)(2,1)} %bitcast.180), channel_id=1, source_target_pairs={{0,4},{1,5},{4,8},{5,9},{8,12},{9,13},{12,14},{13,15},{14,10},{15,... | collective-permute-start | bytes 2359304 | tf_op jit(solution)/shard_map/ppermute | solution.py:384
  5.8 43.6 %collective-permute-start.37 = (bf16[256,1536]{1,0:T(8,128)(2,1)}, bf16[256,1536]{1,0:T(8,128)(2,1)}, u32[]{:S(2)}, u32[]{:S(2)}) collective-permute-start(bf16[256,1536]{1,0:T(8,128)(2,1)} %bitcast.181), channel_id=1, source_target_pairs={{4,0},{5,1},{8,4},{9,5},{12,8},{13,9},{14,12},{15,13},{10,14},{11,... | collective-permute-start | bytes 2359304 | tf_op jit(solution)/shard_map/ppermute | solution.py:387
  15.3 24.9 %collective-permute-start.1 = (bf16[2,48,2176]{2,1,0:T(8,128)(2,1)S(1)}, bf16[2,48,2176]{2,1,0:T(8,128)(2,1)S(1)}, u32[]{:S(2)}, u32[]{:S(2)}) collective-permute-start(bf16[2,48,2176]{2,1,0:T(8,128)(2,1)S(1)} %pad_maximum_fusion.7.refs_0_), channel_id=1, source_target_pairs={{0,1},{1,0},{2,3},{3,2},{4,5},{5,4},{6,7},{7,6},{8,9},{9,8},{10,11... | collective-permute-start | bytes 1253384 | tf_op jit(solution)/shard_map/ppermute | solution.py:390
  47.0 29.0 %collective-permute-start.29 = (bf16[768,768]{1,0:T(8,128)(2,1)S(1)}, bf16[768,768]{1,0:T(8,128)(2,1)S(1)}, u32[]{:S(2)}, u32[]{:S(2)}) collective-permute-start(bf16[768,768]{1,0:T(8,128)(2,1)S(1)} %bitcast.185), channel_id=1, source_target_pairs={{0,16},{16,0},{1,17},{17,1},{2,18},{18,2},{3,19},{19,3},{4,20},{20... | collective-permute-start | bytes 3538952 | tf_op jit(solution)/shard_map/ppermute | solution.py:441
  49.4 47.1 %collective-permute-start.24 = (bf16[8,48,1536]{2,1,0:T(8,128)(2,1)S(1)}, bf16[8,48,1536]{2,1,0:T(8,128)(2,1)}, u32[]{:S(2)}, u32[]{:S(2)}) collective-permute-start(bf16[8,48,1536]{2,1,0:T(8,128)(2,1)S(1)} %bitcast_dynamic-update-slice_fusion.1.refs_0_), channel_id=1, source_target_pairs={{0,16},{16,0},{1,17},{17,1},{2,18},{18,2},{3,19},{19,3},{4,20},{20... | collective-permute-start | bytes 3538952 | tf_op jit(solution)/shard_map/ppermute | solution.py:441
  52.4 47.5 %collective-permute-start.23 = (bf16[8,48,1536]{2,1,0:T(8,128)(2,1)S(1)}, bf16[8,48,1536]{2,1,0:T(8,128)(2,1)S(1)}, u32[]{:S(2)}, u32[]{:S(2)}) collective-permute-start(bf16[8,48,1536]{2,1,0:T(8,128)(2,1)S(1)} %bitcast_dynamic-update-slice_fusion.1.refs_0_), channel_id=1, source_target_pairs={{0,1},{1,0},{2,3},{3,2},{4,5},{5,4},{6,7},{7,6},{8,9},{9,8},{10,11... | collective-permute-start | bytes 3538952 | tf_op jit(solution)/shard_map/ppermute | solution.py:390
  96.5 41.3 %collective-permute-start.25 = (bf16[8,48,1536]{2,1,0:T(8,128)(2,1)}, bf16[8,48,1536]{2,1,0:T(8,128)(2,1)}, u32[]{:S(2)}, u32[]{:S(2)}) collective-permute-start(bf16[8,48,1536]{2,1,0:T(8,128)(2,1)} %collective-permute-done.24.refs_2_), channel_id=1, source_target_pairs={{0,1},{1,0},{2,3},{3,2},{4,5},{5,4},{6,7},{7,6},{8,9},{9,8},{10,11... | collective-permute-start | bytes 3538952 | tf_op jit(solution)/shard_map/ppermute | solution.py:390
  96.5 47.7 %collective-permute-start.28 = (bf16[768,768]{1,0:T(8,128)(2,1)}, bf16[768,768]{1,0:T(8,128)(2,1)}, u32[]{:S(2)}, u32[]{:S(2)}) collective-permute-start(bf16[768,768]{1,0:T(8,128)(2,1)} %bitcast.58), channel_id=1, source_target_pairs={{0,16},{16,0},{1,17},{17,1},{2,18},{18,2},{3,19},{19,3},{4,20},{20... | collective-permute-start | bytes 3538952 | tf_op jit(solution)/shard_map/ppermute | solution.py:441
  100.9 49.6 %collective-permute-start.30 = (bf16[384,1536]{1,0:T(8,128)(2,1)}, bf16[384,1536]{1,0:T(8,128)(2,1)}, u32[]{:S(2)}, u32[]{:S(2)}) collective-permute-start(bf16[384,1536]{1,0:T(8,128)(2,1)} %bitcast.60), channel_id=1, source_target_pairs={{0,16},{16,0},{1,17},{17,1},{2,18},{18,2},{3,19},{19,3},{4,20},{20... | collective-permute-start | bytes 3538952 | tf_op jit(solution)/shard_map/ppermute | solution.py:441
  110.1 41.6 %collective-permute-start.42 = (bf16[256,1536]{1,0:T(8,128)(2,1)}, bf16[256,1536]{1,0:T(8,128)(2,1)}, u32[]{:S(2)}, u32[]{:S(2)}) collective-permute-start(bf16[256,1536]{1,0:T(8,128)(2,1)} %collective-permute-done.33.refs_1_), channel_id=1, source_target_pairs={{0,4},{1,5},{4,8},{5,9},{8,12},{9,13},{12,14},{13,15},{14,10},{15,... | collective-permute-start | bytes 2359304 | tf_op jit(solution)/shard_map/ppermute | solution.py:384
  127.0 25.4 %collective-permute-start.46 = (bf16[256,1536]{1,0:T(8,128)(2,1)}, bf16[256,1536]{1,0:T(8,128)(2,1)}, u32[]{:S(2)}, u32[]{:S(2)}) collective-permute-start(bf16[256,1536]{1,0:T(8,128)(2,1)} %collective-permute-done.37.refs_5_), channel_id=1, source_target_pairs={{4,0},{5,1},{8,4},{9,5},{12,8},{13,9},{14,12},{15,13},{10,14},{11,... | collective-permute-start | bytes 2359304 | tf_op jit(solution)/shard_map/ppermute | solution.py:387
  151.7 30.9 %collective-permute-start.51 = (bf16[256,1536]{1,0:T(8,128)(2,1)}, bf16[256,1536]{1,0:T(8,128)(2,1)S(1)}, u32[]{:S(2)}, u32[]{:S(2)}) collective-permute-start(bf16[256,1536]{1,0:T(8,128)(2,1)} %collective-permute-done.42.refs_1_), channel_id=1, source_target_pairs={{0,4},{1,5},{4,8},{5,9},{8,12},{9,13},{12,14},{13,15},{14,10},{15,... | collective-permute-start | bytes 2359304 | tf_op jit(solution)/shard_map/ppermute | solution.py:384
  152.5 36.6 %collective-permute-start.55 = (bf16[256,1536]{1,0:T(8,128)(2,1)}, bf16[256,1536]{1,0:T(8,128)(2,1)}, u32[]{:S(2)}, u32[]{:S(2)}) collective-permute-start(bf16[256,1536]{1,0:T(8,128)(2,1)} %collective-permute-done.46.refs_5_), channel_id=1, source_target_pairs={{4,0},{5,1},{8,4},{9,5},{12,8},{13,9},{14,12},{15,13},{10,14},{11,... | collective-permute-start | bytes 2359304 | tf_op jit(solution)/shard_map/ppermute | solution.py:387
  153.8 38.2 %collective-permute-start.39 = (bf16[256,1536]{1,0:T(8,128)(2,1)}, bf16[256,1536]{1,0:T(8,128)(2,1)S(1)}, u32[]{:S(2)}, u32[]{:S(2)}) collective-permute-start(bf16[256,1536]{1,0:T(8,128)(2,1)} %collective-permute-done.37.refs_5_), channel_id=1, source_target_pairs={{0,1},{1,0},{2,3},{3,2},{4,5},{5,4},{6,7},{7,6},{8,9},{9,8},{10,11... | collective-permute-start | bytes 2359304 | tf_op jit(solution)/shard_map/ppermute | solution.py:390
  165.8 34.9 %collective-permute-start.41 = (bf16[272,1536]{1,0:T(8,128)(2,1)S(1)}, bf16[272,1536]{1,0:T(8,128)(2,1)}, u32[]{:S(2)}, u32[]{:S(2)}) collective-permute-start(bf16[272,1536]{1,0:T(8,128)(2,1)S(1)} %collective-permute-done.32.refs_0_), channel_id=1, source_target_pairs={{0,4},{1,5},{4,8},{5,9},{8,12},{9,13},{12,14},{13,15},{14,10},{15,... | collective-permute-start | bytes 2506760 | tf_op jit(solution)/shard_map/ppermute | solution.py:384
  172.3 42.3 %collective-permute-start.45 = (bf16[272,1536]{1,0:T(8,128)(2,1)}, bf16[272,1536]{1,0:T(8,128)(2,1)}, u32[]{:S(2)}, u32[]{:S(2)}) collective-permute-start(bf16[272,1536]{1,0:T(8,128)(2,1)} %collective-permute-done.36.refs_4_), channel_id=1, source_target_pairs={{4,0},{5,1},{8,4},{9,5},{12,8},{13,9},{14,12},{15,13},{10,14},{11,... | collective-permute-start | bytes 2506760 | tf_op jit(solution)/shard_map/ppermute | solution.py:387
  182.7 31.4 %collective-permute-start.53 = (bf16[256,1536]{1,0:T(8,128)(2,1)S(1)}, bf16[256,1536]{1,0:T(8,128)(2,1)}, u32[]{:S(2)}, u32[]{:S(2)}) collective-permute-start(bf16[256,1536]{1,0:T(8,128)(2,1)S(1)} %collective-permute-done.51.refs_1_), channel_id=1, source_target_pairs={{0,1},{1,0},{2,3},{3,2},{4,5},{5,4},{6,7},{7,6},{8,9},{9,8},{10,11... | collective-permute-start | bytes 2359304 | tf_op jit(solution)/shard_map/ppermute | solution.py:390
  200.7 25.9 %collective-permute-start.50 = (bf16[272,1536]{1,0:T(8,128)(2,1)}, bf16[272,1536]{1,0:T(8,128)(2,1)}, u32[]{:S(2)}, u32[]{:S(2)}) collective-permute-start(bf16[272,1536]{1,0:T(8,128)(2,1)} %collective-permute-done.41.refs_0_), channel_id=1, source_target_pairs={{0,4},{1,5},{4,8},{5,9},{8,12},{9,13},{12,14},{13,15},{14,10},{15,... | collective-permute-start | bytes 2506760 | tf_op jit(solution)/shard_map/ppermute | solution.py:384
  229.8 32.3 %collective-permute-start.38 = (bf16[272,1536]{1,0:T(8,128)(2,1)}, bf16[272,1536]{1,0:T(8,128)(2,1)}, u32[]{:S(2)}, u32[]{:S(2)}) collective-permute-start(bf16[272,1536]{1,0:T(8,128)(2,1)} %collective-permute-done.36.refs_4_), channel_id=1, source_target_pairs={{0,1},{1,0},{2,3},{3,2},{4,5},{5,4},{6,7},{7,6},{8,9},{9,8},{10,11... | collective-permute-start | bytes 2506760 | tf_op jit(solution)/shard_map/ppermute | solution.py:390
  231.9 30.7 %collective-permute-start.52 = (bf16[272,1536]{1,0:T(8,128)(2,1)}, bf16[272,1536]{1,0:T(8,128)(2,1)S(1)}, u32[]{:S(2)}, u32[]{:S(2)}) collective-permute-start(bf16[272,1536]{1,0:T(8,128)(2,1)} %collective-permute-done.50.refs_0_), channel_id=1, source_target_pairs={{0,1},{1,0},{2,3},{3,2},{4,5},{5,4},{6,7},{7,6},{8,9},{9,8},{10,11... | collective-permute-start | bytes 2506760 | tf_op jit(solution)/shard_map/ppermute | solution.py:390
  235.5 27.6 %collective-permute-start.56 = (bf16[272,1536]{1,0:T(8,128)(2,1)}, bf16[272,1536]{1,0:T(8,128)(2,1)}, u32[]{:S(2)}, u32[]{:S(2)}) collective-permute-start(bf16[272,1536]{1,0:T(8,128)(2,1)} %collective-permute-done.54.refs_4_), channel_id=1, source_target_pairs={{0,1},{1,0},{2,3},{3,2},{4,5},{5,4},{6,7},{7,6},{8,9},{9,8},{10,11... | collective-permute-start | bytes 2506760 | tf_op jit(solution)/shard_map/ppermute | solution.py:390
  251.1 28.9 %collective-permute-start.64 = (bf16[144,1536]{1,0:T(8,128)(2,1)S(1)}, bf16[144,1536]{1,0:T(8,128)(2,1)S(1)}, u32[]{:S(2)}, u32[]{:S(2)}) collective-permute-start(bf16[144,1536]{1,0:T(8,128)(2,1)S(1)} %collective-permute-done.60.refs_1_), channel_id=1, source_target_pairs={{0,1},{1,0},{2,3},{3,2},{4,5},{5,4},{6,7},{7,6},{8,9},{9,8},{10,11... | collective-permute-start | bytes 1327112 | tf_op jit(solution)/shard_map/ppermute | solution.py:390
  262.1 45.7 %collective-permute-start.44 = (bf16[256,1536]{1,0:T(8,128)(2,1)}, bf16[256,1536]{1,0:T(8,128)(2,1)S(1)}, u32[]{:S(2)}, u32[]{:S(2)}) collective-permute-start(bf16[256,1536]{1,0:T(8,128)(2,1)} %collective-permute-done.42.refs_1_), channel_id=1, source_target_pairs={{0,1},{1,0},{2,3},{3,2},{4,5},{5,4},{6,7},{7,6},{8,9},{9,8},{10,11... | collective-permute-start | bytes 2359304 | tf_op jit(solution)/shard_map/ppermute | solution.py:390
  262.5 45.5 %collective-permute-start.48 = (bf16[256,1536]{1,0:T(8,128)(2,1)}, bf16[256,1536]{1,0:T(8,128)(2,1)S(1)}, u32[]{:S(2)}, u32[]{:S(2)}) collective-permute-start(bf16[256,1536]{1,0:T(8,128)(2,1)} %collective-permute-done.46.refs_5_), channel_id=1, source_target_pairs={{0,1},{1,0},{2,3},{3,2},{4,5},{5,4},{6,7},{7,6},{8,9},{9,8},{10,11... | collective-permute-start | bytes 2359304 | tf_op jit(solution)/shard_map/ppermute | solution.py:390
  262.7 46.6 %collective-permute-start.43 = (bf16[272,1536]{1,0:T(8,128)(2,1)}, bf16[272,1536]{1,0:T(8,128)(2,1)}, u32[]{:S(2)}, u32[]{:S(2)}) collective-permute-start(bf16[272,1536]{1,0:T(8,128)(2,1)} %collective-permute-done.41.refs_0_), channel_id=1, source_target_pairs={{0,1},{1,0},{2,3},{3,2},{4,5},{5,4},{6,7},{7,6},{8,9},{9,8},{10,11... | collective-permute-start | bytes 2506760 | tf_op jit(solution)/shard_map/ppermute | solution.py:390
  263.0 46.2 %collective-permute-start.47 = (bf16[272,1536]{1,0:T(8,128)(2,1)}, bf16[272,1536]{1,0:T(8,128)(2,1)}, u32[]{:S(2)}, u32[]{:S(2)}) collective-permute-start(bf16[272,1536]{1,0:T(8,128)(2,1)} %collective-permute-done.45.refs_4_), channel_id=1, source_target_pairs={{0,1},{1,0},{2,3},{3,2},{4,5},{5,4},{6,7},{7,6},{8,9},{9,8},{10,11... | collective-permute-start | bytes 2506760 | tf_op jit(solution)/shard_map/ppermute | solution.py:390
  280.0 46.4 %collective-permute-start.82 = (bf16[272,1536]{1,0:T(8,128)(2,1)}, bf16[272,1536]{1,0:T(8,128)(2,1)S(1)}, u32[]{:S(2)}, u32[]{:S(2)}) collective-permute-start(bf16[272,1536]{1,0:T(8,128)(2,1)} %get-tuple-element.125), channel_id=1, source_target_pairs={{0,1},{1,0},{2,3},{3,2},{4,5},{5,4},{6,7},{7,6},{8,9},{9,8},{10,11... | collective-permute-start | bytes 2506760 | tf_op jit(solution)/shard_map/ppermute | solution.py:390
  307.8 101.2 %collective-permute-start.79 = (bf16[272,1536]{1,0:T(8,128)(2,1)}, bf16[272,1536]{1,0:T(8,128)(2,1)S(1)}, u32[]{:S(2)}, u32[]{:S(2)}) collective-permute-start(bf16[272,1536]{1,0:T(8,128)(2,1)} %get-tuple-element.119), channel_id=1, source_target_pairs={{0,1},{1,0},{2,3},{3,2},{4,5},{5,4},{6,7},{7,6},{8,9},{9,8},{10,11... | collective-permute-start | bytes 2506760 | tf_op jit(solution)/shard_map/ppermute | solution.py:390
  325.9 30.2 %collective-permute-start.81 = (bf16[272,1536]{1,0:T(8,128)(2,1)}, bf16[272,1536]{1,0:T(8,128)(2,1)S(1)}, u32[]{:S(2)}, u32[]{:S(2)}) collective-permute-start(bf16[272,1536]{1,0:T(8,128)(2,1)} %get-tuple-element.123), channel_id=1, source_target_pairs={{0,1},{1,0},{2,3},{3,2},{4,5},{5,4},{6,7},{7,6},{8,9},{9,8},{10,11... | collective-permute-start | bytes 2506760 | tf_op jit(solution)/shard_map/ppermute | solution.py:390
  326.1 46.7 %collective-permute-start.89 = (bf16[272,1536]{1,0:T(8,128)(2,1)}, bf16[272,1536]{1,0:T(8,128)(2,1)S(1)}, u32[]{:S(2)}, u32[]{:S(2)}) collective-permute-start(bf16[272,1536]{1,0:T(8,128)(2,1)} %get-tuple-element.131), channel_id=1, source_target_pairs={{0,1},{1,0},{2,3},{3,2},{4,5},{5,4},{6,7},{7,6},{8,9},{9,8},{10,11... | collective-permute-start | bytes 2506760 | tf_op jit(solution)/shard_map/ppermute | solution.py:390
  326.8 28.8 %collective-permute-start.67 = (bf16[256,1536]{1,0:T(8,128)(2,1)}, bf16[256,1536]{1,0:T(8,128)(2,1)S(1)}, u32[]{:S(2)}, u32[]{:S(2)}) collective-permute-start(bf16[256,1536]{1,0:T(8,128)(2,1)} %get-tuple-element.107), channel_id=1, source_target_pairs={{0,1},{1,0},{2,3},{3,2},{4,5},{5,4},{6,7},{7,6},{8,9},{9,8},{10,11... | collective-permute-start | bytes 2359304 | tf_op jit(solution)/shard_map/ppermute | solution.py:390
  397.6 27.0 %collective-permute-start.87 = (bf16[272,1536]{1,0:T(8,128)(2,1)S(1)}, bf16[272,1536]{1,0:T(8,128)(2,1)S(1)}, u32[]{:S(2)}, u32[]{:S(2)}) collective-permute-start(bf16[272,1536]{1,0:T(8,128)(2,1)S(1)} %add_convert_fusion.2), channel_id=1, source_target_pairs={{0,4},{1,5},{4,8},{5,9},{8,12},{9,13},{12,14},{13,15},{14,10},{15,... | collective-permute-start | bytes 2506760 | tf_op jit(solution)/shard_map/ppermute | solution.py:384
  408.2 55.0 %collective-permute-start.73 = (bf16[256,1536]{1,0:T(8,128)(2,1)}, bf16[256,1536]{1,0:T(8,128)(2,1)}, u32[]{:S(2)}, u32[]{:S(2)}) collective-permute-start(bf16[256,1536]{1,0:T(8,128)(2,1)} %get-tuple-element.111), channel_id=1, source_target_pairs={{0,1},{1,0},{2,3},{3,2},{4,5},{5,4},{6,7},{7,6},{8,9},{9,8},{10,11... | collective-permute-start | bytes 2359304 | tf_op jit(solution)/shard_map/ppermute | solution.py:390
  408.2 58.2 %collective-permute-start.49 = (bf16[256,1536]{1,0:T(8,128)(2,1)}, bf16[256,1536]{1,0:T(8,128)(2,1)}, u32[]{:S(2)}, u32[]{:S(2)}) collective-permute-start(bf16[256,1536]{1,0:T(8,128)(2,1)} %get-tuple-element.103), channel_id=1, source_target_pairs={{0,1},{1,0},{2,3},{3,2},{4,5},{5,4},{6,7},{7,6},{8,9},{9,8},{10,11... | collective-permute-start | bytes 2359304 | tf_op jit(solution)/shard_map/ppermute | solution.py:390
  409.0 54.5 %collective-permute-start.76 = (bf16[256,1536]{1,0:T(8,128)(2,1)}, bf16[256,1536]{1,0:T(8,128)(2,1)}, u32[]{:S(2)}, u32[]{:S(2)}) collective-permute-start(bf16[256,1536]{1,0:T(8,128)(2,1)} %pad_maximum_fusion.6), channel_id=1, source_target_pairs={{4,0},{5,1},{8,4},{9,5},{12,8},{13,9},{14,12},{15,13},{10,14},{11,... | collective-permute-start | bytes 2359304 | tf_op jit(solution)/shard_map/ppermute | solution.py:387
  458.0 94.8 %collective-permute-start.95 = (bf16[2,8,48,2176]{3,2,1,0:T(8,128)(2,1)}, bf16[2,8,48,2176]{3,2,1,0:T(8,128)(2,1)S(1)}, u32[]{:S(2)}, u32[]{:S(2)}) collective-permute-start(bf16[2,8,48,2176]{3,2,1,0:T(8,128)(2,1)} %dynamic-slice_bitcast_fusion), channel_id=1, source_target_pairs={{0,1},{1,0},{2,3},{3,2},{4,5},{5,4},{6,7},{7,6},{8,9},{9,8},{10,11... | collective-permute-start | bytes 10027016 | tf_op jit(solution)/shard_map/ppermute | solution.py:390
  463.5 41.1 %collective-permute-start.104 = (bf16[2,8,48,1536]{3,2,1,0:T(8,128)(2,1)}, bf16[2,8,48,1536]{3,2,1,0:T(8,128)(2,1)}, u32[]{:S(2)}, u32[]{:S(2)}) collective-permute-start(bf16[2,8,48,1536]{3,2,1,0:T(8,128)(2,1)} %dynamic-slice_bitcast_fusion.1), channel_id=1, source_target_pairs={{0,1},{1,0},{2,3},{3,2},{4,5},{5,4},{6,7},{7,6},{8,9},{9,8},{10,11... | collective-permute-start | bytes 7077896 | tf_op jit(solution)/shard_map/ppermute | solution.py:390
  466.4 30.2 %collective-permute-start.40 = (bf16[256,1536]{1,0:T(8,128)(2,1)}, bf16[256,1536]{1,0:T(8,128)(2,1)}, u32[]{:S(2)}, u32[]{:S(2)}) collective-permute-start(bf16[256,1536]{1,0:T(8,128)(2,1)} %get-tuple-element.101), channel_id=1, source_target_pairs={{0,1},{1,0},{2,3},{3,2},{4,5},{5,4},{6,7},{7,6},{8,9},{9,8},{10,11... | collective-permute-start | bytes 2359304 | tf_op jit(solution)/shard_map/ppermute | solution.py:390
  496.6 29.2 %collective-permute-start.113 = (bf16[768,768]{1,0:T(8,128)(2,1)}, bf16[768,768]{1,0:T(8,128)(2,1)S(1)}, u32[]{:S(2)}, u32[]{:S(2)}) collective-permute-start(bf16[768,768]{1,0:T(8,128)(2,1)} %get-tuple-element.168), channel_id=1, source_target_pairs={{0,16},{16,0},{1,17},{17,1},{2,18},{18,2},{3,19},{19,3},{4,20},{20... | collective-permute-start | bytes 3538952 | tf_op jit(solution)/shard_map/ppermute | solution.py:441
  498.1 52.9 %collective-permute-start.114 = (bf16[768,768]{1,0:T(8,128)(2,1)}, bf16[768,768]{1,0:T(8,128)(2,1)S(1)}, u32[]{:S(2)}, u32[]{:S(2)}) collective-permute-start(bf16[768,768]{1,0:T(8,128)(2,1)} %get-tuple-element.169), channel_id=1, source_target_pairs={{0,16},{16,0},{1,17},{17,1},{2,18},{18,2},{3,19},{19,3},{4,20},{20... | collective-permute-start | bytes 3538952 | tf_op jit(solution)/shard_map/ppermute | solution.py:441
  502.1 74.2 %collective-permute-start.115 = (bf16[384,1536]{1,0:T(8,128)(2,1)S(1)}, bf16[384,1536]{1,0:T(8,128)(2,1)S(1)}, u32[]{:S(2)}, u32[]{:S(2)}) collective-permute-start(bf16[384,1536]{1,0:T(8,128)(2,1)S(1)} %copy-done.59), channel_id=1, source_target_pairs={{0,16},{16,0},{1,17},{17,1},{2,18},{18,2},{3,19},{19,3},{4,20},{20... | collective-permute-start | bytes 3538952 | tf_op jit(solution)/shard_map/ppermute | solution.py:441
  504.5 89.4 %collective-permute-start.31 = (bf16[256,1536]{1,0:T(8,128)(2,1)}, bf16[256,1536]{1,0:T(8,128)(2,1)}, u32[]{:S(2)}, u32[]{:S(2)}) collective-permute-start(bf16[256,1536]{1,0:T(8,128)(2,1)} %get-tuple-element.99), channel_id=1, source_target_pairs={{0,1},{1,0},{2,3},{3,2},{4,5},{5,4},{6,7},{7,6},{8,9},{9,8},{10,11... | collective-permute-start | bytes 2359304 | tf_op jit(solution)/shard_map/ppermute | solution.py:390
  525.7 68.2 %collective-permute-start.78 = (bf16[256,1536]{1,0:T(8,128)(2,1)}, bf16[256,1536]{1,0:T(8,128)(2,1)}, u32[]{:S(2)}, u32[]{:S(2)}) collective-permute-start(bf16[256,1536]{1,0:T(8,128)(2,1)} %add_convert_fusion.6), channel_id=1, source_target_pairs={{4,0},{5,1},{8,4},{9,5},{12,8},{13,9},{14,12},{15,13},{10,14},{11,... | collective-permute-start | bytes 2359304 | tf_op jit(solution)/shard_map/ppermute | solution.py:387
  551.0 42.9 %collective-permute-start.71 = (bf16[256,1536]{1,0:T(8,128)(2,1)S(1)}, bf16[256,1536]{1,0:T(8,128)(2,1)}, u32[]{:S(2)}, u32[]{:S(2)}) collective-permute-start(bf16[256,1536]{1,0:T(8,128)(2,1)S(1)} %add_convert_fusion.8), channel_id=1, source_target_pairs={{0,4},{1,5},{4,8},{5,9},{8,12},{9,13},{12,14},{13,15},{14,10},{15,... | collective-permute-start | bytes 2359304 | tf_op jit(solution)/shard_map/ppermute | solution.py:384
  552.9 48.8 %collective-permute-start.105 = (bf16[8,48,1536]{2,1,0:T(8,128)(2,1)}, bf16[8,48,1536]{2,1,0:T(8,128)(2,1)}, u32[]{:S(2)}, u32[]{:S(2)}) collective-permute-start(bf16[8,48,1536]{2,1,0:T(8,128)(2,1)} %fusion.3), channel_id=1, source_target_pairs={{0,16},{16,0},{1,17},{17,1},{2,18},{18,2},{3,19},{19,3},{4,20},{20... | collective-permute-start | bytes 3538952 | tf_op jit(solution)/shard_map/ppermute | solution.py:441
  576.3 59.5 %collective-permute-start.96 = (bf16[8,48,2176]{2,1,0:T(8,128)(2,1)}, bf16[8,48,2176]{2,1,0:T(8,128)(2,1)S(1)}, u32[]{:S(2)}, u32[]{:S(2)}) collective-permute-start(bf16[8,48,2176]{2,1,0:T(8,128)(2,1)} %fusion), channel_id=1, source_target_pairs={{0,16},{16,0},{1,17},{17,1},{2,18},{18,2},{3,19},{19,3},{4,20},{20... | collective-permute-start | bytes 5013512 | tf_op jit(solution)/shard_map/ppermute | solution.py:441
  604.2 35.1 %collective-permute-start.106 = (bf16[48,1536]{1,0:T(8,128)(2,1)S(1)}, bf16[48,1536]{1,0:T(8,128)(2,1)S(1)}, u32[]{:S(2)}, u32[]{:S(2)}) collective-permute-start(bf16[48,1536]{1,0:T(8,128)(2,1)S(1)} %get-tuple-element.232), channel_id=1, source_target_pairs={{0,4},{1,5},{4,8},{5,9},{8,12},{9,13},{12,14},{13,15},{14,10},{15,... | collective-permute-start | bytes 442376 | tf_op jit(solution)/shard_map/ppermute | solution.py:384
  605.8 41.7 %collective-permute-start.110 = (bf16[48,1536]{1,0:T(8,128)(2,1)S(1)}, bf16[48,1536]{1,0:T(8,128)(2,1)S(1)}, u32[]{:S(2)}, u32[]{:S(2)}) collective-permute-start(bf16[48,1536]{1,0:T(8,128)(2,1)S(1)} %get-tuple-element.233), channel_id=1, source_target_pairs={{4,0},{5,1},{8,4},{9,5},{12,8},{13,9},{14,12},{15,13},{10,14},{11,... | collective-permute-start | bytes 442376 | tf_op jit(solution)/shard_map/ppermute | solution.py:387
  (141 other events, 2685.3 us)

commit v2 on v1

v2 whole, which is shorter than its diff:
```python
import functools
import math

import jax
import jax.numpy as jnp
import numpy as np
from jax import lax
from jax.experimental import pallas as pl
from jax.experimental.pallas import tpu as pltpu
from jax.sharding import PartitionSpec as P

WIDTH = 1536
QUERY_HEADS = 12
KEY_VALUE_HEADS = 2
HEAD = 128
GROUP = QUERY_HEADS // KEY_VALUE_HEADS
Q_COLS = QUERY_HEADS * HEAD
KV_COLS = KEY_VALUE_HEADS * HEAD
MISC = Q_COLS + 2 * KV_COLS
EXTRA = 16
LANES = 128
CHUNKS = 4
EPSILON = 1e-06
ROPE_BASE = 10000.0
MASKED = -1e30
SCALE = 1.0 / math.sqrt(HEAD)

f32 = jnp.float32
bf16 = jnp.bfloat16


def dot(a, b, ca=1, cb=0):
    return lax.dot_general(a, b, (((ca,), (cb,)), ((), ())), preferred_element_type=f32)


def vmem(n):
    return [pl.BlockSpec(memory_space=pltpu.VMEM)] * n


def smem():
    return pl.BlockSpec(memory_space=pltpu.SMEM)


def call(body, outs, ins, args, name, flops, scratch=()):
    return pl.pallas_call(
        body,
        out_shape=outs,
        in_specs=ins,
        out_specs=vmem(len(outs)),
        scratch_shapes=list(scratch),
        compiler_params=pltpu.CompilerParams(vmem_limit_bytes=60 * 1024 * 1024),
        cost_estimate=pl.CostEstimate(flops=1 << 20, bytes_accessed=1 << 20, transcendentals=0),
        name=name,
    )(*args)


def sds(shape, dtype):
    return jax.ShapeDtypeStruct(shape, dtype)


def rope_tables(length):
    half = HEAD // 2
    frequency = ROPE_BASE ** (-(np.arange(half, dtype=np.float64) * 2.0 / HEAD))
    angles = np.arange(length, dtype=np.float64)[:, None] * frequency[None, :]
    cos, sin = np.cos(angles), np.sin(angles)
    cosine = np.concatenate([cos, cos], axis=1).astype(np.float32)
    signed = np.concatenate([-sin, sin], axis=1).astype(np.float32)
    return cosine, signed


def place(where_ref, device, piece_refs, targets):
    at = 0
    for ref in piece_refs:
        blocks, rows, _ = ref.shape
        for j in range(blocks):
            start = pl.multiple_of(where_ref[device, at] * rows, 16 if rows % 16 == 0 else 8)
            for target, column in targets:
                target[pl.ds(start, rows), :] = ref[j, :, column : column + target.shape[1]]
            at += 1


def scale_of(z):
    return lax.rsqrt(jnp.mean(z * z, axis=-1, keepdims=True) + EPSILON)


def heads_of(ref, b, length, c):
    return jnp.concatenate(
        [ref[b * length : (b + 1) * length, h * HEAD : (h + 1) * HEAD] for h in range(c * GROUP, (c + 1) * GROUP)],
        axis=0,
    )


def causal_mask(length):
    row = lax.broadcasted_iota(jnp.int32, (length, length), 0)
    column = lax.broadcasted_iota(jnp.int32, (length, length), 1)
    return jnp.concatenate([row >= column] * GROUP, axis=0)


def softmax_of(q, k, keep):
    s = jnp.where(keep, dot(q, k, 1, 1) * SCALE, MASKED)
    e = jnp.exp(s - jnp.max(s, axis=-1, keepdims=True))
    return e / jnp.sum(e, axis=-1, keepdims=True)


def forward_body(seqs, experts, n_pieces, me_ref, where_ref, x_ref, cos_ref, sin_ref, routes_ref, *refs):
    pieces = refs[:n_pieces]
    w_ref, o_ref, misc_ref, gain_ref, n1_ref, q_ref, k_ref, v_ref, mixed_ref, hidden_ref, send_ref, gate_ref = refs[n_pieces:]
    length = x_ref.shape[0] // seqs
    place(where_ref, me_ref[0], pieces, ((w_ref, 0), (misc_ref, MISC), (o_ref, MISC + LANES)))
    gains = jnp.transpose(misc_ref[...].astype(f32))[experts : experts + 8]
    gain_ref[...] = gains
    x = x_ref[...].astype(f32)
    n1 = (x * scale_of(x) * gains[0:1]).astype(bf16)
    n1_ref[...] = n1
    cos = jnp.concatenate([cos_ref[...]] * seqs, axis=0)
    sin = jnp.concatenate([sin_ref[...]] * seqs, axis=0)

    def rotated(u):
        return (u * cos + pltpu.roll(u, HEAD // 2, 1) * sin).astype(bf16)

    kv = dot(n1, w_ref[:, Q_COLS:])
    v_ref[...] = kv[:, KV_COLS:].astype(bf16)
    for c in range(KEY_VALUE_HEADS):
        k_ref[:, c * HEAD : (c + 1) * HEAD] = rotated(kv[:, c * HEAD : (c + 1) * HEAD])
    keep = causal_mask(length)
    for c in range(KEY_VALUE_HEADS):
        cols = GROUP * HEAD
        q = dot(n1, w_ref[:, c * cols : (c + 1) * cols])
        for h in range(GROUP):
            at = c * cols + h * HEAD
            q_ref[:, at : at + HEAD] = rotated(q[:, h * HEAD : (h + 1) * HEAD])
        for b in range(seqs):
            rows = slice(b * length, (b + 1) * length)
            k = k_ref[rows, c * HEAD : (c + 1) * HEAD]
            v = v_ref[rows, c * HEAD : (c + 1) * HEAD]
            p = softmax_of(heads_of(q_ref, b, length, c), k, keep).astype(bf16)
            o = dot(p, v).astype(bf16)
            for h in range(GROUP):
                at = c * cols + h * HEAD
                mixed_ref[rows, at : at + HEAD] = o[h * length : (h + 1) * length]
    tokens = x_ref.shape[0]
    h = x + dot(mixed_ref[...], o_ref[...], 1, 1)
    hidden_ref[...] = h
    n2 = (h * scale_of(h) * gains[1:2]).astype(bf16)
    send_ref[0:tokens] = n2
    z = dot(n2, misc_ref[...])
    lane = lax.broadcasted_iota(jnp.int32, (tokens, LANES), 1)
    chosen = lane == routes_ref[:, 0:1]
    for j in range(1, routes_ref.shape[1]):
        chosen = chosen | (lane == routes_ref[:, j : j + 1])
    top = jnp.max(jnp.where(chosen, z, MASKED), axis=-1, keepdims=True)
    e = jnp.where(chosen, jnp.exp(jnp.where(chosen, z - top, 0.0)), 0.0)
    gate = e / jnp.sum(e, axis=-1, keepdims=True)
    gate_ref[...] = gate
    high = gate.astype(bf16).astype(f32)
    tables = [jnp.transpose(t) for t in (high, gate - high, chosen.astype(f32))]
    blank = jnp.zeros((EXTRA, tokens), f32)
    parts = []
    for first in range(0, experts, EXTRA):
        parts += [t[first : first + EXTRA] for t in tables]
    parts += [blank] * (WIDTH // tokens - len(parts))
    send_ref[tokens:] = jnp.concatenate(parts, axis=1).astype(bf16)


def expert_body(layout, capacity, slots, tokens, seqs, me_ref, *refs):
    arrays, n_in, parts_in = layout
    count = len(arrays)
    ins = refs[:n_in]
    if parts_in == 1:
        weights = [tuple(refs[n_in : n_in + 3])]
        outs = refs[n_in + 3 :]
    else:
        gate_ref, up_ref, down_ref, far_ref, far_down_ref = refs[n_in : n_in + 5]
        hidden = gate_ref.shape[1]
        weights = [
            (gate_ref, up_ref, down_ref),
            (far_ref.at[:, 0:hidden], far_ref.at[:, hidden : 2 * hidden], far_down_ref),
        ]
        outs = refs[n_in + 5 :]
    deep, narrow = weights[0][0].shape[0], weights[0][2].shape[0]
    if parts_in == 1:
        spans = [(slice(0, deep), slice(0, narrow))]
    else:
        spans = [
            (pl.ds(pl.multiple_of(p * deep, LANES), deep), pl.ds(pl.multiple_of(p * narrow, LANES), narrow))
            for p in (me_ref[1], 1 - me_ref[1])
        ]
    half = count // 2
    far_out, far_dx = outs[2 * half : 2 * half + 2]
    out_refs, dx_refs = [], []
    for j in range(half):
        out_refs += [outs[j], far_out.at[j]]
        dx_refs += [outs[half + j], far_dx.at[j]]
    xs_ref, dy_ref, act_ref, du_ref, dw_ref, gs_ref, gcol_ref, dact_ref, dx_ref = outs[2 * half + 2 :]
    length = tokens // seqs
    me = me_ref[2]
    row_in = lax.rem(me, EXTRA)
    row = lax.broadcasted_iota(jnp.int32, (EXTRA, tokens), 0)
    mine = row == row_in
    block = lax.div(me, EXTRA)

    def table(extra, k):
        t = jnp.zeros((EXTRA, tokens), f32)
        for b in range(WIDTH // (3 * tokens)):
            at = (3 * b + k) * tokens
            t = jnp.where(block == b, extra[:, at : at + tokens].astype(f32), t)
        return jnp.sum(jnp.where(mine, t, 0.0), axis=0, keepdims=True)

    def read(pieces, first, rows):
        got = []
        for index, start, size, offset in pieces:
            lo, hi = max(first, start), min(first + rows, start + size)
            if lo < hi:
                got.append(ins[index][offset + lo - start : offset + hi - start])
        return got[0] if len(got) == 1 else jnp.concatenate(got, axis=0)

    tri_a = lax.broadcasted_iota(jnp.int32, (length, length), 0)
    tri_b = lax.broadcasted_iota(jnp.int32, (length, length), 1)
    before = (tri_a < tri_b).astype(bf16)
    slot = lax.broadcasted_iota(jnp.int32, (slots, tokens), 0).astype(f32)
    gates, masks = [], []
    for n2_pieces, _ in arrays:
        extra = read(n2_pieces, tokens, EXTRA)
        gates.append(table(extra, 0) + table(extra, 1))
        masks.append(table(extra, 2))
    picks = []
    for i, (n2_pieces, g_pieces) in enumerate(arrays):
        at = []
        for b in range(seqs):
            m = masks[i][:, b * length : (b + 1) * length]
            earlier = dot(jnp.broadcast_to(m, (16, length)).astype(bf16), before)[0:1]
            keep = (m > 0.5) & (earlier < capacity)
            at.append(jnp.where(keep, earlier + b * (slots // seqs), -1.0))
        pick = (slot == jnp.concatenate(at, axis=1)).astype(f32)
        gcol_ref[i * slots : (i + 1) * slots, :] = jnp.broadcast_to(
            jnp.sum(pick * gates[i], axis=1, keepdims=True), (slots, LANES)
        )
        pick = pick.astype(bf16)
        picks.append(pick)
        rows = slice(i * slots, (i + 1) * slots)
        xs_ref[rows, :] = dot(pick, read(n2_pieces, 0, tokens)).astype(bf16)
        gs_ref[rows, :] = dot(pick, read(g_pieces, 0, tokens)).astype(bf16)
    u = w = y = None
    for (gate_part, up_part, _), (rows, _) in zip(weights, spans, strict=True):
        xs = xs_ref[:, rows]
        more_u, more_w = dot(xs, gate_part[...]), dot(xs, up_part[...])
        u, w = (more_u, more_w) if u is None else (u + more_u, w + more_w)
    s = 1.0 / (1.0 + jnp.exp(-u))
    act_ref[...] = (u * s * w).astype(bf16)
    for (_, _, down_part), (_, rows) in zip(weights, spans, strict=True):
        more = dot(act_ref[:, rows], down_part[...])
        y = more if y is None else y + more
    y = y.astype(bf16).astype(f32)
    gcol = gcol_ref[:, 0:1]
    gs = gs_ref[...].astype(f32)
    dy = (gcol * gs).astype(bf16)
    dy_ref[...] = dy
    dg = jnp.sum(gs * y, axis=1, keepdims=True)
    weighted = (gcol * y).astype(bf16)
    for (_, _, down_part), (_, rows) in zip(weights, spans, strict=True):
        dact_ref[:, rows] = dot(dy, down_part[...], 1, 1)
    dact = dact_ref[...]
    du = (dact * w * s * (1.0 + u * (1.0 - s))).astype(bf16)
    dw = (dact * (u * s)).astype(bf16)
    du_ref[...] = du
    dw_ref[...] = dw
    for (gate_part, up_part, _), (rows, _) in zip(weights, spans, strict=True):
        dx_ref[:, rows] = (dot(du, gate_part[...], 1, 1) + dot(dw, up_part[...], 1, 1)).astype(bf16)
    dx = dx_ref[...]
    for i in range(count):
        rows = slice(i * slots, (i + 1) * slots)
        out_refs[i][...] = dot(picks[i], weighted[rows], 0, 0).astype(bf16)
        dx_refs[i][0:tokens] = dot(picks[i], dx[rows], 0, 0).astype(bf16)
        back = jnp.sum(picks[i].astype(f32) * dg[rows], axis=0, keepdims=True)
        high = back.astype(bf16).astype(f32)
        blank = jnp.zeros((EXTRA, tokens), f32)
        parts = []
        for b in range(WIDTH // (3 * tokens)):
            here = mine & (block == b)
            parts += [jnp.where(here, high, 0.0), jnp.where(here, back - high, 0.0), blank]
        dx_refs[i][tokens:] = jnp.concatenate(parts, axis=1).astype(bf16)


def weights_body(n, half, shift, adds, me_ref, *refs):
    lists = [refs[k * n : (k + 1) * n] for k in range(5)]
    xs, dys, acts, dus, dws = lists
    more = refs[5 * n : 5 * n + adds]
    outs = refs[5 * n + adds :]
    wide, narrow = half
    index = lax.rem(me_ref[1] + shift, me_ref[3])
    x_at = pl.multiple_of(index * wide, LANES)
    a_at = pl.multiple_of(index * narrow, LANES)
    totals = [None, None, None]
    for i in range(n):
        x = xs[i][:, pl.ds(x_at, wide)]
        a = acts[i][:, pl.ds(a_at, narrow)]
        for k, (left, right) in enumerate(((x, dus[i]), (x, dws[i]), (a, dys[i]))):
            now = dot(left, right[...], 0, 0)
            totals[k] = now if totals[k] is None else totals[k] + now
    hidden = totals[0].shape[1]
    columns = (slice(0, hidden), slice(hidden, 2 * hidden), slice(None))
    chunks = outs if shift else more
    rows = (wide + narrow) // CHUNKS
    for k, c in enumerate(columns):
        base, size = (wide, narrow) if k == 2 else (0, wide)
        for j, ref in enumerate(chunks):
            first = (j % CHUNKS) * rows
            lo, hi = max(first, base), min(first + rows, base + size)
            if lo < hi and shift:
                ref[lo - first : hi - first, c] = totals[k][lo - base : hi - base].astype(bf16)
            elif lo < hi and j < CHUNKS:
                value = totals[k][lo - base : hi - base]
                for other in chunks[j::CHUNKS]:
                    value = value + other[lo - first : hi - first, c].astype(f32)
                outs[k][lo - base : hi - base] = value


def blocks_out(where_ref, device, whole_ref, outs):
    keep_ref, send_ref = outs
    sides, count, rows, _ = keep_ref.shape
    for lane, out in enumerate((keep_ref, send_ref)):
        for side in range(sides):
            for k in range(count):
                at = where_ref[device, (2 * k + lane) * sides + side]
                out[side, k] = whole_ref[pl.ds(pl.multiple_of(at * rows, 16), rows), :]


def norm_back(up, hat, scale, gain):
    w = up * gain
    return scale * (w - hat * jnp.mean(w * hat, axis=-1, keepdims=True)), jnp.sum(up * hat, axis=0, keepdims=True)


def hidden_back_body(experts, apart, me_ref, where_ref, a_ref, b_ref, c_ref, d_ref, g_ref, hidden_ref, gain_ref, gate_ref, misc_ref, o_ref, mixed_ref, *outs):
    dh_ref, dmixed_ref, rg_ref, gg_ref, og_ref = outs[:4] + outs[-1:]
    tokens = g_ref.shape[0]
    got = a_ref[...].astype(f32) + b_ref[...].astype(f32) + c_ref[...].astype(f32) + d_ref[...].astype(f32)
    extra = got[tokens:]
    rows = []
    for first in range(experts // EXTRA):
        at = 3 * first * tokens
        rows.append(extra[:, at : at + tokens] + extra[:, at + tokens : at + 2 * tokens])
    rows.append(jnp.zeros((LANES - experts, tokens), f32))
    dg = jnp.transpose(jnp.concatenate(rows, axis=0))
    gate = gate_ref[...]
    dl = gate * (dg - jnp.sum(gate * dg, axis=-1, keepdims=True))
    dz = dl.astype(bf16)
    dn = got[0:tokens] + dot(dz, misc_ref[...], 1, 1)
    h = hidden_ref[...]
    scale = scale_of(h)
    hat = h * scale
    gain = gain_ref[1:2]
    n2 = (hat * gain).astype(bf16)
    rg_ref[...] = dot(n2, dz, 0, 0)
    back, grad = norm_back(dn, hat, scale, gain)
    gg_ref[...] = jnp.broadcast_to(grad, gg_ref.shape)
    dh = g_ref[...].astype(f32) + back
    dh_ref[...] = dh
    da = dh.astype(bf16)
    dmixed_ref[...] = dot(da, o_ref[...]).astype(bf16)
    og_ref[...] = dot(da, mixed_ref[...], 0, 0).astype(bf16)
    if apart:
        blocks_out(where_ref, me_ref[0], og_ref, outs[4:6])


def attend_back_body(seqs, experts, apart, me_ref, where_ref, x_ref, cos_ref, sin_ref, w_ref, gain_ref, n1_ref, q_ref, k_ref, v_ref, do_ref, dh_ref, rg_ref, gg_ref, dx_ref, *outs):
    wg_ref, dqkv_ref = outs[-2:]
    length = x_ref.shape[0] // seqs
    cos = cos_ref[...]
    sin = sin_ref[...]
    keep = causal_mask(length)

    def back(u):
        return (u * cos - pltpu.roll(u, HEAD // 2, 1) * sin).astype(bf16)

    for b in range(seqs):
        rows = slice(b * length, (b + 1) * length)
        for c in range(KEY_VALUE_HEADS):
            cols = slice(c * HEAD, (c + 1) * HEAD)
            k = k_ref[rows, cols]
            v = v_ref[rows, cols]
            q = heads_of(q_ref, b, length, c)
            do = heads_of(do_ref, b, length, c)
            p = softmax_of(q, k, keep)
            dqkv_ref[rows, Q_COLS + KV_COLS + c * HEAD : Q_COLS + KV_COLS + (c + 1) * HEAD] = dot(
                p.astype(bf16), do, 0, 0
            ).astype(bf16)
            dp = dot(do, v, 1, 1)
            ds = (p * (dp - jnp.sum(p * dp, axis=-1, keepdims=True))).astype(bf16)
            dq = dot(ds, k) * SCALE
            for h in range(GROUP):
                at = (c * GROUP + h) * HEAD
                dqkv_ref[rows, at : at + HEAD] = back(dq[h * length : (h + 1) * length])
            dqkv_ref[rows, Q_COLS + c * HEAD : Q_COLS + (c + 1) * HEAD] = back(dot(ds, q, 0, 0) * SCALE)
    dqkv = dqkv_ref[...]
    wg_ref[:, 0:MISC] = dot(n1_ref[...], dqkv, 0, 0).astype(bf16)
    dn = dot(dqkv, w_ref[...], 1, 1)
    x = x_ref[...].astype(f32)
    scale = scale_of(x)
    back_x, grad = norm_back(dn, x * scale, scale, gain_ref[0:1])
    dx_ref[...] = dh_ref[...] + back_x
    row = lax.broadcasted_iota(jnp.int32, (LANES, x.shape[1]), 0)
    gains = jnp.where(row == experts, grad, jnp.where(row == experts + 1, gg_ref[0:1], 0.0))
    wg_ref[:, MISC:] = (rg_ref[...] + jnp.transpose(gains)).astype(bf16)
    if apart:
        blocks_out(where_ref, me_ref[0], wg_ref, outs[:2])


def chip_ring(chips):
    if chips % 4 or chips < 8:
        return list(range(chips))
    high, low = 4, chips // 4
    order = [a * low for a in range(high)]
    for step, a in enumerate(reversed(range(high))):
        rest = list(range(1, low))
        order += [a * low + b for b in (rest if step % 2 == 0 else reversed(rest))]
    return order


class Ring:
    def __init__(self, devices):
        self.devices = devices
        self.chips = devices // 2
        self.half = self.chips // 2
        self.order = chip_ring(self.chips)
        n = self.chips
        self.up = [
            (2 * self.order[p] + lane, 2 * self.order[(p + 1) % n] + lane) for p in range(n) for lane in (0, 1)
        ]
        self.down = [(b, a) for a, b in self.up]
        self.swap = [(d, d ^ 1) for d in range(devices)]
        self.place = np.argsort(np.array(self.order)).astype(np.int32)
        self.offsets = [0] + [s * o for o in range(1, self.half) for s in (-1, 1)] + [self.half]

    def send_up(self, x):
        return lax.ppermute(x, "expert", self.up)

    def send_down(self, x):
        return lax.ppermute(x, "expert", self.down)

    def send_core(self, x):
        return lax.ppermute(x, "expert", self.swap)

    def table(self, dp):
        rows = []
        for y in range(dp):
            for e in range(self.devices):
                row = []
                for o in self.offsets:
                    chip = self.order[(int(self.place[e // 2]) + o) % self.chips]
                    for lane in (e % 2, 1 - e % 2):
                        row += [y * self.devices + 2 * chip + lane, (1 - y) * self.devices + 2 * chip + lane]
                rows.append(row)
        return np.array(rows, np.int32)

    def gather(self, x, split=None):
        return Gather(self, x, split)

    def scatter(self, own, far, split):
        return Scatter(self, own, far, split)


def after(x, *events):
    return lax.optimization_barrier((x, events))[0] if events else x


def total(*terms):
    out = terms[0].astype(f32)
    for t in terms[1:]:
        out = out + t.astype(f32)
    return out.astype(bf16)


class Gather:
    def __init__(self, ring, x, split):
        self.ring, self.split = ring, split
        self.got, self.far = {0: [x]}, {}
        self.hops = 0

    def hop(self, *events):
        ring, s = self.ring, self.hops
        self.hops += 1
        up, down = after((self.got[-s][0], self.got[s][0]), *events)
        if self.hops < ring.half:
            self.got[-self.hops], self.got[self.hops] = [ring.send_up(up)], [ring.send_down(down)]
        elif self.split is None:
            self.got[ring.half] = [ring.send_up(up)]
        else:
            self.got[ring.half] = [ring.send_up(up[: self.split]), ring.send_down(down[self.split :])]

    def swap(self, *offsets):
        for o in offsets:
            if o not in self.far:
                self.far[o] = [self.ring.send_core(p) for p in self.got[o]]


def fence(*things):
    rings = [t for t in things if isinstance(t, Gather)]
    arrays = [t for t in things if not isinstance(t, Gather)]
    held, arrays = lax.optimization_barrier(([(r.got, r.far) for r in rings], arrays))
    for r, (got, far) in zip(rings, held, strict=True):
        r.got, r.far = got, far
    return arrays


class Scatter:
    def __init__(self, ring, own, far, split):
        self.ring, self.own, self.far, self.split = ring, own, far, split
        self.partner, self.left = {}, ring.half

    def swap(self, offsets, *events):
        got = self.ring.send_core(after(self.far[offsets[0]], *events))
        for i, o in enumerate(offsets):
            self.partner[o] = got[i]

    def hop(self, *events):
        ring, own, partner, split, s = self.ring, self.own, self.partner, self.split, self.left
        self.left -= 1
        if s == ring.half:
            first = total(own[s], partner[s])
            up, down = first[:split], first[split:]
        elif s == ring.half - 1:
            more = own[s].shape[0] - split
            up = total(own[s], partner[s], jnp.pad(self.up, ((0, more), (0, 0))))
            down = total(own[-s], partner[-s], jnp.pad(self.down, ((split, 0), (0, 0))))
        else:
            up, down = total(own[s], partner[s], self.up), total(own[-s], partner[-s], self.down)
        self.sent = up, down = after((up, down), *events)
        self.up, self.down = ring.send_up(up), ring.send_down(down)
        return self.up, self.down

    def step(self, *events):
        there = self.hop(*events)
        self.swap([-self.left, self.left] if self.left else [0], *self.sent)
        return there

    def terms(self):
        return self.own[0], self.partner[0], self.up, self.down


def dp_pairs(shift):
    n = lax.axis_size("dp")
    return [(i, (i + shift) % n) for i in range(n)]


def from_dp(x, shift):
    return lax.ppermute(x, "dp", dp_pairs(shift))


def on_device(
    inputs,
    cotangent,
    routes,
    attention_gain,
    query_weight,
    key_matrix,
    value_matrix,
    output_weight,
    mixture_gain,
    router_weight,
    gate_weight,
    up_weight,
    down_weight,
):
    seqs, _, length, _ = inputs.shape
    tokens = seqs * length
    topk = routes.shape[3]
    dp, experts = lax.axis_size("dp"), lax.axis_size("expert")
    assert gate_weight.shape[0] == 1 and experts % EXTRA == 0 and experts * 3 * tokens <= EXTRA * WIDTH * 2
    ring = Ring(experts)
    my_dp, me = lax.axis_index("dp"), lax.axis_index("expert")
    capacity = (5 * length * topk + 4 * experts - 1) // (4 * experts)
    slots = seqs * ((capacity + 7) // 8 * 8)
    x = inputs.reshape(tokens, WIDTH)
    g = cotangent.reshape(tokens, WIDTH)
    cos, sin = (jnp.asarray(t) for t in rope_tables(length))
    split = length
    where_i = jnp.stack([my_dp * experts + me, my_dp, me, jnp.full_like(me, dp)]).astype(jnp.int32)

    rows = query_weight.shape[0]
    misc = jnp.concatenate(
        [
            router_weight,
            attention_gain[:, None],
            mixture_gain[:, None],
            jnp.zeros((rows, LANES - experts - 2), bf16),
        ],
        axis=1,
    )
    dense_own = jnp.concatenate([query_weight, key_matrix, value_matrix, misc, output_weight.T], axis=1)
    g_ring = ring.gather(g, split)
    g_ring.hop()
    apart = dp == 2 and rows % 16 == 0
    if apart:
        table = jnp.asarray(ring.table(dp))
        far = from_dp(dense_own, 1)
        d_ring = ring.gather(jnp.stack([dense_own, far]), 1)
        d_ring.hop()
        expert_start = (far,)
    else:
        table = jnp.zeros((dp * experts, 1), jnp.int32)
        both = lax.all_gather(dense_own, ("dp", "expert"), axis=0, tiled=True)
        dense = [both[None]]
        expert_start = (both,)

    hidden_size = gate_weight.shape[2]
    wide, narrow = WIDTH // dp, hidden_size // dp
    in_parts = dp == 2 and wide % LANES == 0 and narrow % LANES == 0
    if in_parts:
        flat = [jnp.concatenate([gate_weight[0], up_weight[0]], axis=1)]
        halves = [from_dp(after(flat[0], *expert_start), 1)]
        halves.append(from_dp(after(down_weight[0], *halves), 1))
        expert_weights = [gate_weight[0], up_weight[0], down_weight[0], *halves]
    else:
        expert_weights = [
            lax.all_gather(after(w[0], *expert_start), "dp", axis=0, tiled=True)
            for w in (gate_weight, up_weight, down_weight)
        ]
        flat, halves = [], []

    if apart:
        d_ring.hop(g_ring.got[-1], g_ring.got[1], *flat)
        while d_ring.hops < ring.half:
            d_ring.hop(*(halves[:1] if d_ring.hops == ring.half - 1 else ()))
        d_ring.swap(*ring.offsets)
        fence(d_ring, g_ring)
        dense = []
        for o in ring.offsets:
            dense += d_ring.got[o] + d_ring.far[o]
    g_ring.hop()

    w_full, o_t, misc_full, gains, n1, q, k, v, mixed, hidden, send, gate_values = call(
        functools.partial(forward_body, seqs, experts, len(dense)),
        [
            sds((WIDTH, MISC), bf16),
            sds((WIDTH, Q_COLS), bf16),
            sds((WIDTH, LANES), bf16),
            sds((8, WIDTH), f32),
            sds((tokens, WIDTH), bf16),
            sds((tokens, Q_COLS), bf16),
            sds((tokens, KV_COLS), bf16),
            sds((tokens, KV_COLS), bf16),
            sds((tokens, Q_COLS), bf16),
            sds((tokens, WIDTH), f32),
            sds((tokens + EXTRA, WIDTH), bf16),
            sds((tokens, LANES), f32),
        ],
        [smem(), smem()] + vmem(4 + len(dense)),
        [where_i, table, x, cos, sin, routes.reshape(tokens, topk), *dense],
        "forward",
        2 * tokens * WIDTH * (MISC + Q_COLS),
    )

    n_ring = ring.gather(send, split)
    out_own, out_far, dx_own, dx_far = {}, {}, {}, {}
    kept = {}
    groups = [[0]] + [[-s, s] for s in range(1, ring.half)] + [[ring.half]]

    def far_of(group):
        return ring.send_core(jnp.concatenate([p for o in group for r in (n_ring, g_ring) for p in r.got[o]]))

    def experts_on(group, far, *events):
        args, arrays, offset = [far], [], 0
        for o in group:
            own, other = [], []
            for pieces in (n_ring.got[o], g_ring.got[o]):
                start, first = 0, len(args)
                own.append([])
                other.append([])
                for j, p in enumerate(pieces):
                    args.append(p)
                    own[-1].append((first + j, start, p.shape[0], 0))
                    other[-1].append((0, start, p.shape[0], offset))
                    start += p.shape[0]
                    offset += p.shape[0]
            arrays += [tuple(own), tuple(other)]
        count = len(arrays)
        rows_ = count * slots
        outs = call(
            functools.partial(expert_body, (arrays, len(args), 2 if in_parts else 1), capacity, slots, tokens, seqs),
            [sds((tokens, WIDTH), bf16)] * len(group)
            + [sds((tokens + EXTRA, WIDTH), bf16)] * len(group)
            + [sds((len(group), tokens, WIDTH), bf16), sds((len(group), tokens + EXTRA, WIDTH), bf16)]
            + [sds((rows_, WIDTH), bf16)] * 2
            + [sds((rows_, hidden_size), bf16)] * 3,
            [smem()] + vmem(len(args) + len(expert_weights)),
            [after(where_i, *events), *args, *expert_weights],
            "experts",
            2 * rows_ * WIDTH * hidden_size * 6,
            [
                pltpu.VMEM((rows_, WIDTH), bf16),
                pltpu.VMEM((rows_, LANES), f32),
                pltpu.VMEM((rows_, hidden_size), f32),
                pltpu.VMEM((rows_, WIDTH), bf16),
            ],
        )
        n = len(group)
        for i, o in enumerate(group):
            out_own[o], dx_own[o] = outs[i], outs[n + i]
        out_far[group[0]], dx_far[group[0]] = outs[2 * n : 2 * n + 2]
        kept[group[0]] = outs[2 * n + 2 :]
        return kept[group[0]]

    fence(g_ring, n_ring, expert_weights[-1])
    far = []
    for hop in range(1, ring.half + 1):
        n_ring.hop()
        if g_ring.hops < ring.half:
            g_ring.hop()
        near, far = far, far_of(groups[hop - 1])
        if hop > 1:
            group = groups[hop - 2]
            far, kept[group[0]] = fence(n_ring, g_ring, far, experts_on(group, near))
        else:
            (far,) = fence(n_ring, g_ring, far)
    (last,) = fence(n_ring, g_ring, far_of(groups[-1]))
    experts_on(groups[-1], last)
    dx_ring = ring.scatter(dx_own, dx_far, split)
    dx_ring.swap(groups[-1])
    there = dx_ring.hop()
    experts_on(groups[-2], far, *dx_ring.sent)
    dx_ring.swap(groups[-2], *there)
    dx_ring.hop()
    dx_ring.swap(groups[-3], *dx_ring.sent)
    kept = [[kept[group[0]][i] for group in groups] for i in range(5)]

    saved = [a for k_ in kept for a in k_]
    if wide % LANES == 0 and narrow % LANES == 0:

        def part(shift, outs, more, *events):
            return call(
                functools.partial(weights_body, len(groups), (wide, narrow), shift, len(more)),
                outs,
                [smem()] + vmem(len(saved) + len(more)),
                [after(where_i, *events), *saved, *more],
                "expert_weights",
                2 * experts * slots * wide * hidden_size * 3,
            )

        more = []
        for shift in range(1, dp):
            parts = part(shift, [sds(((wide + narrow) // CHUNKS, WIDTH), bf16)] * CHUNKS, [], *dx_ring.sent, *more)
            for p in parts:
                more.append(from_dp(after(p, *more[-1:]), shift))
        weights_sent = (parts[0],)
    else:
        xs, dys, acts, dus, dws = (jnp.concatenate(k_) for k_ in kept)
        expert_grads = tuple(
            lax.psum_scatter(dot(a, b, 0, 0).astype(bf16), "dp", scatter_dimension=0, tiled=True).astype(f32)
            for a, b in ((xs, dus), (xs, dws), (acts, dys))
        )
        weights_sent, more = (), []
    dx_ring.step(*weights_sent)
    while dx_ring.left:
        dx_ring.step(*more[:1])
    dx_terms = dx_ring.terms()
    out_ring = ring.scatter(out_own, out_far, split)
    out_ring.swap(groups[-1], *dx_ring.sent)
    out_ring.step(*dx_terms[2:], *more[1:2])

    def block_outs(columns):
        return [sds((dp, ring.chips, rows, columns), bf16)] * 2

    dh, dmixed, router_part, gain_part, *o_part = call(
        functools.partial(hidden_back_body, experts, apart),
        [sds((tokens, WIDTH), f32), sds((tokens, Q_COLS), bf16), sds((WIDTH, LANES), f32), sds((8, WIDTH), f32)]
        + (block_outs(Q_COLS) if apart else [sds((WIDTH, Q_COLS), bf16)]),
        [smem(), smem()] + vmem(11),
        [after(where_i, *out_ring.sent), table, *dx_terms, g, hidden, gains, gate_values, misc_full, o_t, mixed],
        "hidden_back",
        4 * tokens * WIDTH * Q_COLS,
        [pltpu.VMEM((WIDTH, Q_COLS), bf16)] if apart else [],
    )
    out_ring.step(dh, *more[2:3])
    o_got = [ring.send_core(after(o_part[1], *out_ring.sent))] if apart else []
    input_grad, *qkv_part = call(
        functools.partial(attend_back_body, seqs, experts, apart),
        [sds((tokens, WIDTH), f32)]
        + (block_outs(MISC + LANES) if apart else [sds((WIDTH, MISC + LANES), bf16)]),
        [smem(), smem()] + vmem(13),
        [after(where_i, *out_ring.sent), table, x, cos, sin, w_full, gains, n1, q, k, v, dmixed, dh, router_part, gain_part],
        "attend_back",
        4 * tokens * WIDTH * MISC,
        ([pltpu.VMEM((WIDTH, MISC + LANES), bf16)] if apart else []) + [pltpu.VMEM((tokens, MISC), bf16)],
    )

    out_ring.step(input_grad, *more, *o_got)
    if wide % LANES == 0 and narrow % LANES == 0:
        expert_grads = part(
            0, [sds((wide, hidden_size), f32)] * 2 + [sds((narrow, WIDTH), f32)], more, *out_ring.sent
        )
    gate_grad, up_grad, down_grad = expert_grads

    def over_y(keep, got, *events):
        far = from_dp(after(total(keep[1], got[1]), *events), 1)
        return total(keep[0], got[0], far)

    class Blocks:
        def __init__(self, both):
            self.term = {o: both[k_] for k_, o in enumerate(ring.offsets)}
            self.up, self.down, self.left = None, None, ring.half

        def hop(self, *events):
            s = self.left
            self.left -= 1
            up = self.term[s] if self.up is None else total(self.up, self.term[s])
            if s == ring.half:
                self.up = ring.send_up(after(up, *events))
                return (self.up,)
            down = self.term[-s] if self.down is None else total(self.down, self.term[-s])
            up, down = after((up, down), *events)
            self.up, self.down = ring.send_up(up), ring.send_down(down)
            return self.up, self.down

        def result(self):
            while self.left:
                self.hop()
            return self.up.astype(f32) + self.down.astype(f32) + self.term[0].astype(f32)

    if apart:
        qkv_got = ring.send_core(after(qkv_part[1], *out_ring.sent))
        o_sum = over_y(o_part[0], *o_got, *out_ring.sent)
        while out_ring.left:
            there = out_ring.step(gate_grad, o_sum, qkv_got)
        qkv_sum = over_y(qkv_part[0], qkv_got, *out_ring.sent)
        o_blocks, qkv_blocks = Blocks(o_sum), Blocks(qkv_sum)
        there += o_blocks.hop(*out_ring.sent)
        qkv_blocks.hop(*there)
        o_grad, qkv_grad = o_blocks.result(), qkv_blocks.result()
    else:
        while out_ring.left:
            out_ring.step()
        o_grad, qkv_grad = (
            lax.psum_scatter(p[0], ("dp", "expert"), scatter_dimension=0, tiled=True).astype(f32)
            for p in (o_part, qkv_part)
        )

    outputs = total(hidden, *out_ring.terms()).reshape(inputs.shape)
    return (
        outputs,
        input_grad.reshape(inputs.shape),
        qkv_grad[:, MISC + experts],
        qkv_grad[:, :Q_COLS],
        qkv_grad[:, Q_COLS : Q_COLS + KV_COLS],
        qkv_grad[:, Q_COLS + KV_COLS : MISC],
        o_grad.T,
        qkv_grad[:, MISC + experts + 1],
        qkv_grad[:, MISC : MISC + experts],
        gate_grad[None],
        up_grad[None],
        down_grad[None],
    )


def solution(mesh):
    both = ("dp", "expert")
    tokens = P(None, both, None, None)
    expert = P("expert", "dp", None)
    in_specs = (
        tokens,
        tokens,
        tokens,
        P(both),
        P(both, None),
        P(both, None),
        P(both, None),
        P(None, both),
        P(both),
        P(both, None),
        expert,
        expert,
        expert,
    )
    out_specs = (
        tokens,
        tokens,
        P(both),
        P(both, None),
        P(both, None),
        P(both, None),
        P(None, both),
        P(both),
        P(both, None),
        expert,
        expert,
        expert,
    )
    return jax.shard_map(on_device, mesh=mesh, in_specs=in_specs, out_specs=out_specs, check_vma=False)
```

time: 683 us -> 522 us (0.76)
  waiting for transfers between devices: 356 us -> 246 us
  starting transfers between devices: 96.9 us -> 71.7 us
  local copies, waits for them, and re-layouts: 27.3 us -> 12.9 us
  between operations: 14 us -> 1.98 us
    ppermute x10 -> x9, waiting for transfers between devices: 130 us -> 70 us  [from_dp(): return lax.ppermute(x, 'dp', dp_pairs(shift))]
    ppermute x32 -> x28, waiting for transfers between devices: 167 us -> 108 us  [send_up(): return lax.ppermute(x, 'expert', self.up)]
    ppermute x32 -> x28, starting transfers between devices: 52.4 us -> 34.3 us  [send_up(): return lax.ppermute(x, 'expert', self.up)]
    convert_element_type x11 -> x0, other arithmetic: 14.1 us -> none  [the longest x2 5.99 us: reduced(): far = from_dp(of_y(1 - my_dp).astype(bf16), 1)]
    convert_element_type x16 -> x19, other arithmetic: 11.9 us -> 24.8 us  [total(): return out.astype(bf16)]
    ppermute x46 -> x26, waiting for transfers between devices: 3.62 us -> 12.2 us  [send_core(): return lax.ppermute(x, 'expert', self.swap)]
    squeeze x4 -> x2, local copies, waits for them, and re-layouts: 7.4 us -> 0.05 us  [__init__(): self.term = {o: both[k_] for k_, o in enumerate(ring.offsets)}]
    ppermute x10 -> x9, starting transfers between devices: 13.8 us -> 10.7 us  [from_dp(): return lax.ppermute(x, 'dp', dp_pairs(shift))]
  transfers between devices with their start and end apart: 116 -> 89, of which waited for: 47 -> 47; matrix products, arithmetic and copies ran while one was open for 8% -> 4% of each run, Pallas kernels for 21% -> 26%
where the time goes in v2:
time: 522 us; the launch traced here: 514 us
  waiting for transfers between devices  246 us (47%)
  Pallas kernels  143 us (27%)
  starting transfers between devices  71.7 us (14%)
  other arithmetic  38.6 us (7%)
  local copies, waits for them, and re-layouts  12.9 us (2%)
    pallas_call x10, Pallas kernels, call(): pl.pallas_call(body, out_shape=outs, in_specs=ins, out_specs=vmem(len(out...  143 us
    ppermute x28, waiting for transfers between devices, send_up(): return lax.ppermute(x, 'expert', self.up)  108 us
    ppermute x9, waiting for transfers between devices, from_dp(): return lax.ppermute(x, 'dp', dp_pairs(shift))  70 us
    ppermute x26, waiting for transfers between devices, send_down(): return lax.ppermute(x, 'expert', self.down)  55.5 us
    ppermute x28, starting transfers between devices, send_up(): return lax.ppermute(x, 'expert', self.up)  34.3 us
    convert_element_type x19, other arithmetic, total(): return out.astype(bf16)  24.8 us
    ppermute x26, starting transfers between devices, send_down(): return lax.ppermute(x, 'expert', self.down)  23.2 us
    ppermute x26, waiting for transfers between devices, send_core(): return lax.ppermute(x, 'expert', self.swap)  12.2 us
  transfers between devices with their start and end apart: 89, of which 47 were waited for; matrix products, arithmetic and copies ran while one was open for 4% of the time, Pallas kernels for 26%

profile of v2, /device:TPU:0, one launch (start us, length us, event | category | flops | bytes accessed | tf_op | source)
XLA Modules:
  0.0 513.9 jit_solution(2556706891273059804)
XLA Ops:
  4.2 3.0 collective-permute-start
  9.2 6.3 %collective-permute-done = bf16[48,3712]{1,0:T(8,128)(2,1)S(1)} collective-permute-done((bf16[48,3712]{1,0:T(8,128)(2,1)S(1)}, bf16[48,3712]{1,0:T(8,128)(2,1)S(1)}, u32[]{:S(2)}, u32[]{:S(2)}) %collective-permute-start) | collective-permute-done | bytes 356384 | tf_op jit(solution)/shard_map/ppermute | solution.py:546
  15.6 1.8 collective-permute-start.2
  19.1 1.8 collective-permute-start.9
  20.9 7.0 %collective-permute-done.4.refs_4_ = bf16[256,1536]{1,0:T(8,128)(2,1)} collective-permute-done((bf16[256,1536]{1,0:T(8,128)(2,1)}, bf16[256,1536]{1,0:T(8,128)(2,1)}, u32[]{:S(2)}, u32[]{:S(2)}) %collective-permute-start.4) | collective-permute-done | bytes 786464 | tf_op jit(solution)/shard_map/ppermute | solution.py:438
  29.5 12.2 %collective-permute-done.2.refs_4_ = bf16[2,48,3712]{2,1,0:T(8,128)(2,1)S(1)} collective-permute-done((bf16[2,48,3712]{2,1,0:T(8,128)(2,1)S(1)}, bf16[2,48,3712]{2,1,0:T(8,128)(2,1)S(1)}, u32[]{:S(2)}, u32[]{:S(2)}) %collective-permute-start.2) | collective-permute-done | bytes 712736 | tf_op jit(solution)/shard_map/ppermute | solution.py:438
  44.9 14.2 %collective-permute-done.5.refs_6_ = bf16[2,48,3712]{2,1,0:T(8,128)(2,1)S(1)} collective-permute-done((bf16[2,48,3712]{2,1,0:T(8,128)(2,1)S(1)}, bf16[2,48,3712]{2,1,0:T(8,128)(2,1)S(1)}, u32[]{:S(2)}, u32[]{:S(2)}) %collective-permute-start.5) | collective-permute-done | bytes 712736 | tf_op jit(solution)/shard_map/ppermute | solution.py:435
  61.7 12.7 %collective-permute-done.6.refs_10_ = bf16[2,48,3712]{2,1,0:T(8,128)(2,1)S(1)} collective-permute-done((bf16[2,48,3712]{2,1,0:T(8,128)(2,1)S(1)}, bf16[2,48,3712]{2,1,0:T(8,128)(2,1)S(1)}, u32[]{:S(2)}, u32[]{:S(2)}) %collective-permute-start.6) | collective-permute-done | bytes 712736 | tf_op jit(solution)/shard_map/ppermute | solution.py:435
  79.4 7.6 %collective-permute-done.11.refs_15_ = bf16[1,48,3712]{2,1,0:T(8,128)(2,1)S(1)} collective-permute-done((bf16[1,48,3712]{2,1,0:T(8,128)(2,1)S(1)}, bf16[1,48,3712]{2,1,0:T(8,128)(2,1)S(1)}, u32[]{:S(2)}, u32[]{:S(2)}) %collective-permute-start.11) | collective-permute-done | bytes 356384 | tf_op jit(solution)/shard_map/ppermute | solution.py:438
  93.4 13.3 %forward.1 = (bf16[1536,2048]{1,0:T(8,128)(2,1)}, bf16[1536,1536]{1,0:T(8,128)(2,1)}, bf16[1536,128]{1,0:T(8,128)(2,1)}, f32[8,1536]{1,0:T(8,128)}, bf16[256,153...) custom-call(s32[4]{0:T(128)} %pad_add_fusion.me_ref, ...), custom_call_target="tpu_custom_call" | custom-call | flops 1048576 | bytes 1048576 | tf_op jit(solution)/shard_map/forward/pallas_call | solution.py:45
  106.8 3.0 collective-permute-done.21.refs_2_
  116.1 34.6 %collective-permute-done.26.refs_2_ = bf16[256,1536]{1,0:T(8,128)(2,1)S(1)} collective-permute-done((bf16[256,1536]{1,0:T(8,128)(2,1)}, bf16[256,1536]{1,0:T(8,128)(2,1)S(1)}, u32[]{:S(2)}, u32[]{:S(2)}) %collective-permute-start.26) | collective-permute-done | bytes 786464 | tf_op jit(solution)/shard_map/ppermute | solution.py:435
  150.8 3.8 pad_maximum_fusion
  159.0 11.2 %experts.5 = (bf16[256,1536]{1,0:T(8,128)(2,1)}, bf16[272,1536]{1,0:T(8,128)(2,1)}, bf16[1,256,1536]{2,1,0:T(8,128)(2,1)}, bf16[1,272,1536]{2,1,0:T(8,128)(2,1)}...) custom-call(s32[4]{0:T(128)} %pad_add_fusion.me_ref, ...), custom_call_target="tpu_custom_call" | custom-call | flops 1048576 | bytes 1048576 | tf_op jit(solution)/shard_map/experts/pallas_call | solution.py:45
  170.2 14.7 %collective-permute-done.32.refs_4_ = bf16[128,1536]{1,0:T(8,128)(2,1)S(1)} collective-permute-done((bf16[128,1536]{1,0:T(8,128)(2,1)S(1)}, bf16[128,1536]{1,0:T(8,128)(2,1)S(1)}, u32[]{:S(2)}, u32[]{:S(2)}) %collective-permute-start.32) | collective-permute-done | bytes 393248 | tf_op jit(solution)/shard_map/ppermute | solution.py:438
  184.9 3.6 pad_maximum_fusion.1
  190.6 16.9 %experts.6 = (bf16[256,1536]{1,0:T(8,128)(2,1)}, bf16[256,1536]{1,0:T(8,128)(2,1)}, bf16[272,1536]{1,0:T(8,128)(2,1)}, bf16[272,1536]{1,0:T(8,128)(2,1)}, bf16[2...) custom-call(s32[4]{0:T(128)} %pad_add_fusion.me_ref, ...), custom_call_target="tpu_custom_call" | custom-call | flops 1048576 | bytes 1048576 | tf_op jit(solution)/shard_map/experts/pallas_call | solution.py:45
  207.5 2.0 collective-permute-done.34.refs_1_
  211.1 2.0 pad_maximum_fusion.2
  215.5 16.9 %experts.7 = (bf16[256,1536]{1,0:T(8,128)(2,1)}, bf16[256,1536]{1,0:T(8,128)(2,1)}, bf16[272,1536]{1,0:T(8,128)(2,1)}, bf16[272,1536]{1,0:T(8,128)(2,1)}, bf16[2...) custom-call(s32[4]{0:T(128)} %pad_add_fusion.me_ref, ...), custom_call_target="tpu_custom_call" | custom-call | flops 1048576 | bytes 1048576 | tf_op jit(solution)/shard_map/experts/pallas_call | solution.py:45
  232.6 3.5 collective-permute-done.40.refs_0_
  237.2 11.2 %experts.8 = (bf16[256,1536]{1,0:T(8,128)(2,1)}, bf16[272,1536]{1,0:T(8,128)(2,1)}, bf16[1,256,1536]{2,1,0:T(8,128)(2,1)}, bf16[1,272,1536]{2,1,0:T(8,128)(2,1)}...) custom-call(s32[4]{0:T(128)} %pad_add_fusion.me_ref, ...), custom_call_target="tpu_custom_call" | custom-call | flops 1048576 | bytes 1048576 | tf_op jit(solution)/shard_map/experts/pallas_call | solution.py:45
  248.6 2.4 collective-permute-done.41
  255.0 16.9 %experts.9 = (bf16[256,1536]{1,0:T(8,128)(2,1)}, bf16[256,1536]{1,0:T(8,128)(2,1)}, bf16[272,1536]{1,0:T(8,128)(2,1)}, bf16[272,1536]{1,0:T(8,128)(2,1)}, bf16[2...) custom-call(s32[4]{0:T(128)} %pad_add_fusion.me_ref, ...), custom_call_target="tpu_custom_call" | custom-call | flops 1048576 | bytes 1048576 | tf_op jit(solution)/shard_map/experts/pallas_call | solution.py:45
  272.0 3.7 collective-permute-done.44
  275.7 3.1 fusion.12
  281.2 14.0 %expert_weights.2 = (bf16[288,1536]{1,0:T(8,128)(2,1)}, bf16[288,1536]{1,0:T(8,128)(2,1)}, bf16[288,1536]{1,0:T(8,128)(2,1)}, bf16[288,1536]{1,0:T(8,128)(2,1)}) custom-call(s32[4]{0:T(128)} %pad_add_fusion.me_ref, bf16[160,1536]{1,0:T(8,128)(2,1)} %get-tuple-element.354.refs_0_, bf16[320,1536]{1,0:T(8,128)(2,1)} %get-tuple-element.355.refs_1_, ...), custom_call_target="tpu_custom_call" | custom-call | flops 1048576 | bytes 1048576 | tf_op jit(solution)/shard_map/expert_weights/pallas_call | solution.py:45
  295.2 5.0 collective-permute-done.47
  300.5 2.2 fusion.8
  305.4 18.4 %collective-permute-done.49 = bf16[272,1536]{1,0:T(8,128)(2,1)S(1)} collective-permute-done((bf16[272,1536]{1,0:T(8,128)(2,1)S(1)}, bf16[272,1536]{1,0:T(8,128)(2,1)S(1)}, u32[]{:S(2)}, u32[]{:S(2)}) %collective-permute-start.49) | collective-permute-done | bytes 835616 | tf_op jit(solution)/shard_map/ppermute | solution.py:435
  330.3 18.1 %collective-permute-done.55.refs_26_ = bf16[288,1536]{1,0:T(8,128)(2,1)S(1)} collective-permute-done((bf16[288,1536]{1,0:T(8,128)(2,1)S(1)}, bf16[288,1536]{1,0:T(8,128)(2,1)S(1)}, u32[]{:S(2)}, u32[]{:S(2)}) %collective-permute-start.55) | collective-permute-done | bytes 884768 | tf_op jit(solution)/shard_map/ppermute | solution.py:546
  353.7 10.6 %hidden_back.1 = (f32[256,1536]{1,0:T(8,128)}, bf16[256,1536]{1,0:T(8,128)(2,1)}, f32[1536,128]{1,0:T(8,128)}, f32[8,1536]{1,0:T(8,128)}, bf16[2,8,48,1536]{3,2,...) custom-call(s32[4]{0:T(128)} %pad_add_fusion.me_ref, s32[32,32]{1,0:T(8,128)} %constant.25.clone.where_ref, ...), custom_call_target="tpu_custom_call" | custom-call | flops 1048576 | bytes 1048576 | tf_op jit(solution)/shard_map/hidden_back/pallas_call | solution.py:45
  364.4 3.2 fusion.28
  367.6 5.7 %collective-permute-done.60.refs_27_ = bf16[288,1536]{1,0:T(8,128)(2,1)S(1)} collective-permute-done((bf16[288,1536]{1,0:T(8,128)(2,1)}, bf16[288,1536]{1,0:T(8,128)(2,1)S(1)}, u32[]{:S(2)}, u32[]{:S(2)}) %collective-permute-start.60) | collective-permute-done | bytes 884768 | tf_op jit(solution)/shard_map/ppermute | solution.py:546
  377.9 15.5 %attend_back.1 = (f32[256,1536]{1,0:T(8,128)}, bf16[2,8,48,2176]{3,2,1,0:T(8,128)(2,1)}, bf16[2,8,48,2176]{3,2,1,0:T(8,128)(2,1)}) custom-call(s32[4]{0:T(128)} %pad_add_fusion.me_ref, s32[32,32]{1,0:T(8,128)} %constant.25.clone.where_ref, bf16[256,1536]{1,0:T(8,128)(2,1)} %bitcast.193, f32[128,128]{1,0:T(8,128)} %constant.23.clone.cos_ref, ...), custom_call_target="tpu_custom_call" | custom-call | flops 1048576 | bytes 1048576 | tf_op jit(solution)/shard_map/attend_back/pallas_call | solution.py:45
  395.8 3.7 fusion.24
  401.0 2.7 fusion.32
  407.2 16.1 %expert_weights.3 = (f32[768,768]{1,0:T(8,128)}, f32[768,768]{1,0:T(8,128)}, f32[384,1536]{1,0:T(8,128)}) custom-call(s32[4]{0:T(128)} %pad_add_fusion.me_ref, bf16[160,1536]{1,0:T(8,128)(2,1)} %get-tuple-element.354.refs_0_, bf16[320,1536]{1,0:T(8,128)(2,1)} %get-tuple-element.355.refs_1_, bf16[320,1536]{1,0:T(8,128)(2,1)} %get-tuple-element.356.refs_2_, ...), custom_call_target="tpu_custom_call" | custom-call | flops 1048576 | bytes 1048576 | tf_op jit(solution)/shard_map/expert_weights/pallas_call | solution.py:45
  423.3 9.1 %collective-permute-done.69 = bf16[8,48,1536]{2,1,0:T(8,128)(2,1)} collective-permute-done((bf16[8,48,1536]{2,1,0:T(8,128)(2,1)}, bf16[8,48,1536]{2,1,0:T(8,128)(2,1)}, u32[]{:S(2)}, u32[]{:S(2)}) %collective-permute-start.69) | collective-permute-done | bytes 1179680 | tf_op jit(solution)/shard_map/ppermute | solution.py:546
  432.4 2.4 fusion.1
  434.9 2.4 fusion.20
  443.1 2.7 collective-permute-done.75
  445.9 30.3 %collective-permute-done.74 = bf16[8,48,2176]{2,1,0:T(8,128)(2,1)S(1)} collective-permute-done((bf16[8,48,2176]{2,1,0:T(8,128)(2,1)S(1)}, bf16[8,48,2176]{2,1,0:T(8,128)(2,1)S(1)}, u32[]{:S(2)}, u32[]{:S(2)}) %collective-permute-start.74) | collective-permute-done | bytes 1671200 | tf_op jit(solution)/shard_map/ppermute | solution.py:546
  479.6 3.3 collective-permute-done.83
  485.4 1.9 collective-permute-done.76
  492.7 2.9 collective-permute-done.77
  499.3 2.3 collective-permute-done.78
  506.8 2.4 collective-permute-done.79
  (311 shorter events, 107.7 us)
Async XLA Ops:
  7.2 20.8 %collective-permute-start.4 = (bf16[256,1536]{1,0:T(8,128)(2,1)}, bf16[256,1536]{1,0:T(8,128)(2,1)}, u32[]{:S(2)}, u32[]{:S(2)}) collective-permute-start(bf16[256,1536]{1,0:T(8,128)(2,1)} %bitcast.187), channel_id=1, source_target_pairs={{4,0},{5,1},{8,4},{9,5},{12,8},{13,9},{14,12},{15,13},{10,14},{11,... | collective-permute-start | bytes 2359304 | tf_op jit(solution)/shard_map/ppermute | solution.py:438
  8.7 20.8 %collective-permute-start.3 = (bf16[256,1536]{1,0:T(8,128)(2,1)}, bf16[256,1536]{1,0:T(8,128)(2,1)}, u32[]{:S(2)}, u32[]{:S(2)}) collective-permute-start(bf16[256,1536]{1,0:T(8,128)(2,1)} %bitcast.188), channel_id=1, source_target_pairs={{0,4},{1,5},{4,8},{5,9},{8,12},{9,13},{12,14},{13,15},{14,10},{15,... | collective-permute-start | bytes 2359304 | tf_op jit(solution)/shard_map/ppermute | solution.py:435
  15.6 26.1 %collective-permute-start.2 = (bf16[2,48,3712]{2,1,0:T(8,128)(2,1)S(1)}, bf16[2,48,3712]{2,1,0:T(8,128)(2,1)S(1)}, u32[]{:S(2)}, u32[]{:S(2)}) collective-permute-start(bf16[2,48,3712]{2,1,0:T(8,128)(2,1)S(1)} %pad_maximum_fusion.6.refs_0_), channel_id=1, source_target_pairs={{4,0},{5,1},{8,4},{9,5},{12,8},{13,9},{14,12},{15,13},{10,14},{11,... | collective-permute-start | bytes 2138120 | tf_op jit(solution)/shard_map/ppermute | solution.py:438
  17.4 25.5 %collective-permute-start.1 = (bf16[2,48,3712]{2,1,0:T(8,128)(2,1)S(1)}, bf16[2,48,3712]{2,1,0:T(8,128)(2,1)S(1)}, u32[]{:S(2)}, u32[]{:S(2)}) collective-permute-start(bf16[2,48,3712]{2,1,0:T(8,128)(2,1)S(1)} %pad_maximum_fusion.6.refs_0_), channel_id=1, source_target_pairs={{0,4},{1,5},{4,8},{5,9},{8,12},{9,13},{12,14},{13,15},{14,10},{15,... | collective-permute-start | bytes 2138120 | tf_op jit(solution)/shard_map/ppermute | solution.py:435
  19.1 55.9 %collective-permute-start.9 = (bf16[768,1536]{1,0:T(8,128)(2,1)S(1)}, bf16[768,1536]{1,0:T(8,128)(2,1)S(1)}, u32[]{:S(2)}, u32[]{:S(2)}) collective-permute-start(bf16[768,1536]{1,0:T(8,128)(2,1)S(1)} %pad_maximum_fusion.3), channel_id=1, source_target_pairs={{0,16},{16,0},{1,17},{17,1},{2,18},{18,2},{3,19},{19,3},{4,20},{20... | collective-permute-start | bytes 7077896 | tf_op jit(solution)/shard_map/ppermute | solution.py:546
  78.8 28.1 %collective-permute-start.23 = (bf16[384,1536]{1,0:T(8,128)(2,1)}, bf16[384,1536]{1,0:T(8,128)(2,1)S(1)}, u32[]{:S(2)}, u32[]{:S(2)}) collective-permute-start(bf16[384,1536]{1,0:T(8,128)(2,1)} %bitcast.13.refs_5_.refs_7_), channel_id=1, source_target_pairs={{0,16},{16,0},{1,17},{17,1},{2,18},{18,2},{3,19},{19,3},{4,20},{20... | collective-permute-start | bytes 3538952 | tf_op jit(solution)/shard_map/ppermute | solution.py:546
  89.9 19.9 %collective-permute-start.21 = (bf16[256,1536]{1,0:T(8,128)(2,1)}, bf16[256,1536]{1,0:T(8,128)(2,1)}, u32[]{:S(2)}, u32[]{:S(2)}) collective-permute-start(bf16[256,1536]{1,0:T(8,128)(2,1)} %collective-permute-done.3.refs_2_), channel_id=1, source_target_pairs={{0,4},{1,5},{4,8},{5,9},{8,12},{9,13},{12,14},{13,15},{14,10},{15,... | collective-permute-start | bytes 2359304 | tf_op jit(solution)/shard_map/ppermute | solution.py:435
  90.8 19.6 %collective-permute-start.22 = (bf16[256,1536]{1,0:T(8,128)(2,1)}, bf16[256,1536]{1,0:T(8,128)(2,1)}, u32[]{:S(2)}, u32[]{:S(2)}) collective-permute-start(bf16[256,1536]{1,0:T(8,128)(2,1)} %collective-permute-done.4.refs_4_), channel_id=1, source_target_pairs={{4,0},{5,1},{8,4},{9,5},{12,8},{13,9},{14,12},{15,13},{10,14},{11,... | collective-permute-start | bytes 2359304 | tf_op jit(solution)/shard_map/ppermute | solution.py:438
  111.9 38.8 %collective-permute-start.28 = (bf16[528,1536]{1,0:T(8,128)(2,1)S(1)}, bf16[528,1536]{1,0:T(8,128)(2,1)}, u32[]{:S(2)}, u32[]{:S(2)}) collective-permute-start(bf16[528,1536]{1,0:T(8,128)(2,1)S(1)} %pad_maximum_fusion.4), channel_id=1, source_target_pairs={{0,1},{1,0},{2,3},{3,2},{4,5},{5,4},{6,7},{7,6},{8,9},{9,8},{10,11... | collective-permute-start | bytes 4866056 | tf_op jit(solution)/shard_map/ppermute | solution.py:441
  112.0 38.7 %collective-permute-start.25 = (bf16[272,1536]{1,0:T(8,128)(2,1)S(1)}, bf16[272,1536]{1,0:T(8,128)(2,1)}, u32[]{:S(2)}, u32[]{:S(2)}) collective-permute-start(bf16[272,1536]{1,0:T(8,128)(2,1)S(1)} %copy-done.12), channel_id=1, source_target_pairs={{4,0},{5,1},{8,4},{9,5},{12,8},{13,9},{14,12},{15,13},{10,14},{11,... | collective-permute-start | bytes 2506760 | tf_op jit(solution)/shard_map/ppermute | solution.py:438
  113.2 37.5 %collective-permute-start.24 = (bf16[272,1536]{1,0:T(8,128)(2,1)S(1)}, bf16[272,1536]{1,0:T(8,128)(2,1)}, u32[]{:S(2)}, u32[]{:S(2)}) collective-permute-start(bf16[272,1536]{1,0:T(8,128)(2,1)S(1)} %copy-done.12), channel_id=1, source_target_pairs={{0,4},{1,5},{4,8},{5,9},{8,12},{9,13},{12,14},{13,15},{14,10},{15,... | collective-permute-start | bytes 2506760 | tf_op jit(solution)/shard_map/ppermute | solution.py:435
  114.1 36.6 %collective-permute-start.26 = (bf16[256,1536]{1,0:T(8,128)(2,1)}, bf16[256,1536]{1,0:T(8,128)(2,1)S(1)}, u32[]{:S(2)}, u32[]{:S(2)}) collective-permute-start(bf16[256,1536]{1,0:T(8,128)(2,1)} %collective-permute-done.21.refs_2_), channel_id=1, source_target_pairs={{0,4},{1,5},{4,8},{5,9},{8,12},{9,13},{12,14},{13,15},{14,10},{15,... | collective-permute-start | bytes 2359304 | tf_op jit(solution)/shard_map/ppermute | solution.py:435
  115.7 35.0 %collective-permute-start.27 = (bf16[256,1536]{1,0:T(8,128)(2,1)}, bf16[256,1536]{1,0:T(8,128)(2,1)S(1)}, u32[]{:S(2)}, u32[]{:S(2)}) collective-permute-start(bf16[256,1536]{1,0:T(8,128)(2,1)} %collective-permute-done.22.refs_4_), channel_id=1, source_target_pairs={{4,0},{5,1},{8,4},{9,5},{12,8},{13,9},{14,12},{15,13},{10,14},{11,... | collective-permute-start | bytes 2359304 | tf_op jit(solution)/shard_map/ppermute | solution.py:438
  154.6 30.3 %collective-permute-start.33 = (bf16[1056,1536]{1,0:T(8,128)(2,1)}, bf16[1056,1536]{1,0:T(8,128)(2,1)}, u32[]{:S(2)}, u32[]{:S(2)}) collective-permute-start(bf16[1056,1536]{1,0:T(8,128)(2,1)} %pad_maximum_fusion), channel_id=1, source_target_pairs={{0,1},{1,0},{2,3},{3,2},{4,5},{5,4},{6,7},{7,6},{8,9},{9,8},{10,11... | collective-permute-start | bytes 9732104 | tf_op jit(solution)/shard_map/ppermute | solution.py:441
  154.6 30.3 %collective-permute-start.29 = (bf16[272,1536]{1,0:T(8,128)(2,1)}, bf16[272,1536]{1,0:T(8,128)(2,1)S(1)}, u32[]{:S(2)}, u32[]{:S(2)}) collective-permute-start(bf16[272,1536]{1,0:T(8,128)(2,1)} %collective-permute-done.24.refs_1_), channel_id=1, source_target_pairs={{0,4},{1,5},{4,8},{5,9},{8,12},{9,13},{12,14},{13,15},{14,10},{15,... | collective-permute-start | bytes 2506760 | tf_op jit(solution)/shard_map/ppermute | solution.py:435
  155.5 29.3 %collective-permute-start.30 = (bf16[272,1536]{1,0:T(8,128)(2,1)}, bf16[272,1536]{1,0:T(8,128)(2,1)S(1)}, u32[]{:S(2)}, u32[]{:S(2)}) collective-permute-start(bf16[272,1536]{1,0:T(8,128)(2,1)} %collective-permute-done.25.refs_3_), channel_id=1, source_target_pairs={{4,0},{5,1},{8,4},{9,5},{12,8},{13,9},{14,12},{15,13},{10,14},{11,... | collective-permute-start | bytes 2506760 | tf_op jit(solution)/shard_map/ppermute | solution.py:438
  156.7 28.1 %collective-permute-start.32 = (bf16[128,1536]{1,0:T(8,128)(2,1)S(1)}, bf16[128,1536]{1,0:T(8,128)(2,1)S(1)}, u32[]{:S(2)}, u32[]{:S(2)}) collective-permute-start(bf16[128,1536]{1,0:T(8,128)(2,1)S(1)} %slice.159), channel_id=1, source_target_pairs={{4,0},{5,1},{8,4},{9,5},{12,8},{13,9},{14,12},{15,13},{10,14},{11,... | collective-permute-start | bytes 1179656 | tf_op jit(solution)/shard_map/ppermute | solution.py:438
  158.4 26.5 %collective-permute-start.31 = (bf16[128,1536]{1,0:T(8,128)(2,1)S(1)}, bf16[128,1536]{1,0:T(8,128)(2,1)S(1)}, u32[]{:S(2)}, u32[]{:S(2)}) collective-permute-start(bf16[128,1536]{1,0:T(8,128)(2,1)S(1)} %slice.158), channel_id=1, source_target_pairs={{0,4},{1,5},{4,8},{5,9},{8,12},{9,13},{12,14},{13,15},{14,10},{15,... | collective-permute-start | bytes 1179656 | tf_op jit(solution)/shard_map/ppermute | solution.py:435
  188.5 22.6 %collective-permute-start.36 = (bf16[1056,1536]{1,0:T(8,128)(2,1)}, bf16[1056,1536]{1,0:T(8,128)(2,1)}, u32[]{:S(2)}, u32[]{:S(2)}) collective-permute-start(bf16[1056,1536]{1,0:T(8,128)(2,1)} %pad_maximum_fusion.1), channel_id=1, source_target_pairs={{0,1},{1,0},{2,3},{3,2},{4,5},{5,4},{6,7},{7,6},{8,9},{9,8},{10,11... | collective-permute-start | bytes 9732104 | tf_op jit(solution)/shard_map/ppermute | solution.py:441
  188.5 21.0 %collective-permute-start.34 = (bf16[272,1536]{1,0:T(8,128)(2,1)S(1)}, bf16[272,1536]{1,0:T(8,128)(2,1)S(1)}, u32[]{:S(2)}, u32[]{:S(2)}) collective-permute-start(bf16[272,1536]{1,0:T(8,128)(2,1)S(1)} %collective-permute-done.29.refs_1_), channel_id=1, source_target_pairs={{0,4},{1,5},{4,8},{5,9},{8,12},{9,13},{12,14},{13,15},{14,10},{15,... | collective-permute-start | bytes 2506760 | tf_op jit(solution)/shard_map/ppermute | solution.py:435
  190.2 20.9 %collective-permute-start.35 = (bf16[272,1536]{1,0:T(8,128)(2,1)}, bf16[272,1536]{1,0:T(8,128)(2,1)S(1)}, u32[]{:S(2)}, u32[]{:S(2)}) collective-permute-start(bf16[272,1536]{1,0:T(8,128)(2,1)} %copy-done.11), channel_id=1, source_target_pairs={{4,0},{5,1},{8,4},{9,5},{12,8},{13,9},{14,12},{15,13},{10,14},{11,... | collective-permute-start | bytes 2506760 | tf_op jit(solution)/shard_map/ppermute | solution.py:438
  252.4 19.5 %collective-permute-start.43 = (bf16[144,1536]{1,0:T(8,128)(2,1)S(1)}, bf16[144,1536]{1,0:T(8,128)(2,1)S(1)}, u32[]{:S(2)}, u32[]{:S(2)}) collective-permute-start(bf16[144,1536]{1,0:T(8,128)(2,1)S(1)} %slice.209), channel_id=1, source_target_pairs={{4,0},{5,1},{8,4},{9,5},{12,8},{13,9},{14,12},{15,13},{10,14},{11,... | collective-permute-start | bytes 1327112 | tf_op jit(solution)/shard_map/ppermute | solution.py:438
  278.9 21.6 %collective-permute-start.45 = (bf16[2,272,1536]{2,1,0:T(8,128)(2,1)}, bf16[2,272,1536]{2,1,0:T(8,128)(2,1)S(1)}, u32[]{:S(2)}, u32[]{:S(2)}) collective-permute-start(bf16[2,272,1536]{2,1,0:T(8,128)(2,1)} %get-tuple-element.351), channel_id=1, source_target_pairs={{0,1},{1,0},{2,3},{3,2},{4,5},{5,4},{6,7},{7,6},{8,9},{9,8},{10,11... | collective-permute-start | bytes 5013512 | tf_op jit(solution)/shard_map/ppermute | solution.py:441
  279.0 21.2 %collective-permute-start.47 = (bf16[272,1536]{1,0:T(8,128)(2,1)}, bf16[272,1536]{1,0:T(8,128)(2,1)}, u32[]{:S(2)}, u32[]{:S(2)}) collective-permute-start(bf16[272,1536]{1,0:T(8,128)(2,1)} %get-tuple-element.478), channel_id=1, source_target_pairs={{4,0},{5,1},{8,4},{9,5},{12,8},{13,9},{14,12},{15,13},{10,14},{11,... | collective-permute-start | bytes 2506760 | tf_op jit(solution)/shard_map/ppermute | solution.py:438
  279.4 21.0 %collective-permute-start.46 = (bf16[272,1536]{1,0:T(8,128)(2,1)}, bf16[272,1536]{1,0:T(8,128)(2,1)}, u32[]{:S(2)}, u32[]{:S(2)}) collective-permute-start(bf16[272,1536]{1,0:T(8,128)(2,1)} %get-tuple-element.479), channel_id=1, source_target_pairs={{0,4},{1,5},{4,8},{5,9},{8,12},{9,13},{12,14},{13,15},{14,10},{15,... | collective-permute-start | bytes 2506760 | tf_op jit(solution)/shard_map/ppermute | solution.py:435
  302.8 22.4 %collective-permute-start.48 = (bf16[2,272,1536]{2,1,0:T(8,128)(2,1)S(1)}, bf16[2,272,1536]{2,1,0:T(8,128)(2,1)S(1)}, u32[]{:S(2)}, u32[]{:S(2)}) collective-permute-start(bf16[2,272,1536]{2,1,0:T(8,128)(2,1)S(1)} %copy-done.54), channel_id=1, source_target_pairs={{0,1},{1,0},{2,3},{3,2},{4,5},{5,4},{6,7},{7,6},{8,9},{9,8},{10,11... | collective-permute-start | bytes 5013512 | tf_op jit(solution)/shard_map/ppermute | solution.py:441
  302.8 21.0 %collective-permute-start.49 = (bf16[272,1536]{1,0:T(8,128)(2,1)S(1)}, bf16[272,1536]{1,0:T(8,128)(2,1)S(1)}, u32[]{:S(2)}, u32[]{:S(2)}) collective-permute-start(bf16[272,1536]{1,0:T(8,128)(2,1)S(1)} %get-tuple-element.380), channel_id=1, source_target_pairs={{0,4},{1,5},{4,8},{5,9},{8,12},{9,13},{12,14},{13,15},{14,10},{15,... | collective-permute-start | bytes 2506760 | tf_op jit(solution)/shard_map/ppermute | solution.py:435
  304.5 20.7 %collective-permute-start.50 = (bf16[272,1536]{1,0:T(8,128)(2,1)S(1)}, bf16[272,1536]{1,0:T(8,128)(2,1)S(1)}, u32[]{:S(2)}, u32[]{:S(2)}) collective-permute-start(bf16[272,1536]{1,0:T(8,128)(2,1)S(1)} %get-tuple-element.381), channel_id=1, source_target_pairs={{4,0},{5,1},{8,4},{9,5},{12,8},{13,9},{14,12},{15,13},{10,14},{11,... | collective-permute-start | bytes 2506760 | tf_op jit(solution)/shard_map/ppermute | solution.py:438
  304.9 21.4 %collective-permute-start.51 = (bf16[288,1536]{1,0:T(8,128)(2,1)S(1)}, bf16[288,1536]{1,0:T(8,128)(2,1)S(1)}, u32[]{:S(2)}, u32[]{:S(2)}) collective-permute-start(bf16[288,1536]{1,0:T(8,128)(2,1)S(1)} %copy-done.56), channel_id=1, source_target_pairs={{0,16},{16,0},{1,17},{17,1},{2,18},{18,2},{3,19},{19,3},{4,20},{20... | collective-permute-start | bytes 2654216 | tf_op jit(solution)/shard_map/ppermute | solution.py:546
  326.6 21.9 %collective-permute-start.55 = (bf16[288,1536]{1,0:T(8,128)(2,1)S(1)}, bf16[288,1536]{1,0:T(8,128)(2,1)S(1)}, u32[]{:S(2)}, u32[]{:S(2)}) collective-permute-start(bf16[288,1536]{1,0:T(8,128)(2,1)S(1)} %copy-done.55), channel_id=1, source_target_pairs={{0,16},{16,0},{1,17},{17,1},{2,18},{18,2},{3,19},{19,3},{4,20},{20... | collective-permute-start | bytes 2654216 | tf_op jit(solution)/shard_map/ppermute | solution.py:546
  327.1 21.4 %collective-permute-start.53 = (bf16[272,1536]{1,0:T(8,128)(2,1)S(1)}, bf16[272,1536]{1,0:T(8,128)(2,1)S(1)}, u32[]{:S(2)}, u32[]{:S(2)}) collective-permute-start(bf16[272,1536]{1,0:T(8,128)(2,1)S(1)} %get-tuple-element.384), channel_id=1, source_target_pairs={{0,4},{1,5},{4,8},{5,9},{8,12},{9,13},{12,14},{13,15},{14,10},{15,... | collective-permute-start | bytes 2506760 | tf_op jit(solution)/shard_map/ppermute | solution.py:435
  328.5 20.4 %collective-permute-start.54 = (bf16[272,1536]{1,0:T(8,128)(2,1)S(1)}, bf16[272,1536]{1,0:T(8,128)(2,1)S(1)}, u32[]{:S(2)}, u32[]{:S(2)}) collective-permute-start(bf16[272,1536]{1,0:T(8,128)(2,1)S(1)} %get-tuple-element.385), channel_id=1, source_target_pairs={{4,0},{5,1},{8,4},{9,5},{12,8},{13,9},{14,12},{15,13},{10,14},{11,... | collective-permute-start | bytes 2506760 | tf_op jit(solution)/shard_map/ppermute | solution.py:438
  352.1 21.2 %collective-permute-start.60 = (bf16[288,1536]{1,0:T(8,128)(2,1)}, bf16[288,1536]{1,0:T(8,128)(2,1)S(1)}, u32[]{:S(2)}, u32[]{:S(2)}) collective-permute-start(bf16[288,1536]{1,0:T(8,128)(2,1)} %get-tuple-element.404), channel_id=1, source_target_pairs={{0,16},{16,0},{1,17},{17,1},{2,18},{18,2},{3,19},{19,3},{4,20},{20... | collective-permute-start | bytes 2654216 | tf_op jit(solution)/shard_map/ppermute | solution.py:546
  374.2 25.3 %collective-permute-start.65 = (bf16[2,8,48,1536]{3,2,1,0:T(8,128)(2,1)}, bf16[2,8,48,1536]{3,2,1,0:T(8,128)(2,1)S(1)}, u32[]{:S(2)}, u32[]{:S(2)}) collective-permute-start(bf16[2,8,48,1536]{3,2,1,0:T(8,128)(2,1)} %get-tuple-element.422), channel_id=1, source_target_pairs={{0,1},{1,0},{2,3},{3,2},{4,5},{5,4},{6,7},{7,6},{8,9},{9,8},{10,11... | collective-permute-start | bytes 7077896 | tf_op jit(solution)/shard_map/ppermute | solution.py:441
  374.2 21.6 %collective-permute-start.61 = (bf16[2,256,1536]{2,1,0:T(8,128)(2,1)}, bf16[2,256,1536]{2,1,0:T(8,128)(2,1)S(1)}, u32[]{:S(2)}, u32[]{:S(2)}) collective-permute-start(bf16[2,256,1536]{2,1,0:T(8,128)(2,1)} %get-tuple-element.407), channel_id=1, source_target_pairs={{0,1},{1,0},{2,3},{3,2},{4,5},{5,4},{6,7},{7,6},{8,9},{9,8},{10,11... | collective-permute-start | bytes 4718600 | tf_op jit(solution)/shard_map/ppermute | solution.py:441
  374.7 19.8 %collective-permute-start.62 = (bf16[256,1536]{1,0:T(8,128)(2,1)}, bf16[256,1536]{1,0:T(8,128)(2,1)}, u32[]{:S(2)}, u32[]{:S(2)}) collective-permute-start(bf16[256,1536]{1,0:T(8,128)(2,1)} %get-tuple-element.405), channel_id=1, source_target_pairs={{0,4},{1,5},{4,8},{5,9},{8,12},{9,13},{12,14},{13,15},{14,10},{15,... | collective-permute-start | bytes 2359304 | tf_op jit(solution)/shard_map/ppermute | solution.py:435
  376.3 19.5 %collective-permute-start.63 = (bf16[256,1536]{1,0:T(8,128)(2,1)}, bf16[256,1536]{1,0:T(8,128)(2,1)}, u32[]{:S(2)}, u32[]{:S(2)}) collective-permute-start(bf16[256,1536]{1,0:T(8,128)(2,1)} %get-tuple-element.406), channel_id=1, source_target_pairs={{4,0},{5,1},{8,4},{9,5},{12,8},{13,9},{14,12},{15,13},{10,14},{11,... | collective-permute-start | bytes 2359304 | tf_op jit(solution)/shard_map/ppermute | solution.py:438
  376.8 22.8 %collective-permute-start.64 = (bf16[288,1536]{1,0:T(8,128)(2,1)}, bf16[288,1536]{1,0:T(8,128)(2,1)}, u32[]{:S(2)}, u32[]{:S(2)}) collective-permute-start(bf16[288,1536]{1,0:T(8,128)(2,1)} %get-tuple-element.420), channel_id=1, source_target_pairs={{0,16},{16,0},{1,17},{17,1},{2,18},{18,2},{3,19},{19,3},{4,20},{20... | collective-permute-start | bytes 2654216 | tf_op jit(solution)/shard_map/ppermute | solution.py:546
  401.0 36.3 %collective-permute-start.70 = (bf16[2,8,48,2176]{3,2,1,0:T(8,128)(2,1)}, bf16[2,8,48,2176]{3,2,1,0:T(8,128)(2,1)S(1)}, u32[]{:S(2)}, u32[]{:S(2)}) collective-permute-start(bf16[2,8,48,2176]{3,2,1,0:T(8,128)(2,1)} %get-tuple-element.432), channel_id=1, source_target_pairs={{0,1},{1,0},{2,3},{3,2},{4,5},{5,4},{6,7},{7,6},{8,9},{9,8},{10,11... | collective-permute-start | bytes 10027016 | tf_op jit(solution)/shard_map/ppermute | solution.py:441
  403.7 28.7 %collective-permute-start.69 = (bf16[8,48,1536]{2,1,0:T(8,128)(2,1)}, bf16[8,48,1536]{2,1,0:T(8,128)(2,1)}, u32[]{:S(2)}, u32[]{:S(2)}) collective-permute-start(bf16[8,48,1536]{2,1,0:T(8,128)(2,1)} %fusion.32), channel_id=1, source_target_pairs={{0,16},{16,0},{1,17},{17,1},{2,18},{18,2},{3,19},{19,3},{4,20},{20... | collective-permute-start | bytes 3538952 | tf_op jit(solution)/shard_map/ppermute | solution.py:546
  404.7 30.2 %collective-permute-start.66 = (bf16[2,256,1536]{2,1,0:T(8,128)(2,1)}, bf16[2,256,1536]{2,1,0:T(8,128)(2,1)}, u32[]{:S(2)}, u32[]{:S(2)}) collective-permute-start(bf16[2,256,1536]{2,1,0:T(8,128)(2,1)} %get-tuple-element.425), channel_id=1, source_target_pairs={{0,1},{1,0},{2,3},{3,2},{4,5},{5,4},{6,7},{7,6},{8,9},{9,8},{10,11... | collective-permute-start | bytes 4718600 | tf_op jit(solution)/shard_map/ppermute | solution.py:441
  404.9 29.9 %collective-permute-start.67 = (bf16[256,1536]{1,0:T(8,128)(2,1)}, bf16[256,1536]{1,0:T(8,128)(2,1)S(1)}, u32[]{:S(2)}, u32[]{:S(2)}) collective-permute-start(bf16[256,1536]{1,0:T(8,128)(2,1)} %get-tuple-element.423), channel_id=1, source_target_pairs={{0,4},{1,5},{4,8},{5,9},{8,12},{9,13},{12,14},{13,15},{14,10},{15,... | collective-permute-start | bytes 2359304 | tf_op jit(solution)/shard_map/ppermute | solution.py:435
  406.2 28.6 %collective-permute-start.68 = (bf16[256,1536]{1,0:T(8,128)(2,1)}, bf16[256,1536]{1,0:T(8,128)(2,1)}, u32[]{:S(2)}, u32[]{:S(2)}) collective-permute-start(bf16[256,1536]{1,0:T(8,128)(2,1)} %get-tuple-element.424), channel_id=1, source_target_pairs={{4,0},{5,1},{8,4},{9,5},{12,8},{13,9},{14,12},{15,13},{10,14},{11,... | collective-permute-start | bytes 2359304 | tf_op jit(solution)/shard_map/ppermute | solution.py:438
  437.9 38.2 %collective-permute-start.74 = (bf16[8,48,2176]{2,1,0:T(8,128)(2,1)S(1)}, bf16[8,48,2176]{2,1,0:T(8,128)(2,1)S(1)}, u32[]{:S(2)}, u32[]{:S(2)}) collective-permute-start(bf16[8,48,2176]{2,1,0:T(8,128)(2,1)S(1)} %fusion.2), channel_id=1, source_target_pairs={{0,16},{16,0},{1,17},{17,1},{2,18},{18,2},{3,19},{19,3},{4,20},{20... | collective-permute-start | bytes 5013512 | tf_op jit(solution)/shard_map/ppermute | solution.py:546
  440.4 39.2 %collective-permute-start.86 = (bf16[48,1536]{1,0:T(8,128)(2,1)S(1)}, bf16[48,1536]{1,0:T(8,128)(2,1)S(1)}, u32[]{:S(2)}, u32[]{:S(2)}) collective-permute-start(bf16[48,1536]{1,0:T(8,128)(2,1)S(1)} %get-tuple-element.490), channel_id=1, source_target_pairs={{4,0},{5,1},{8,4},{9,5},{12,8},{13,9},{14,12},{15,13},{10,14},{11,... | collective-permute-start | bytes 442376 | tf_op jit(solution)/shard_map/ppermute | solution.py:438
  441.1 37.1 %collective-permute-start.72 = (bf16[256,1536]{1,0:T(8,128)(2,1)S(1)}, bf16[256,1536]{1,0:T(8,128)(2,1)S(1)}, u32[]{:S(2)}, u32[]{:S(2)}) collective-permute-start(bf16[256,1536]{1,0:T(8,128)(2,1)S(1)} %get-tuple-element.433), channel_id=1, source_target_pairs={{0,4},{1,5},{4,8},{5,9},{8,12},{9,13},{12,14},{13,15},{14,10},{15,... | collective-permute-start | bytes 2359304 | tf_op jit(solution)/shard_map/ppermute | solution.py:435
  442.4 35.8 %collective-permute-start.73 = (bf16[256,1536]{1,0:T(8,128)(2,1)S(1)}, bf16[256,1536]{1,0:T(8,128)(2,1)S(1)}, u32[]{:S(2)}, u32[]{:S(2)}) collective-permute-start(bf16[256,1536]{1,0:T(8,128)(2,1)S(1)} %get-tuple-element.434), channel_id=1, source_target_pairs={{4,0},{5,1},{8,4},{9,5},{12,8},{13,9},{14,12},{15,13},{10,14},{11,... | collective-permute-start | bytes 2359304 | tf_op jit(solution)/shard_map/ppermute | solution.py:438
  445.8 59.5 %collective-permute-start.71 = (bf16[1,256,1536]{2,1,0:T(8,128)(2,1)S(1)}, bf16[1,256,1536]{2,1,0:T(8,128)(2,1)S(1)}, u32[]{:S(2)}, u32[]{:S(2)}) collective-permute-start(bf16[1,256,1536]{2,1,0:T(8,128)(2,1)S(1)} %copy-done.58), channel_id=1, source_target_pairs={{0,1},{1,0},{2,3},{3,2},{4,5},{5,4},{6,7},{7,6},{8,9},{9,8},{10,11... | collective-permute-start | bytes 2359304 | tf_op jit(solution)/shard_map/ppermute | solution.py:441
  (101 other events, 1240.2 us)

commit v3 on v2

--- a/solution.py
+++ b/solution.py
@@ -41,14 +41,14 @@
     return pl.BlockSpec(memory_space=pltpu.SMEM)
 
 
-def call(body, outs, ins, args, name, flops, scratch=()):
+def call(body, outs, ins, args, name, vmem_mb, scratch=()):
     return pl.pallas_call(
         body,
         out_shape=outs,
         in_specs=ins,
         out_specs=vmem(len(outs)),
         scratch_shapes=list(scratch),
-        compiler_params=pltpu.CompilerParams(vmem_limit_bytes=60 * 1024 * 1024),
+        compiler_params=pltpu.CompilerParams(vmem_limit_bytes=vmem_mb * 1024 * 1024),
         cost_estimate=pl.CostEstimate(flops=1 << 20, bytes_accessed=1 << 20, transcendentals=0),
         name=name,
     )(*args)
@@ -647,7 +647,7 @@
         [smem(), smem()] + vmem(4 + len(dense)),
         [where_i, table, x, cos, sin, routes.reshape(tokens, topk), *dense],
         "forward",
-        2 * tokens * WIDTH * (MISC + Q_COLS),
+        60,
     )
 
     n_ring = ring.gather(send, split)
@@ -655,8 +655,8 @@
     kept = {}
     groups = [[0]] + [[-s, s] for s in range(1, ring.half)] + [[ring.half]]
 
-    def far_of(group):
-        return ring.send_core(jnp.concatenate([p for o in group for r in (n_ring, g_ring) for p in r.got[o]]))
+    def pieces_of(group):
+        return jnp.concatenate([p for o in group for r in (n_ring, g_ring) for p in r.got[o]])
 
     def experts_on(group, far, *events):
         args, arrays, offset = [far], [], 0
@@ -685,7 +685,7 @@
             [smem()] + vmem(len(args) + len(expert_weights)),
             [after(where_i, *events), *args, *expert_weights],
             "experts",
-            2 * rows_ * WIDTH * hidden_size * 6,
+            36,
             [
                 pltpu.VMEM((rows_, WIDTH), bf16),
                 pltpu.VMEM((rows_, LANES), f32),
@@ -700,19 +700,20 @@
         kept[group[0]] = outs[2 * n + 2 :]
         return kept[group[0]]
 
-    fence(g_ring, n_ring, expert_weights[-1])
+    waiting, _ = fence(pieces_of(groups[0]), expert_weights[-1], n_ring, g_ring)
     far = []
     for hop in range(1, ring.half + 1):
         n_ring.hop()
         if g_ring.hops < ring.half:
             g_ring.hop()
-        near, far = far, far_of(groups[hop - 1])
+        near, far = far, ring.send_core(waiting)
+        waiting = pieces_of(groups[hop])
         if hop > 1:
             group = groups[hop - 2]
-            far, kept[group[0]] = fence(n_ring, g_ring, far, experts_on(group, near))
+            waiting, far, kept[group[0]] = fence(waiting, far, experts_on(group, near), n_ring, g_ring)
         else:
-            (far,) = fence(n_ring, g_ring, far)
-    (last,) = fence(n_ring, g_ring, far_of(groups[-1]))
+            waiting, far = fence(waiting, far, n_ring, g_ring)
+    (last,) = fence(ring.send_core(waiting))
     experts_on(groups[-1], last)
     dx_ring = ring.scatter(dx_own, dx_far, split)
     dx_ring.swap(groups[-1])
@@ -733,7 +734,7 @@
                 [smem()] + vmem(len(saved) + len(more)),
                 [after(where_i, *events), *saved, *more],
                 "expert_weights",
-                2 * experts * slots * wide * hidden_size * 3,
+                36,
             )
 
         more = []
@@ -767,7 +768,7 @@
         [smem(), smem()] + vmem(11),
         [after(where_i, *out_ring.sent), table, *dx_terms, g, hidden, gains, gate_values, misc_full, o_t, mixed],
         "hidden_back",
-        4 * tokens * WIDTH * Q_COLS,
+        36,
         [pltpu.VMEM((WIDTH, Q_COLS), bf16)] if apart else [],
     )
     out_ring.step(dh, *more[2:3])
@@ -779,7 +780,7 @@
         [smem(), smem()] + vmem(13),
         [after(where_i, *out_ring.sent), table, x, cos, sin, w_full, gains, n1, q, k, v, dmixed, dh, router_part, gain_part],
         "attend_back",
-        4 * tokens * WIDTH * MISC,
+        36,
         ([pltpu.VMEM((WIDTH, MISC + LANES), bf16)] if apart else []) + [pltpu.VMEM((tokens, MISC), bf16)],
     )
 

time: 522 us -> 498 us (0.954)
  Pallas kernels: 143 us -> 109 us
  local copies, waits for them, and re-layouts: 12.9 us -> 19.5 us
    pallas_call x10, Pallas kernels: 143 us -> 109 us  [call(): pl.pallas_call(body, out_shape=outs, in_specs=ins, out_specs=vmem(len(out...]
    ppermute x28, waiting for transfers between devices: 108 us -> 96.6 us  [send_up(): return lax.ppermute(x, 'expert', self.up)]
    ppermute x26, waiting for transfers between devices: 55.5 us -> 66.6 us  [send_down(): return lax.ppermute(x, 'expert', self.down)]
    unnamed x123 -> x269, local copies, waits for them, and re-layouts: 6.9 us -> 14.4 us
    ppermute x9, waiting for transfers between devices: 70 us -> 77.4 us  [from_dp(): return lax.ppermute(x, 'dp', dp_pairs(shift))]
  transfers between devices with their start and end apart: 89 -> 89, of which waited for: 47 -> 49; matrix products, arithmetic and copies ran while one was open for 4% -> 7% of each run, Pallas kernels for 26% -> 21%
where the time goes in v3:
time: 498 us; the launch traced here: 490 us
  waiting for transfers between devices  251 us (50%)
  Pallas kernels  109 us (22%)
  starting transfers between devices  72.6 us (15%)
  other arithmetic  34.8 us (7%)
  local copies, waits for them, and re-layouts  19.5 us (4%)
    pallas_call x10, Pallas kernels, call(): pl.pallas_call(body, out_shape=outs, in_specs=ins, out_specs=vmem(len(out...  109 us
    ppermute x28, waiting for transfers between devices, send_up(): return lax.ppermute(x, 'expert', self.up)  96.6 us
    ppermute x9, waiting for transfers between devices, from_dp(): return lax.ppermute(x, 'dp', dp_pairs(shift))  77.4 us
    ppermute x26, waiting for transfers between devices, send_down(): return lax.ppermute(x, 'expert', self.down)  66.6 us
    ppermute x28, starting transfers between devices, send_up(): return lax.ppermute(x, 'expert', self.up)  34.6 us
    ppermute x26, starting transfers between devices, send_down(): return lax.ppermute(x, 'expert', self.down)  24.3 us
    convert_element_type x19, other arithmetic, total(): return out.astype(bf16)  21.8 us
    unnamed x269, local copies, waits for them, and re-layouts  14.4 us
  transfers between devices with their start and end apart: 89, of which 49 were waited for; matrix products, arithmetic and copies ran while one was open for 7% of the time, Pallas kernels for 21%

profile of v3, /device:TPU:0, one launch (start us, length us, event | category | flops | bytes accessed | tf_op | source)
XLA Modules:
  0.0 490.4 jit_solution(5897444439480502474)
XLA Ops:
  4.2 3.0 collective-permute-start
  9.2 6.3 %collective-permute-done = bf16[48,3712]{1,0:T(8,128)(2,1)S(1)} collective-permute-done((bf16[48,3712]{1,0:T(8,128)(2,1)S(1)}, bf16[48,3712]{1,0:T(8,128)(2,1)S(1)}, u32[]{:S(2)}, u32[]{:S(2)}) %collective-permute-start) | collective-permute-done | bytes 356384 | tf_op jit(solution)/shard_map/ppermute | solution.py:546
  15.6 1.8 collective-permute-start.2
  19.1 1.8 collective-permute-start.9
  20.9 7.0 %collective-permute-done.4.refs_4_ = bf16[256,1536]{1,0:T(8,128)(2,1)} collective-permute-done((bf16[256,1536]{1,0:T(8,128)(2,1)}, bf16[256,1536]{1,0:T(8,128)(2,1)}, u32[]{:S(2)}, u32[]{:S(2)}) %collective-permute-start.4) | collective-permute-done | bytes 786464 | tf_op jit(solution)/shard_map/ppermute | solution.py:438
  29.5 12.2 %collective-permute-done.2.refs_4_ = bf16[2,48,3712]{2,1,0:T(8,128)(2,1)S(1)} collective-permute-done((bf16[2,48,3712]{2,1,0:T(8,128)(2,1)S(1)}, bf16[2,48,3712]{2,1,0:T(8,128)(2,1)S(1)}, u32[]{:S(2)}, u32[]{:S(2)}) %collective-permute-start.2) | collective-permute-done | bytes 712736 | tf_op jit(solution)/shard_map/ppermute | solution.py:438
  44.9 14.2 %collective-permute-done.5.refs_6_ = bf16[2,48,3712]{2,1,0:T(8,128)(2,1)S(1)} collective-permute-done((bf16[2,48,3712]{2,1,0:T(8,128)(2,1)S(1)}, bf16[2,48,3712]{2,1,0:T(8,128)(2,1)S(1)}, u32[]{:S(2)}, u32[]{:S(2)}) %collective-permute-start.5) | collective-permute-done | bytes 712736 | tf_op jit(solution)/shard_map/ppermute | solution.py:435
  61.6 12.7 %collective-permute-done.6.refs_10_ = bf16[2,48,3712]{2,1,0:T(8,128)(2,1)S(1)} collective-permute-done((bf16[2,48,3712]{2,1,0:T(8,128)(2,1)S(1)}, bf16[2,48,3712]{2,1,0:T(8,128)(2,1)S(1)}, u32[]{:S(2)}, u32[]{:S(2)}) %collective-permute-start.6) | collective-permute-done | bytes 712736 | tf_op jit(solution)/shard_map/ppermute | solution.py:435
  79.3 7.7 %collective-permute-done.11.refs_15_ = bf16[1,48,3712]{2,1,0:T(8,128)(2,1)S(1)} collective-permute-done((bf16[1,48,3712]{2,1,0:T(8,128)(2,1)S(1)}, bf16[1,48,3712]{2,1,0:T(8,128)(2,1)S(1)}, u32[]{:S(2)}, u32[]{:S(2)}) %collective-permute-start.11) | collective-permute-done | bytes 356384 | tf_op jit(solution)/shard_map/ppermute | solution.py:438
  93.4 13.3 %forward.1 = (bf16[1536,2048]{1,0:T(8,128)(2,1)}, bf16[1536,1536]{1,0:T(8,128)(2,1)}, bf16[1536,128]{1,0:T(8,128)(2,1)}, f32[8,1536]{1,0:T(8,128)}, bf16[256,153...) custom-call(s32[4]{0:T(128)} %pad_add_fusion.me_ref, ...), custom_call_target="tpu_custom_call" | custom-call | flops 1048576 | bytes 1048576 | tf_op jit(solution)/shard_map/forward/pallas_call | solution.py:45
  114.5 17.3 %collective-permute-done.25.refs_3_ = bf16[272,1536]{1,0:T(8,128)(2,1)S(1)} collective-permute-done((bf16[272,1536]{1,0:T(8,128)(2,1)S(1)}, bf16[272,1536]{1,0:T(8,128)(2,1)S(1)}, u32[]{:S(2)}, u32[]{:S(2)}) %collective-permute-start.25) | collective-permute-done | bytes 835616 | tf_op jit(solution)/shard_map/ppermute | solution.py:438
  133.0 3.3 pad_maximum_fusion
  136.3 12.8 %collective-permute-done.26.refs_2_ = bf16[256,1536]{1,0:T(8,128)(2,1)S(1)} collective-permute-done((bf16[256,1536]{1,0:T(8,128)(2,1)}, bf16[256,1536]{1,0:T(8,128)(2,1)S(1)}, u32[]{:S(2)}, u32[]{:S(2)}) %collective-permute-start.26) | collective-permute-done | bytes 786464 | tf_op jit(solution)/shard_map/ppermute | solution.py:435
  153.6 7.3 %experts.5 = (bf16[256,1536]{1,0:T(8,128)(2,1)S(1)}, bf16[272,1536]{1,0:T(8,128)(2,1)S(1)}, bf16[1,256,1536]{2,1,0:T(8,128)(2,1)S(1)}, bf16[1,272,1536]{2,1,0:T(...) custom-call(s32[4]{0:T(128)S(1)} %copy-done.101, ...), custom_call_target="tpu_custom_call" | custom-call | flops 1048576 | bytes 1048576 | tf_op jit(solution)/shard_map/experts/pallas_call | solution.py:45
  161.9 8.7 %collective-permute-done.29.refs_1_ = bf16[272,1536]{1,0:T(8,128)(2,1)S(1)} collective-permute-done((bf16[272,1536]{1,0:T(8,128)(2,1)S(1)}, bf16[272,1536]{1,0:T(8,128)(2,1)S(1)}, u32[]{:S(2)}, u32[]{:S(2)}) %collective-permute-start.29) | collective-permute-done | bytes 835616 | tf_op jit(solution)/shard_map/ppermute | solution.py:435
  171.6 3.2 pad_maximum_fusion.1
  174.8 4.4 collective-permute-done.32.refs_4_
  182.2 12.9 %experts.6 = (bf16[256,1536]{1,0:T(8,128)(2,1)S(1)}, bf16[256,1536]{1,0:T(8,128)(2,1)S(1)}, bf16[272,1536]{1,0:T(8,128)(2,1)S(1)}, bf16[272,1536]{1,0:T(8,128)(2...) custom-call(s32[4]{0:T(128)S(1)} %copy-done.101, ...), custom_call_target="tpu_custom_call" | custom-call | flops 1048576 | bytes 1048576 | tf_op jit(solution)/shard_map/experts/pallas_call | solution.py:45
  196.4 3.9 collective-permute-done.34.refs_1_
  201.7 1.9 pad_maximum_fusion.2
  204.3 2.0 collective-permute-start.37
  206.3 14.6 %experts.7 = (bf16[256,1536]{1,0:T(8,128)(2,1)S(1)}, bf16[256,1536]{1,0:T(8,128)(2,1)S(1)}, bf16[272,1536]{1,0:T(8,128)(2,1)S(1)}, bf16[272,1536]{1,0:T(8,128)(2...) custom-call(s32[4]{0:T(128)S(1)} %copy-done.101, ...), custom_call_target="tpu_custom_call" | custom-call | flops 1048576 | bytes 1048576 | tf_op jit(solution)/shard_map/experts/pallas_call | solution.py:45
  222.9 2.6 collective-permute-done.40.refs_0_
  226.5 7.3 %experts.8 = (bf16[256,1536]{1,0:T(8,128)(2,1)S(1)}, bf16[272,1536]{1,0:T(8,128)(2,1)S(1)}, bf16[1,256,1536]{2,1,0:T(8,128)(2,1)S(1)}, bf16[1,272,1536]{2,1,0:T(...) custom-call(s32[4]{0:T(128)S(1)} %copy-done.101, ...), custom_call_target="tpu_custom_call" | custom-call | flops 1048576 | bytes 1048576 | tf_op jit(solution)/shard_map/experts/pallas_call | solution.py:45
  234.1 2.2 collective-permute-done.41
  238.9 13.5 %experts.9 = (bf16[256,1536]{1,0:T(8,128)(2,1)S(1)}, bf16[256,1536]{1,0:T(8,128)(2,1)S(1)}, bf16[272,1536]{1,0:T(8,128)(2,1)S(1)}, bf16[272,1536]{1,0:T(8,128)(2...) custom-call(s32[4]{0:T(128)S(1)} %copy-done.101, ...), custom_call_target="tpu_custom_call" | custom-call | flops 1048576 | bytes 1048576 | tf_op jit(solution)/shard_map/experts/pallas_call | solution.py:45
  253.4 3.5 collective-permute-done.44
  260.2 9.5 %expert_weights.2 = (bf16[288,1536]{1,0:T(8,128)(2,1)S(1)}, bf16[288,1536]{1,0:T(8,128)(2,1)S(1)}, bf16[288,1536]{1,0:T(8,128)(2,1)}, bf16[288,1536]{1,0:T(8,128)(2,1)}) custom-call(s32[4]{0:T(128)S(1)} %copy-done.101, bf16[160,1536]{1,0:T(8,128)(2,1)S(1)} %copy-done.14, bf16[320,1536]{1,0:T(8,128)(2,1)S(1)} %get-tuple-element.347.refs_1_, ...), custom_call_target="tpu_custom_call" | custom-call | flops 1048576 | bytes 1048576 | tf_op jit(solution)/shard_map/expert_weights/pallas_call | solution.py:45
  269.7 9.0 %collective-permute-done.47 = bf16[272,1536]{1,0:T(8,128)(2,1)S(1)} collective-permute-done((bf16[272,1536]{1,0:T(8,128)(2,1)S(1)}, bf16[272,1536]{1,0:T(8,128)(2,1)S(1)}, u32[]{:S(2)}, u32[]{:S(2)}) %collective-permute-start.47) | collective-permute-done | bytes 835616 | tf_op jit(solution)/shard_map/ppermute | solution.py:438
  283.1 18.5 %collective-permute-done.49 = bf16[272,1536]{1,0:T(8,128)(2,1)S(1)} collective-permute-done((bf16[272,1536]{1,0:T(8,128)(2,1)S(1)}, bf16[272,1536]{1,0:T(8,128)(2,1)S(1)}, u32[]{:S(2)}, u32[]{:S(2)}) %collective-permute-start.49) | collective-permute-done | bytes 835616 | tf_op jit(solution)/shard_map/ppermute | solution.py:435
  307.0 19.1 %collective-permute-done.55.refs_26_ = bf16[288,1536]{1,0:T(8,128)(2,1)S(1)} collective-permute-done((bf16[288,1536]{1,0:T(8,128)(2,1)S(1)}, bf16[288,1536]{1,0:T(8,128)(2,1)S(1)}, u32[]{:S(2)}, u32[]{:S(2)}) %collective-permute-start.55) | collective-permute-done | bytes 884768 | tf_op jit(solution)/shard_map/ppermute | solution.py:546
  331.5 8.3 %hidden_back.1 = (f32[256,1536]{1,0:T(8,128)S(1)}, bf16[256,1536]{1,0:T(8,128)(2,1)S(1)}, f32[1536,128]{1,0:T(8,128)S(1)}, f32[8,1536]{1,0:T(8,128)S(1)}, bf16[2...) custom-call(s32[4]{0:T(128)S(1)} %copy-done.101, s32[32,32]{1,0:T(8,128)S(1)} %copy-done.97, ...), custom_call_target="tpu_custom_call" | custom-call | flops 1048576 | bytes 1048576 | tf_op jit(solution)/shard_map/hidden_back/pallas_call | solution.py:45
  340.5 3.9 fusion.28
  344.4 6.8 %collective-permute-done.60.refs_27_ = bf16[288,1536]{1,0:T(8,128)(2,1)S(1)} collective-permute-done((bf16[288,1536]{1,0:T(8,128)(2,1)}, bf16[288,1536]{1,0:T(8,128)(2,1)S(1)}, u32[]{:S(2)}, u32[]{:S(2)}) %collective-permute-start.60) | collective-permute-done | bytes 884768 | tf_op jit(solution)/shard_map/ppermute | solution.py:546
  357.1 11.8 %attend_back.1 = (f32[256,1536]{1,0:T(8,128)}, bf16[2,8,48,2176]{3,2,1,0:T(8,128)(2,1)S(1)}, bf16[2,8,48,2176]{3,2,1,0:T(8,128)(2,1)S(1)}) custom-call(s32[4]{0:T(128)S(1)} %copy-done.101, s32[32,32]{1,0:T(8,128)S(1)} %copy-done.97, bf16[256,1536]{1,0:T(8,128)(2,1)S(1)} %bitcast.193, f32[128,128]{1,0:T(8,128)S(1)} %copy-done.95, f32[128,128]{1,0:T(8,128)S(1)} %copy-done.94, ...), custom_call_target="tpu_custom_call" | custom-call | flops 1048576 | bytes 1048576 | tf_op jit(solution)/shard_map/attend_back/pallas_call | solution.py:45
  370.7 1.8 collective-permute-done.62
  373.8 4.0 fusion.24
  383.1 10.9 %expert_weights.3 = (f32[768,768]{1,0:T(8,128)}, f32[768,768]{1,0:T(8,128)}, f32[384,1536]{1,0:T(8,128)}) custom-call(s32[4]{0:T(128)S(1)} %copy-done.101, bf16[160,1536]{1,0:T(8,128)(2,1)S(1)} %copy-done.14, bf16[320,1536]{1,0:T(8,128)(2,1)S(1)} %get-tuple-element.347.refs_1_, bf16[320,1536]{1,0:T(8,128)(2,1)S(1)} %get-tuple-element.348.refs_2_, ...), custom_call_target="tpu_custom_call" | custom-call | flops 1048576 | bytes 1048576 | tf_op jit(solution)/shard_map/expert_weights/pallas_call | solution.py:45
  394.0 14.3 %collective-permute-done.69 = bf16[8,48,1536]{2,1,0:T(8,128)(2,1)} collective-permute-done((bf16[8,48,1536]{2,1,0:T(8,128)(2,1)S(1)}, bf16[8,48,1536]{2,1,0:T(8,128)(2,1)}, u32[]{:S(2)}, u32[]{:S(2)}) %collective-permute-start.69) | collective-permute-done | bytes 1179680 | tf_op jit(solution)/shard_map/ppermute | solution.py:546
  408.2 2.4 fusion.1
  412.5 1.9 fusion.2
  419.4 2.7 collective-permute-done.75
  422.2 30.4 %collective-permute-done.74 = bf16[8,48,2176]{2,1,0:T(8,128)(2,1)S(1)} collective-permute-done((bf16[8,48,2176]{2,1,0:T(8,128)(2,1)S(1)}, bf16[8,48,2176]{2,1,0:T(8,128)(2,1)S(1)}, u32[]{:S(2)}, u32[]{:S(2)}) %collective-permute-start.74) | collective-permute-done | bytes 1671200 | tf_op jit(solution)/shard_map/ppermute | solution.py:546
  453.9 2.0 fusion
  461.4 2.8 collective-permute-done.76
  469.5 2.9 collective-permute-done.77
  475.9 3.1 collective-permute-done.78
  483.8 2.3 collective-permute-done.79
  (457 shorter events, 117.9 us)
Async XLA Ops:
  7.2 20.8 %collective-permute-start.4 = (bf16[256,1536]{1,0:T(8,128)(2,1)}, bf16[256,1536]{1,0:T(8,128)(2,1)}, u32[]{:S(2)}, u32[]{:S(2)}) collective-permute-start(bf16[256,1536]{1,0:T(8,128)(2,1)} %bitcast.187), channel_id=1, source_target_pairs={{4,0},{5,1},{8,4},{9,5},{12,8},{13,9},{14,12},{15,13},{10,14},{11,... | collective-permute-start | bytes 2359304 | tf_op jit(solution)/shard_map/ppermute | solution.py:438
  8.7 20.8 %collective-permute-start.3 = (bf16[256,1536]{1,0:T(8,128)(2,1)}, bf16[256,1536]{1,0:T(8,128)(2,1)}, u32[]{:S(2)}, u32[]{:S(2)}) collective-permute-start(bf16[256,1536]{1,0:T(8,128)(2,1)} %bitcast.188), channel_id=1, source_target_pairs={{0,4},{1,5},{4,8},{5,9},{8,12},{9,13},{12,14},{13,15},{14,10},{15,... | collective-permute-start | bytes 2359304 | tf_op jit(solution)/shard_map/ppermute | solution.py:435
  15.6 26.1 %collective-permute-start.2 = (bf16[2,48,3712]{2,1,0:T(8,128)(2,1)S(1)}, bf16[2,48,3712]{2,1,0:T(8,128)(2,1)S(1)}, u32[]{:S(2)}, u32[]{:S(2)}) collective-permute-start(bf16[2,48,3712]{2,1,0:T(8,128)(2,1)S(1)} %pad_maximum_fusion.6.refs_0_), channel_id=1, source_target_pairs={{4,0},{5,1},{8,4},{9,5},{12,8},{13,9},{14,12},{15,13},{10,14},{11,... | collective-permute-start | bytes 2138120 | tf_op jit(solution)/shard_map/ppermute | solution.py:438
  17.4 25.5 %collective-permute-start.1 = (bf16[2,48,3712]{2,1,0:T(8,128)(2,1)S(1)}, bf16[2,48,3712]{2,1,0:T(8,128)(2,1)S(1)}, u32[]{:S(2)}, u32[]{:S(2)}) collective-permute-start(bf16[2,48,3712]{2,1,0:T(8,128)(2,1)S(1)} %pad_maximum_fusion.6.refs_0_), channel_id=1, source_target_pairs={{0,4},{1,5},{4,8},{5,9},{8,12},{9,13},{12,14},{13,15},{14,10},{15,... | collective-permute-start | bytes 2138120 | tf_op jit(solution)/shard_map/ppermute | solution.py:435
  19.1 55.9 %collective-permute-start.9 = (bf16[768,1536]{1,0:T(8,128)(2,1)S(1)}, bf16[768,1536]{1,0:T(8,128)(2,1)S(1)}, u32[]{:S(2)}, u32[]{:S(2)}) collective-permute-start(bf16[768,1536]{1,0:T(8,128)(2,1)S(1)} %pad_maximum_fusion.3), channel_id=1, source_target_pairs={{0,16},{16,0},{1,17},{17,1},{2,18},{18,2},{3,19},{19,3},{4,20},{20... | collective-permute-start | bytes 7077896 | tf_op jit(solution)/shard_map/ppermute | solution.py:546
  78.8 29.6 %collective-permute-start.23 = (bf16[384,1536]{1,0:T(8,128)(2,1)}, bf16[384,1536]{1,0:T(8,128)(2,1)}, u32[]{:S(2)}, u32[]{:S(2)}) collective-permute-start(bf16[384,1536]{1,0:T(8,128)(2,1)} %bitcast.13.refs_5_.refs_7_), channel_id=1, source_target_pairs={{0,16},{16,0},{1,17},{17,1},{2,18},{18,2},{3,19},{19,3},{4,20},{20... | collective-permute-start | bytes 3538952 | tf_op jit(solution)/shard_map/ppermute | solution.py:546
  89.9 19.9 %collective-permute-start.21 = (bf16[256,1536]{1,0:T(8,128)(2,1)}, bf16[256,1536]{1,0:T(8,128)(2,1)}, u32[]{:S(2)}, u32[]{:S(2)}) collective-permute-start(bf16[256,1536]{1,0:T(8,128)(2,1)} %collective-permute-done.3.refs_2_), channel_id=1, source_target_pairs={{0,4},{1,5},{4,8},{5,9},{8,12},{9,13},{12,14},{13,15},{14,10},{15,... | collective-permute-start | bytes 2359304 | tf_op jit(solution)/shard_map/ppermute | solution.py:435
  90.8 19.6 %collective-permute-start.22 = (bf16[256,1536]{1,0:T(8,128)(2,1)}, bf16[256,1536]{1,0:T(8,128)(2,1)}, u32[]{:S(2)}, u32[]{:S(2)}) collective-permute-start(bf16[256,1536]{1,0:T(8,128)(2,1)} %collective-permute-done.4.refs_4_), channel_id=1, source_target_pairs={{4,0},{5,1},{8,4},{9,5},{12,8},{13,9},{14,12},{15,13},{10,14},{11,... | collective-permute-start | bytes 2359304 | tf_op jit(solution)/shard_map/ppermute | solution.py:438
  110.4 38.7 %collective-permute-start.28 = (bf16[528,1536]{1,0:T(8,128)(2,1)S(1)}, bf16[528,1536]{1,0:T(8,128)(2,1)S(1)}, u32[]{:S(2)}, u32[]{:S(2)}) collective-permute-start(bf16[528,1536]{1,0:T(8,128)(2,1)S(1)} %pad_maximum_fusion.4), channel_id=1, source_target_pairs={{0,1},{1,0},{2,3},{3,2},{4,5},{5,4},{6,7},{7,6},{8,9},{9,8},{10,11... | collective-permute-start | bytes 4866056 | tf_op jit(solution)/shard_map/ppermute | solution.py:441
  110.4 21.4 %collective-permute-start.25 = (bf16[272,1536]{1,0:T(8,128)(2,1)S(1)}, bf16[272,1536]{1,0:T(8,128)(2,1)S(1)}, u32[]{:S(2)}, u32[]{:S(2)}) collective-permute-start(bf16[272,1536]{1,0:T(8,128)(2,1)S(1)} %copy-done.10), channel_id=1, source_target_pairs={{4,0},{5,1},{8,4},{9,5},{12,8},{13,9},{14,12},{15,13},{10,14},{11,... | collective-permute-start | bytes 2506760 | tf_op jit(solution)/shard_map/ppermute | solution.py:438
  111.6 21.4 %collective-permute-start.24 = (bf16[272,1536]{1,0:T(8,128)(2,1)S(1)}, bf16[272,1536]{1,0:T(8,128)(2,1)S(1)}, u32[]{:S(2)}, u32[]{:S(2)}) collective-permute-start(bf16[272,1536]{1,0:T(8,128)(2,1)S(1)} %copy-done.10), channel_id=1, source_target_pairs={{0,4},{1,5},{4,8},{5,9},{8,12},{9,13},{12,14},{13,15},{14,10},{15,... | collective-permute-start | bytes 2506760 | tf_op jit(solution)/shard_map/ppermute | solution.py:435
  112.5 36.7 %collective-permute-start.26 = (bf16[256,1536]{1,0:T(8,128)(2,1)}, bf16[256,1536]{1,0:T(8,128)(2,1)S(1)}, u32[]{:S(2)}, u32[]{:S(2)}) collective-permute-start(bf16[256,1536]{1,0:T(8,128)(2,1)} %collective-permute-done.21.refs_2_), channel_id=1, source_target_pairs={{0,4},{1,5},{4,8},{5,9},{8,12},{9,13},{12,14},{13,15},{14,10},{15,... | collective-permute-start | bytes 2359304 | tf_op jit(solution)/shard_map/ppermute | solution.py:435
  114.1 35.1 %collective-permute-start.27 = (bf16[256,1536]{1,0:T(8,128)(2,1)}, bf16[256,1536]{1,0:T(8,128)(2,1)S(1)}, u32[]{:S(2)}, u32[]{:S(2)}) collective-permute-start(bf16[256,1536]{1,0:T(8,128)(2,1)} %collective-permute-done.22.refs_4_), channel_id=1, source_target_pairs={{4,0},{5,1},{8,4},{9,5},{12,8},{13,9},{14,12},{15,13},{10,14},{11,... | collective-permute-start | bytes 2359304 | tf_op jit(solution)/shard_map/ppermute | solution.py:438
  149.2 30.1 %collective-permute-start.33 = (bf16[1056,1536]{1,0:T(8,128)(2,1)}, bf16[1056,1536]{1,0:T(8,128)(2,1)S(1)}, u32[]{:S(2)}, u32[]{:S(2)}) collective-permute-start(bf16[1056,1536]{1,0:T(8,128)(2,1)} %pad_maximum_fusion), channel_id=1, source_target_pairs={{0,1},{1,0},{2,3},{3,2},{4,5},{5,4},{6,7},{7,6},{8,9},{9,8},{10,11... | collective-permute-start | bytes 9732104 | tf_op jit(solution)/shard_map/ppermute | solution.py:441
  149.2 21.4 %collective-permute-start.29 = (bf16[272,1536]{1,0:T(8,128)(2,1)S(1)}, bf16[272,1536]{1,0:T(8,128)(2,1)S(1)}, u32[]{:S(2)}, u32[]{:S(2)}) collective-permute-start(bf16[272,1536]{1,0:T(8,128)(2,1)S(1)} %collective-permute-done.24.refs_1_), channel_id=1, source_target_pairs={{0,4},{1,5},{4,8},{5,9},{8,12},{9,13},{12,14},{13,15},{14,10},{15,... | collective-permute-start | bytes 2506760 | tf_op jit(solution)/shard_map/ppermute | solution.py:435
  150.1 21.4 %collective-permute-start.30 = (bf16[272,1536]{1,0:T(8,128)(2,1)S(1)}, bf16[272,1536]{1,0:T(8,128)(2,1)S(1)}, u32[]{:S(2)}, u32[]{:S(2)}) collective-permute-start(bf16[272,1536]{1,0:T(8,128)(2,1)S(1)} %collective-permute-done.25.refs_3_), channel_id=1, source_target_pairs={{4,0},{5,1},{8,4},{9,5},{12,8},{13,9},{14,12},{15,13},{10,14},{11,... | collective-permute-start | bytes 2506760 | tf_op jit(solution)/shard_map/ppermute | solution.py:438
  151.3 27.9 %collective-permute-start.32 = (bf16[128,1536]{1,0:T(8,128)(2,1)S(1)}, bf16[128,1536]{1,0:T(8,128)(2,1)S(1)}, u32[]{:S(2)}, u32[]{:S(2)}) collective-permute-start(bf16[128,1536]{1,0:T(8,128)(2,1)S(1)} %slice.159), channel_id=1, source_target_pairs={{4,0},{5,1},{8,4},{9,5},{12,8},{13,9},{14,12},{15,13},{10,14},{11,... | collective-permute-start | bytes 1179656 | tf_op jit(solution)/shard_map/ppermute | solution.py:438
  153.0 26.3 %collective-permute-start.31 = (bf16[128,1536]{1,0:T(8,128)(2,1)S(1)}, bf16[128,1536]{1,0:T(8,128)(2,1)S(1)}, u32[]{:S(2)}, u32[]{:S(2)}) collective-permute-start(bf16[128,1536]{1,0:T(8,128)(2,1)S(1)} %slice.158), channel_id=1, source_target_pairs={{0,4},{1,5},{4,8},{5,9},{8,12},{9,13},{12,14},{13,15},{14,10},{15,... | collective-permute-start | bytes 1179656 | tf_op jit(solution)/shard_map/ppermute | solution.py:435
  179.2 24.4 %collective-permute-start.36 = (bf16[1056,1536]{1,0:T(8,128)(2,1)}, bf16[1056,1536]{1,0:T(8,128)(2,1)}, u32[]{:S(2)}, u32[]{:S(2)}) collective-permute-start(bf16[1056,1536]{1,0:T(8,128)(2,1)} %pad_maximum_fusion.1), channel_id=1, source_target_pairs={{0,1},{1,0},{2,3},{3,2},{4,5},{5,4},{6,7},{7,6},{8,9},{9,8},{10,11... | collective-permute-start | bytes 9732104 | tf_op jit(solution)/shard_map/ppermute | solution.py:441
  179.3 21.0 %collective-permute-start.34 = (bf16[272,1536]{1,0:T(8,128)(2,1)S(1)}, bf16[272,1536]{1,0:T(8,128)(2,1)S(1)}, u32[]{:S(2)}, u32[]{:S(2)}) collective-permute-start(bf16[272,1536]{1,0:T(8,128)(2,1)S(1)} %collective-permute-done.29.refs_1_), channel_id=1, source_target_pairs={{0,4},{1,5},{4,8},{5,9},{8,12},{9,13},{12,14},{13,15},{14,10},{15,... | collective-permute-start | bytes 2506760 | tf_op jit(solution)/shard_map/ppermute | solution.py:435
  181.1 20.6 %collective-permute-start.35 = (bf16[272,1536]{1,0:T(8,128)(2,1)S(1)}, bf16[272,1536]{1,0:T(8,128)(2,1)S(1)}, u32[]{:S(2)}, u32[]{:S(2)}) collective-permute-start(bf16[272,1536]{1,0:T(8,128)(2,1)S(1)} %collective-permute-done.30.refs_3_), channel_id=1, source_target_pairs={{4,0},{5,1},{8,4},{9,5},{12,8},{13,9},{14,12},{15,13},{10,14},{11,... | collective-permute-start | bytes 2506760 | tf_op jit(solution)/shard_map/ppermute | solution.py:438
  203.6 18.3 %collective-permute-start.39 = (bf16[1056,1536]{1,0:T(8,128)(2,1)}, bf16[1056,1536]{1,0:T(8,128)(2,1)}, u32[]{:S(2)}, u32[]{:S(2)}) collective-permute-start(bf16[1056,1536]{1,0:T(8,128)(2,1)} %pad_maximum_fusion.2), channel_id=1, source_target_pairs={{0,1},{1,0},{2,3},{3,2},{4,5},{5,4},{6,7},{7,6},{8,9},{9,8},{10,11... | collective-permute-start | bytes 9732104 | tf_op jit(solution)/shard_map/ppermute | solution.py:441
  257.6 21.5 %collective-permute-start.45 = (bf16[2,272,1536]{2,1,0:T(8,128)(2,1)}, bf16[2,272,1536]{2,1,0:T(8,128)(2,1)S(1)}, u32[]{:S(2)}, u32[]{:S(2)}) collective-permute-start(bf16[2,272,1536]{2,1,0:T(8,128)(2,1)} %get-tuple-element.343), channel_id=1, source_target_pairs={{0,1},{1,0},{2,3},{3,2},{4,5},{5,4},{6,7},{7,6},{8,9},{9,8},{10,11... | collective-permute-start | bytes 5013512 | tf_op jit(solution)/shard_map/ppermute | solution.py:441
  257.8 20.9 %collective-permute-start.47 = (bf16[272,1536]{1,0:T(8,128)(2,1)S(1)}, bf16[272,1536]{1,0:T(8,128)(2,1)S(1)}, u32[]{:S(2)}, u32[]{:S(2)}) collective-permute-start(bf16[272,1536]{1,0:T(8,128)(2,1)S(1)} %get-tuple-element.470), channel_id=1, source_target_pairs={{4,0},{5,1},{8,4},{9,5},{12,8},{13,9},{14,12},{15,13},{10,14},{11,... | collective-permute-start | bytes 2506760 | tf_op jit(solution)/shard_map/ppermute | solution.py:438
  258.3 20.8 %collective-permute-start.46 = (bf16[272,1536]{1,0:T(8,128)(2,1)S(1)}, bf16[272,1536]{1,0:T(8,128)(2,1)S(1)}, u32[]{:S(2)}, u32[]{:S(2)}) collective-permute-start(bf16[272,1536]{1,0:T(8,128)(2,1)S(1)} %get-tuple-element.471), channel_id=1, source_target_pairs={{0,4},{1,5},{4,8},{5,9},{8,12},{9,13},{12,14},{13,15},{14,10},{15,... | collective-permute-start | bytes 2506760 | tf_op jit(solution)/shard_map/ppermute | solution.py:435
  280.5 22.3 %collective-permute-start.48 = (bf16[2,272,1536]{2,1,0:T(8,128)(2,1)S(1)}, bf16[2,272,1536]{2,1,0:T(8,128)(2,1)S(1)}, u32[]{:S(2)}, u32[]{:S(2)}) collective-permute-start(bf16[2,272,1536]{2,1,0:T(8,128)(2,1)S(1)} %copy-done.104), channel_id=1, source_target_pairs={{0,1},{1,0},{2,3},{3,2},{4,5},{5,4},{6,7},{7,6},{8,9},{9,8},{10,11... | collective-permute-start | bytes 5013512 | tf_op jit(solution)/shard_map/ppermute | solution.py:441
  280.5 21.0 %collective-permute-start.49 = (bf16[272,1536]{1,0:T(8,128)(2,1)S(1)}, bf16[272,1536]{1,0:T(8,128)(2,1)S(1)}, u32[]{:S(2)}, u32[]{:S(2)}) collective-permute-start(bf16[272,1536]{1,0:T(8,128)(2,1)S(1)} %get-tuple-element.372), channel_id=1, source_target_pairs={{0,4},{1,5},{4,8},{5,9},{8,12},{9,13},{12,14},{13,15},{14,10},{15,... | collective-permute-start | bytes 2506760 | tf_op jit(solution)/shard_map/ppermute | solution.py:435
  282.1 20.7 %collective-permute-start.50 = (bf16[272,1536]{1,0:T(8,128)(2,1)S(1)}, bf16[272,1536]{1,0:T(8,128)(2,1)S(1)}, u32[]{:S(2)}, u32[]{:S(2)}) collective-permute-start(bf16[272,1536]{1,0:T(8,128)(2,1)S(1)} %get-tuple-element.373), channel_id=1, source_target_pairs={{4,0},{5,1},{8,4},{9,5},{12,8},{13,9},{14,12},{15,13},{10,14},{11,... | collective-permute-start | bytes 2506760 | tf_op jit(solution)/shard_map/ppermute | solution.py:438
  282.6 21.5 %collective-permute-start.51 = (bf16[288,1536]{1,0:T(8,128)(2,1)S(1)}, bf16[288,1536]{1,0:T(8,128)(2,1)S(1)}, u32[]{:S(2)}, u32[]{:S(2)}) collective-permute-start(bf16[288,1536]{1,0:T(8,128)(2,1)S(1)} %get-tuple-element.371), channel_id=1, source_target_pairs={{0,16},{16,0},{1,17},{17,1},{2,18},{18,2},{3,19},{19,3},{4,20},{20... | collective-permute-start | bytes 2654216 | tf_op jit(solution)/shard_map/ppermute | solution.py:546
  304.1 22.1 %collective-permute-start.55 = (bf16[288,1536]{1,0:T(8,128)(2,1)S(1)}, bf16[288,1536]{1,0:T(8,128)(2,1)S(1)}, u32[]{:S(2)}, u32[]{:S(2)}) collective-permute-start(bf16[288,1536]{1,0:T(8,128)(2,1)S(1)} %get-tuple-element.380), channel_id=1, source_target_pairs={{0,16},{16,0},{1,17},{17,1},{2,18},{18,2},{3,19},{19,3},{4,20},{20... | collective-permute-start | bytes 2654216 | tf_op jit(solution)/shard_map/ppermute | solution.py:546
  304.6 22.4 %collective-permute-start.53 = (bf16[272,1536]{1,0:T(8,128)(2,1)S(1)}, bf16[272,1536]{1,0:T(8,128)(2,1)S(1)}, u32[]{:S(2)}, u32[]{:S(2)}) collective-permute-start(bf16[272,1536]{1,0:T(8,128)(2,1)S(1)} %get-tuple-element.376), channel_id=1, source_target_pairs={{0,4},{1,5},{4,8},{5,9},{8,12},{9,13},{12,14},{13,15},{14,10},{15,... | collective-permute-start | bytes 2506760 | tf_op jit(solution)/shard_map/ppermute | solution.py:435
  306.2 20.9 %collective-permute-start.54 = (bf16[272,1536]{1,0:T(8,128)(2,1)S(1)}, bf16[272,1536]{1,0:T(8,128)(2,1)S(1)}, u32[]{:S(2)}, u32[]{:S(2)}) collective-permute-start(bf16[272,1536]{1,0:T(8,128)(2,1)S(1)} %get-tuple-element.377), channel_id=1, source_target_pairs={{4,0},{5,1},{8,4},{9,5},{12,8},{13,9},{14,12},{15,13},{10,14},{11,... | collective-permute-start | bytes 2506760 | tf_op jit(solution)/shard_map/ppermute | solution.py:438
  330.0 21.3 %collective-permute-start.60 = (bf16[288,1536]{1,0:T(8,128)(2,1)}, bf16[288,1536]{1,0:T(8,128)(2,1)S(1)}, u32[]{:S(2)}, u32[]{:S(2)}) collective-permute-start(bf16[288,1536]{1,0:T(8,128)(2,1)} %get-tuple-element.396), channel_id=1, source_target_pairs={{0,16},{16,0},{1,17},{17,1},{2,18},{18,2},{3,19},{19,3},{4,20},{20... | collective-permute-start | bytes 2654216 | tf_op jit(solution)/shard_map/ppermute | solution.py:546
  352.2 25.6 %collective-permute-start.65 = (bf16[2,8,48,1536]{3,2,1,0:T(8,128)(2,1)}, bf16[2,8,48,1536]{3,2,1,0:T(8,128)(2,1)}, u32[]{:S(2)}, u32[]{:S(2)}) collective-permute-start(bf16[2,8,48,1536]{3,2,1,0:T(8,128)(2,1)} %get-tuple-element.414), channel_id=1, source_target_pairs={{0,1},{1,0},{2,3},{3,2},{4,5},{5,4},{6,7},{7,6},{8,9},{9,8},{10,11... | collective-permute-start | bytes 7077896 | tf_op jit(solution)/shard_map/ppermute | solution.py:441
  352.2 21.5 %collective-permute-start.61 = (bf16[2,256,1536]{2,1,0:T(8,128)(2,1)}, bf16[2,256,1536]{2,1,0:T(8,128)(2,1)}, u32[]{:S(2)}, u32[]{:S(2)}) collective-permute-start(bf16[2,256,1536]{2,1,0:T(8,128)(2,1)} %get-tuple-element.399), channel_id=1, source_target_pairs={{0,1},{1,0},{2,3},{3,2},{4,5},{5,4},{6,7},{7,6},{8,9},{9,8},{10,11... | collective-permute-start | bytes 4718600 | tf_op jit(solution)/shard_map/ppermute | solution.py:441
  352.7 19.8 %collective-permute-start.62 = (bf16[256,1536]{1,0:T(8,128)(2,1)}, bf16[256,1536]{1,0:T(8,128)(2,1)}, u32[]{:S(2)}, u32[]{:S(2)}) collective-permute-start(bf16[256,1536]{1,0:T(8,128)(2,1)} %get-tuple-element.397), channel_id=1, source_target_pairs={{0,4},{1,5},{4,8},{5,9},{8,12},{9,13},{12,14},{13,15},{14,10},{15,... | collective-permute-start | bytes 2359304 | tf_op jit(solution)/shard_map/ppermute | solution.py:435
  354.2 19.5 %collective-permute-start.63 = (bf16[256,1536]{1,0:T(8,128)(2,1)}, bf16[256,1536]{1,0:T(8,128)(2,1)}, u32[]{:S(2)}, u32[]{:S(2)}) collective-permute-start(bf16[256,1536]{1,0:T(8,128)(2,1)} %get-tuple-element.398), channel_id=1, source_target_pairs={{4,0},{5,1},{8,4},{9,5},{12,8},{13,9},{14,12},{15,13},{10,14},{11,... | collective-permute-start | bytes 2359304 | tf_op jit(solution)/shard_map/ppermute | solution.py:438
  354.7 23.1 %collective-permute-start.64 = (bf16[288,1536]{1,0:T(8,128)(2,1)}, bf16[288,1536]{1,0:T(8,128)(2,1)S(1)}, u32[]{:S(2)}, u32[]{:S(2)}) collective-permute-start(bf16[288,1536]{1,0:T(8,128)(2,1)} %get-tuple-element.412), channel_id=1, source_target_pairs={{0,16},{16,0},{1,17},{17,1},{2,18},{18,2},{3,19},{19,3},{4,20},{20... | collective-permute-start | bytes 2654216 | tf_op jit(solution)/shard_map/ppermute | solution.py:546
  377.8 34.6 %collective-permute-start.70 = (bf16[2,8,48,2176]{3,2,1,0:T(8,128)(2,1)}, bf16[2,8,48,2176]{3,2,1,0:T(8,128)(2,1)}, u32[]{:S(2)}, u32[]{:S(2)}) collective-permute-start(bf16[2,8,48,2176]{3,2,1,0:T(8,128)(2,1)} %copy-done.102), channel_id=1, source_target_pairs={{0,1},{1,0},{2,3},{3,2},{4,5},{5,4},{6,7},{7,6},{8,9},{9,8},{10,11... | collective-permute-start | bytes 10027016 | tf_op jit(solution)/shard_map/ppermute | solution.py:441
  379.7 28.5 %collective-permute-start.69 = (bf16[8,48,1536]{2,1,0:T(8,128)(2,1)S(1)}, bf16[8,48,1536]{2,1,0:T(8,128)(2,1)}, u32[]{:S(2)}, u32[]{:S(2)}) collective-permute-start(bf16[8,48,1536]{2,1,0:T(8,128)(2,1)S(1)} %fusion.32), channel_id=1, source_target_pairs={{0,16},{16,0},{1,17},{17,1},{2,18},{18,2},{3,19},{19,3},{4,20},{20... | collective-permute-start | bytes 3538952 | tf_op jit(solution)/shard_map/ppermute | solution.py:546
  380.6 30.1 %collective-permute-start.66 = (bf16[2,256,1536]{2,1,0:T(8,128)(2,1)S(1)}, bf16[2,256,1536]{2,1,0:T(8,128)(2,1)S(1)}, u32[]{:S(2)}, u32[]{:S(2)}) collective-permute-start(bf16[2,256,1536]{2,1,0:T(8,128)(2,1)S(1)} %copy-done.106), channel_id=1, source_target_pairs={{0,1},{1,0},{2,3},{3,2},{4,5},{5,4},{6,7},{7,6},{8,9},{9,8},{10,11... | collective-permute-start | bytes 4718600 | tf_op jit(solution)/shard_map/ppermute | solution.py:441
  380.8 29.9 %collective-permute-start.67 = (bf16[256,1536]{1,0:T(8,128)(2,1)}, bf16[256,1536]{1,0:T(8,128)(2,1)S(1)}, u32[]{:S(2)}, u32[]{:S(2)}) collective-permute-start(bf16[256,1536]{1,0:T(8,128)(2,1)} %get-tuple-element.415), channel_id=1, source_target_pairs={{0,4},{1,5},{4,8},{5,9},{8,12},{9,13},{12,14},{13,15},{14,10},{15,... | collective-permute-start | bytes 2359304 | tf_op jit(solution)/shard_map/ppermute | solution.py:435
  382.1 28.6 %collective-permute-start.68 = (bf16[256,1536]{1,0:T(8,128)(2,1)}, bf16[256,1536]{1,0:T(8,128)(2,1)}, u32[]{:S(2)}, u32[]{:S(2)}) collective-permute-start(bf16[256,1536]{1,0:T(8,128)(2,1)} %get-tuple-element.416), channel_id=1, source_target_pairs={{4,0},{5,1},{8,4},{9,5},{12,8},{13,9},{14,12},{15,13},{10,14},{11,... | collective-permute-start | bytes 2359304 | tf_op jit(solution)/shard_map/ppermute | solution.py:438
  414.4 38.2 %collective-permute-start.74 = (bf16[8,48,2176]{2,1,0:T(8,128)(2,1)S(1)}, bf16[8,48,2176]{2,1,0:T(8,128)(2,1)S(1)}, u32[]{:S(2)}, u32[]{:S(2)}) collective-permute-start(bf16[8,48,2176]{2,1,0:T(8,128)(2,1)S(1)} %fusion.2), channel_id=1, source_target_pairs={{0,16},{16,0},{1,17},{17,1},{2,18},{18,2},{3,19},{19,3},{4,20},{20... | collective-permute-start | bytes 5013512 | tf_op jit(solution)/shard_map/ppermute | solution.py:546
  416.6 40.8 %collective-permute-start.86 = (bf16[48,1536]{1,0:T(8,128)(2,1)S(1)}, bf16[48,1536]{1,0:T(8,128)(2,1)S(1)}, u32[]{:S(2)}, u32[]{:S(2)}) collective-permute-start(bf16[48,1536]{1,0:T(8,128)(2,1)S(1)} %get-tuple-element.482), channel_id=1, source_target_pairs={{4,0},{5,1},{8,4},{9,5},{12,8},{13,9},{14,12},{15,13},{10,14},{11,... | collective-permute-start | bytes 442376 | tf_op jit(solution)/shard_map/ppermute | solution.py:438
  417.4 38.7 %collective-permute-start.72 = (bf16[256,1536]{1,0:T(8,128)(2,1)S(1)}, bf16[256,1536]{1,0:T(8,128)(2,1)S(1)}, u32[]{:S(2)}, u32[]{:S(2)}) collective-permute-start(bf16[256,1536]{1,0:T(8,128)(2,1)S(1)} %get-tuple-element.425), channel_id=1, source_target_pairs={{0,4},{1,5},{4,8},{5,9},{8,12},{9,13},{12,14},{13,15},{14,10},{15,... | collective-permute-start | bytes 2359304 | tf_op jit(solution)/shard_map/ppermute | solution.py:435
  418.7 37.4 %collective-permute-start.73 = (bf16[256,1536]{1,0:T(8,128)(2,1)S(1)}, bf16[256,1536]{1,0:T(8,128)(2,1)S(1)}, u32[]{:S(2)}, u32[]{:S(2)}) collective-permute-start(bf16[256,1536]{1,0:T(8,128)(2,1)S(1)} %get-tuple-element.426), channel_id=1, source_target_pairs={{4,0},{5,1},{8,4},{9,5},{12,8},{13,9},{14,12},{15,13},{10,14},{11,... | collective-permute-start | bytes 2359304 | tf_op jit(solution)/shard_map/ppermute | solution.py:438
  422.1 60.2 %collective-permute-start.71 = (bf16[1,256,1536]{2,1,0:T(8,128)(2,1)S(1)}, bf16[1,256,1536]{2,1,0:T(8,128)(2,1)S(1)}, u32[]{:S(2)}, u32[]{:S(2)}) collective-permute-start(bf16[1,256,1536]{2,1,0:T(8,128)(2,1)S(1)} %copy-done.110), channel_id=1, source_target_pairs={{0,1},{1,0},{2,3},{3,2},{4,5},{5,4},{6,7},{7,6},{8,9},{9,8},{10,11... | collective-permute-start | bytes 2359304 | tf_op jit(solution)/shard_map/ppermute | solution.py:441
  (174 other events, 2065.8 us)

commit v4 on v3

--- a/solution.py
+++ b/solution.py
@@ -19,7 +19,7 @@
 MISC = Q_COLS + 2 * KV_COLS
 EXTRA = 16
 LANES = 128
-CHUNKS = 4
+CHUNKS = (9, 9, 7, 11)
 EPSILON = 1e-06
 ROPE_BASE = 10000.0
 MASKED = -1e30
@@ -281,6 +281,14 @@
         dx_refs[i][tokens:] = jnp.concatenate(parts, axis=1).astype(bf16)
 
 
+def chunk_edges(rows):
+    unit, at, edges = rows // sum(CHUNKS), 0, []
+    for c in CHUNKS:
+        edges.append((at, at + c * unit))
+        at += c * unit
+    return edges
+
+
 def weights_body(n, half, shift, adds, me_ref, *refs):
     lists = [refs[k * n : (k + 1) * n] for k in range(5)]
     xs, dys, acts, dus, dws = lists
@@ -300,17 +308,17 @@
     hidden = totals[0].shape[1]
     columns = (slice(0, hidden), slice(hidden, 2 * hidden), slice(None))
     chunks = outs if shift else more
-    rows = (wide + narrow) // CHUNKS
+    edges = chunk_edges(wide + narrow)
     for k, c in enumerate(columns):
         base, size = (wide, narrow) if k == 2 else (0, wide)
         for j, ref in enumerate(chunks):
-            first = (j % CHUNKS) * rows
-            lo, hi = max(first, base), min(first + rows, base + size)
+            first, end = edges[j % len(CHUNKS)]
+            lo, hi = max(first, base), min(end, base + size)
             if lo < hi and shift:
                 ref[lo - first : hi - first, c] = totals[k][lo - base : hi - base].astype(bf16)
-            elif lo < hi and j < CHUNKS:
+            elif lo < hi and j < len(CHUNKS):
                 value = totals[k][lo - base : hi - base]
-                for other in chunks[j::CHUNKS]:
+                for other in chunks[j :: len(CHUNKS)]:
                     value = value + other[lo - first : hi - first, c].astype(f32)
                 outs[k][lo - base : hi - base] = value
 
@@ -594,7 +602,7 @@
         table = jnp.asarray(ring.table(dp))
         far = from_dp(dense_own, 1)
         d_ring = ring.gather(jnp.stack([dense_own, far]), 1)
-        d_ring.hop()
+        d_ring.hop(g_ring.got[-1], g_ring.got[1])
         expert_start = (far,)
     else:
         table = jnp.zeros((dp * experts, 1), jnp.int32)
@@ -739,7 +747,9 @@
 
         more = []
         for shift in range(1, dp):
-            parts = part(shift, [sds(((wide + narrow) // CHUNKS, WIDTH), bf16)] * CHUNKS, [], *dx_ring.sent, *more)
+            parts = part(
+                shift, [sds((end - at, WIDTH), bf16) for at, end in chunk_edges(wide + narrow)], [], *dx_ring.sent, *more
+            )
             for p in parts:
                 more.append(from_dp(after(p, *more[-1:]), shift))
         weights_sent = (parts[0],)

time: 498 us -> 495 us (level)
    ppermute x26, waiting for transfers between devices: 66.6 us -> 58.6 us  [send_down(): return lax.ppermute(x, 'expert', self.down)]
    ppermute x26, starting transfers between devices: 24.3 us -> 18.2 us  [send_down(): return lax.ppermute(x, 'expert', self.down)]
    ppermute x28, starting transfers between devices: 34.6 us -> 40.7 us  [send_up(): return lax.ppermute(x, 'expert', self.up)]
    ppermute x28, waiting for transfers between devices: 96.6 us -> 102 us  [send_up(): return lax.ppermute(x, 'expert', self.up)]
    unnamed x269 -> x275, local copies, waits for them, and re-layouts: 14.4 us -> 14.3 us
  transfers between devices with their start and end apart: 89 -> 89, of which waited for: 49 -> 51; matrix products, arithmetic and copies ran while one was open for 7% -> 7% of each run, Pallas kernels for 21% -> 21%
where the time goes in v4:
time: 495 us; the launch traced here: 488 us
  waiting for transfers between devices  249 us (50%)
  Pallas kernels  108 us (22%)
  starting transfers between devices  72.4 us (15%)
  other arithmetic  35.8 us (7%)
  local copies, waits for them, and re-layouts  20.1 us (4%)
    pallas_call x10, Pallas kernels, call(): pl.pallas_call(body, out_shape=outs, in_specs=ins, out_specs=vmem(len(out...  108 us
    ppermute x28, waiting for transfers between devices, send_up(): return lax.ppermute(x, 'expert', self.up)  102 us
    ppermute x9, waiting for transfers between devices, from_dp(): return lax.ppermute(x, 'dp', dp_pairs(shift))  77.7 us
    ppermute x26, waiting for transfers between devices, send_down(): return lax.ppermute(x, 'expert', self.down)  58.6 us
    ppermute x28, starting transfers between devices, send_up(): return lax.ppermute(x, 'expert', self.up)  40.7 us
    convert_element_type x19, other arithmetic, total(): return out.astype(bf16)  21.4 us
    ppermute x26, starting transfers between devices, send_down(): return lax.ppermute(x, 'expert', self.down)  18.2 us
    unnamed x275, local copies, waits for them, and re-layouts  14.3 us
  transfers between devices with their start and end apart: 89, of which 51 were waited for; matrix products, arithmetic and copies ran while one was open for 7% of the time, Pallas kernels for 21%

profile of v4, /device:TPU:0, one launch (start us, length us, event | category | flops | bytes accessed | tf_op | source)
XLA Modules:
  0.0 487.6 jit_solution(13748314665988939439)
XLA Ops:
  4.1 3.0 collective-permute-start
  10.9 4.5 collective-permute-done
  18.2 8.2 %collective-permute-done.2.refs_4_ = bf16[256,1536]{1,0:T(8,128)(2,1)} collective-permute-done((bf16[256,1536]{1,0:T(8,128)(2,1)}, bf16[256,1536]{1,0:T(8,128)(2,1)}, u32[]{:S(2)}, u32[]{:S(2)}) %collective-permute-start.2) | collective-permute-done | bytes 786464 | tf_op jit(solution)/shard_map/ppermute | solution.py:446
  29.6 14.2 %collective-permute-done.3.refs_2_ = bf16[2,48,3712]{2,1,0:T(8,128)(2,1)S(1)} collective-permute-done((bf16[2,48,3712]{2,1,0:T(8,128)(2,1)S(1)}, bf16[2,48,3712]{2,1,0:T(8,128)(2,1)S(1)}, u32[]{:S(2)}, u32[]{:S(2)}) %collective-permute-start.3) | collective-permute-done | bytes 712736 | tf_op jit(solution)/shard_map/ppermute | solution.py:443
  46.3 14.1 %collective-permute-done.5.refs_6_ = bf16[2,48,3712]{2,1,0:T(8,128)(2,1)S(1)} collective-permute-done((bf16[2,48,3712]{2,1,0:T(8,128)(2,1)S(1)}, bf16[2,48,3712]{2,1,0:T(8,128)(2,1)S(1)}, u32[]{:S(2)}, u32[]{:S(2)}) %collective-permute-start.5) | collective-permute-done | bytes 712736 | tf_op jit(solution)/shard_map/ppermute | solution.py:443
  62.9 5.1 %collective-permute-done.9.refs_6_.refs_8_ = bf16[768,1536]{1,0:T(8,128)(2,1)S(1)} collective-permute-done((bf16[768,1536]{1,0:T(8,128)(2,1)S(1)}, bf16[768,1536]{1,0:T(8,128)(2,1)S(1)}, u32[]{:S(2)}, u32[]{:S(2)}) %collective-permute-start.9) | collective-permute-done | bytes 2359328 | tf_op jit(solution)/shard_map/ppermute | solution.py:554
  68.0 6.7 %collective-permute-done.6.refs_10_ = bf16[2,48,3712]{2,1,0:T(8,128)(2,1)S(1)} collective-permute-done((bf16[2,48,3712]{2,1,0:T(8,128)(2,1)S(1)}, bf16[2,48,3712]{2,1,0:T(8,128)(2,1)S(1)}, u32[]{:S(2)}, u32[]{:S(2)}) %collective-permute-start.6) | collective-permute-done | bytes 712736 | tf_op jit(solution)/shard_map/ppermute | solution.py:443
  79.2 7.6 %collective-permute-done.11.refs_15_ = bf16[1,48,3712]{2,1,0:T(8,128)(2,1)S(1)} collective-permute-done((bf16[1,48,3712]{2,1,0:T(8,128)(2,1)S(1)}, bf16[1,48,3712]{2,1,0:T(8,128)(2,1)S(1)}, u32[]{:S(2)}, u32[]{:S(2)}) %collective-permute-start.11) | collective-permute-done | bytes 356384 | tf_op jit(solution)/shard_map/ppermute | solution.py:446
  92.7 13.3 %forward.1 = (bf16[1536,2048]{1,0:T(8,128)(2,1)}, bf16[1536,1536]{1,0:T(8,128)(2,1)}, bf16[1536,128]{1,0:T(8,128)(2,1)}, f32[8,1536]{1,0:T(8,128)}, bf16[256,153...) custom-call(s32[4]{0:T(128)} %pad_add_fusion.me_ref, ...), custom_call_target="tpu_custom_call" | custom-call | flops 1048576 | bytes 1048576 | tf_op jit(solution)/shard_map/forward/pallas_call | solution.py:45
  114.4 17.3 %collective-permute-done.25.refs_3_ = bf16[272,1536]{1,0:T(8,128)(2,1)S(1)} collective-permute-done((bf16[272,1536]{1,0:T(8,128)(2,1)S(1)}, bf16[272,1536]{1,0:T(8,128)(2,1)S(1)}, u32[]{:S(2)}, u32[]{:S(2)}) %collective-permute-start.25) | collective-permute-done | bytes 835616 | tf_op jit(solution)/shard_map/ppermute | solution.py:446
  132.3 3.3 pad_maximum_fusion
  135.6 12.8 %collective-permute-done.26.refs_2_ = bf16[256,1536]{1,0:T(8,128)(2,1)S(1)} collective-permute-done((bf16[256,1536]{1,0:T(8,128)(2,1)}, bf16[256,1536]{1,0:T(8,128)(2,1)S(1)}, u32[]{:S(2)}, u32[]{:S(2)}) %collective-permute-start.26) | collective-permute-done | bytes 786464 | tf_op jit(solution)/shard_map/ppermute | solution.py:443
  152.9 7.0 %experts.5 = (bf16[256,1536]{1,0:T(8,128)(2,1)S(1)}, bf16[272,1536]{1,0:T(8,128)(2,1)S(1)}, bf16[1,256,1536]{2,1,0:T(8,128)(2,1)S(1)}, bf16[1,272,1536]{2,1,0:T(...) custom-call(s32[4]{0:T(128)S(1)} %copy-done.104, ...), custom_call_target="tpu_custom_call" | custom-call | flops 1048576 | bytes 1048576 | tf_op jit(solution)/shard_map/experts/pallas_call | solution.py:45
  160.9 9.0 %collective-permute-done.29.refs_1_ = bf16[272,1536]{1,0:T(8,128)(2,1)S(1)} collective-permute-done((bf16[272,1536]{1,0:T(8,128)(2,1)S(1)}, bf16[272,1536]{1,0:T(8,128)(2,1)S(1)}, u32[]{:S(2)}, u32[]{:S(2)}) %collective-permute-start.29) | collective-permute-done | bytes 835616 | tf_op jit(solution)/shard_map/ppermute | solution.py:443
  171.5 3.2 pad_maximum_fusion.1
  174.8 4.4 collective-permute-done.32.refs_4_
  181.5 13.7 %experts.6 = (bf16[256,1536]{1,0:T(8,128)(2,1)S(1)}, bf16[256,1536]{1,0:T(8,128)(2,1)S(1)}, bf16[272,1536]{1,0:T(8,128)(2,1)S(1)}, bf16[272,1536]{1,0:T(8,128)(2...) custom-call(s32[4]{0:T(128)S(1)} %copy-done.104, ...), custom_call_target="tpu_custom_call" | custom-call | flops 1048576 | bytes 1048576 | tf_op jit(solution)/shard_map/experts/pallas_call | solution.py:45
  195.2 5.0 %collective-permute-done.34.refs_1_ = bf16[272,1536]{1,0:T(8,128)(2,1)S(1)} collective-permute-done((bf16[272,1536]{1,0:T(8,128)(2,1)S(1)}, bf16[272,1536]{1,0:T(8,128)(2,1)S(1)}, u32[]{:S(2)}, u32[]{:S(2)}) %collective-permute-start.34) | collective-permute-done | bytes 835616 | tf_op jit(solution)/shard_map/ppermute | solution.py:443
  201.6 1.9 pad_maximum_fusion.2
  204.2 2.0 collective-permute-start.37
  206.3 13.7 %experts.7 = (bf16[256,1536]{1,0:T(8,128)(2,1)S(1)}, bf16[256,1536]{1,0:T(8,128)(2,1)S(1)}, bf16[272,1536]{1,0:T(8,128)(2,1)S(1)}, bf16[272,1536]{1,0:T(8,128)(2...) custom-call(s32[4]{0:T(128)S(1)} %copy-done.104, ...), custom_call_target="tpu_custom_call" | custom-call | flops 1048576 | bytes 1048576 | tf_op jit(solution)/shard_map/experts/pallas_call | solution.py:45
  223.2 2.6 collective-permute-done.40.refs_0_
  226.8 6.9 %experts.8 = (bf16[256,1536]{1,0:T(8,128)(2,1)S(1)}, bf16[272,1536]{1,0:T(8,128)(2,1)S(1)}, bf16[1,256,1536]{2,1,0:T(8,128)(2,1)S(1)}, bf16[1,272,1536]{2,1,0:T(...) custom-call(s32[4]{0:T(128)S(1)} %copy-done.104, ...), custom_call_target="tpu_custom_call" | custom-call | flops 1048576 | bytes 1048576 | tf_op jit(solution)/shard_map/experts/pallas_call | solution.py:45
  234.0 2.2 collective-permute-done.41
  238.9 13.2 %experts.9 = (bf16[256,1536]{1,0:T(8,128)(2,1)S(1)}, bf16[256,1536]{1,0:T(8,128)(2,1)S(1)}, bf16[272,1536]{1,0:T(8,128)(2,1)S(1)}, bf16[272,1536]{1,0:T(8,128)(2...) custom-call(s32[4]{0:T(128)S(1)} %copy-done.104, ...), custom_call_target="tpu_custom_call" | custom-call | flops 1048576 | bytes 1048576 | tf_op jit(solution)/shard_map/experts/pallas_call | solution.py:45
  253.0 3.5 collective-permute-done.44
  259.8 9.4 %expert_weights.2 = (bf16[288,1536]{1,0:T(8,128)(2,1)S(1)}, bf16[288,1536]{1,0:T(8,128)(2,1)S(1)}, bf16[224,1536]{1,0:T(8,128)(2,1)}, bf16[352,1536]{1,0:T(8,128)(2,1)}) custom-call(s32[4]{0:T(128)S(1)} %copy-done.104, bf16[160,1536]{1,0:T(8,128)(2,1)S(1)} %copy-done.16, bf16[320,1536]{1,0:T(8,128)(2,1)S(1)} %get-tuple-element.351.refs_1_, ...), custom_call_target="tpu_custom_call" | custom-call | flops 1048576 | bytes 1048576 | tf_op jit(solution)/shard_map/expert_weights/pallas_call | solution.py:45
  269.2 9.0 %collective-permute-done.47 = bf16[272,1536]{1,0:T(8,128)(2,1)S(1)} collective-permute-done((bf16[272,1536]{1,0:T(8,128)(2,1)S(1)}, bf16[272,1536]{1,0:T(8,128)(2,1)S(1)}, u32[]{:S(2)}, u32[]{:S(2)}) %collective-permute-start.47) | collective-permute-done | bytes 835616 | tf_op jit(solution)/shard_map/ppermute | solution.py:446
  282.7 18.4 %collective-permute-done.49 = bf16[272,1536]{1,0:T(8,128)(2,1)S(1)} collective-permute-done((bf16[272,1536]{1,0:T(8,128)(2,1)S(1)}, bf16[272,1536]{1,0:T(8,128)(2,1)S(1)}, u32[]{:S(2)}, u32[]{:S(2)}) %collective-permute-start.49) | collective-permute-done | bytes 835616 | tf_op jit(solution)/shard_map/ppermute | solution.py:443
  307.3 18.3 %collective-permute-done.55.refs_26_ = bf16[288,1536]{1,0:T(8,128)(2,1)S(1)} collective-permute-done((bf16[288,1536]{1,0:T(8,128)(2,1)S(1)}, bf16[288,1536]{1,0:T(8,128)(2,1)S(1)}, u32[]{:S(2)}, u32[]{:S(2)}) %collective-permute-start.55) | collective-permute-done | bytes 884768 | tf_op jit(solution)/shard_map/ppermute | solution.py:554
  331.1 8.3 %hidden_back.1 = (f32[256,1536]{1,0:T(8,128)S(1)}, bf16[256,1536]{1,0:T(8,128)(2,1)S(1)}, f32[1536,128]{1,0:T(8,128)S(1)}, f32[8,1536]{1,0:T(8,128)S(1)}, bf16[2...) custom-call(s32[4]{0:T(128)S(1)} %copy-done.104, s32[32,32]{1,0:T(8,128)S(1)} %copy-done.100, ...), custom_call_target="tpu_custom_call" | custom-call | flops 1048576 | bytes 1048576 | tf_op jit(solution)/shard_map/hidden_back/pallas_call | solution.py:45
  340.1 3.9 fusion.28
  343.9 2.6 collective-permute-done.60.refs_27_
  352.4 11.8 %attend_back.1 = (f32[256,1536]{1,0:T(8,128)}, bf16[2,8,48,2176]{3,2,1,0:T(8,128)(2,1)S(1)}, bf16[2,8,48,2176]{3,2,1,0:T(8,128)(2,1)S(1)}) custom-call(s32[4]{0:T(128)S(1)} %copy-done.104, s32[32,32]{1,0:T(8,128)S(1)} %copy-done.100, bf16[256,1536]{1,0:T(8,128)(2,1)S(1)} %bitcast.199, f32[128,128]{1,0:T(8,128)S(1)} %copy-done.98, f32[128,128]{1,0:T(8,128)S(1)} %copy-done.97, ...), custom_call_target="tpu_custom_call" | custom-call | flops 1048576 | bytes 1048576 | tf_op jit(solution)/shard_map/attend_back/pallas_call | solution.py:45
  369.1 4.0 fusion.24
  373.1 2.3 collective-permute-done.64.refs_28_
  380.7 10.9 %expert_weights.3 = (f32[768,768]{1,0:T(8,128)}, f32[768,768]{1,0:T(8,128)}, f32[384,1536]{1,0:T(8,128)}) custom-call(s32[4]{0:T(128)S(1)} %copy-done.104, bf16[160,1536]{1,0:T(8,128)(2,1)S(1)} %copy-done.16, bf16[320,1536]{1,0:T(8,128)(2,1)S(1)} %get-tuple-element.351.refs_1_, bf16[320,1536]{1,0:T(8,128)(2,1)S(1)} %get-tuple-element.352.refs_2_, ...), custom_call_target="tpu_custom_call" | custom-call | flops 1048576 | bytes 1048576 | tf_op jit(solution)/shard_map/expert_weights/pallas_call | solution.py:45
  391.6 14.1 %collective-permute-done.69 = bf16[8,48,1536]{2,1,0:T(8,128)(2,1)} collective-permute-done((bf16[8,48,1536]{2,1,0:T(8,128)(2,1)S(1)}, bf16[8,48,1536]{2,1,0:T(8,128)(2,1)}, u32[]{:S(2)}, u32[]{:S(2)}) %collective-permute-start.69) | collective-permute-done | bytes 1179680 | tf_op jit(solution)/shard_map/ppermute | solution.py:554
  405.7 2.1 fusion.1
  409.6 1.9 fusion.2
  416.7 2.7 collective-permute-done.75
  419.5 30.2 %collective-permute-done.74 = bf16[8,48,2176]{2,1,0:T(8,128)(2,1)S(1)} collective-permute-done((bf16[8,48,2176]{2,1,0:T(8,128)(2,1)S(1)}, bf16[8,48,2176]{2,1,0:T(8,128)(2,1)S(1)}, u32[]{:S(2)}, u32[]{:S(2)}) %collective-permute-start.74) | collective-permute-done | bytes 1671200 | tf_op jit(solution)/shard_map/ppermute | solution.py:554
  451.2 2.0 fusion
  458.7 2.8 collective-permute-done.76
  466.8 2.6 collective-permute-done.77
  473.3 2.6 collective-permute-done.78
  475.8 1.9 collective-permute-done.81
  481.4 2.3 collective-permute-done.79
  (463 shorter events, 122.4 us)
Async XLA Ops:
  7.1 19.3 %collective-permute-start.2 = (bf16[256,1536]{1,0:T(8,128)(2,1)}, bf16[256,1536]{1,0:T(8,128)(2,1)}, u32[]{:S(2)}, u32[]{:S(2)}) collective-permute-start(bf16[256,1536]{1,0:T(8,128)(2,1)} %bitcast.193), channel_id=1, source_target_pairs={{4,0},{5,1},{8,4},{9,5},{12,8},{13,9},{14,12},{15,13},{10,14},{11,... | collective-permute-start | bytes 2359304 | tf_op jit(solution)/shard_map/ppermute | solution.py:446
  8.6 19.0 %collective-permute-start.1 = (bf16[256,1536]{1,0:T(8,128)(2,1)}, bf16[256,1536]{1,0:T(8,128)(2,1)}, u32[]{:S(2)}, u32[]{:S(2)}) collective-permute-start(bf16[256,1536]{1,0:T(8,128)(2,1)} %bitcast.194), channel_id=1, source_target_pairs={{0,4},{1,5},{4,8},{5,9},{8,12},{9,13},{12,14},{13,15},{14,10},{15,... | collective-permute-start | bytes 2359304 | tf_op jit(solution)/shard_map/ppermute | solution.py:443
  15.4 52.5 %collective-permute-start.9 = (bf16[768,1536]{1,0:T(8,128)(2,1)S(1)}, bf16[768,1536]{1,0:T(8,128)(2,1)S(1)}, u32[]{:S(2)}, u32[]{:S(2)}) collective-permute-start(bf16[768,1536]{1,0:T(8,128)(2,1)S(1)} %pad_maximum_fusion.3), channel_id=1, source_target_pairs={{0,16},{16,0},{1,17},{17,1},{2,18},{18,2},{3,19},{19,3},{4,20},{20... | collective-permute-start | bytes 7077896 | tf_op jit(solution)/shard_map/ppermute | solution.py:554
  78.7 29.0 %collective-permute-start.23 = (bf16[384,1536]{1,0:T(8,128)(2,1)S(1)}, bf16[384,1536]{1,0:T(8,128)(2,1)}, u32[]{:S(2)}, u32[]{:S(2)}) collective-permute-start(bf16[384,1536]{1,0:T(8,128)(2,1)S(1)} %bitcast.187), channel_id=1, source_target_pairs={{0,16},{16,0},{1,17},{17,1},{2,18},{18,2},{3,19},{19,3},{4,20},{20... | collective-permute-start | bytes 3538952 | tf_op jit(solution)/shard_map/ppermute | solution.py:554
  89.2 19.9 %collective-permute-start.21 = (bf16[256,1536]{1,0:T(8,128)(2,1)}, bf16[256,1536]{1,0:T(8,128)(2,1)}, u32[]{:S(2)}, u32[]{:S(2)}) collective-permute-start(bf16[256,1536]{1,0:T(8,128)(2,1)} %collective-permute-done.1.refs_2_), channel_id=1, source_target_pairs={{0,4},{1,5},{4,8},{5,9},{8,12},{9,13},{12,14},{13,15},{14,10},{15,... | collective-permute-start | bytes 2359304 | tf_op jit(solution)/shard_map/ppermute | solution.py:443
  90.8 19.6 %collective-permute-start.22 = (bf16[256,1536]{1,0:T(8,128)(2,1)}, bf16[256,1536]{1,0:T(8,128)(2,1)}, u32[]{:S(2)}, u32[]{:S(2)}) collective-permute-start(bf16[256,1536]{1,0:T(8,128)(2,1)} %collective-permute-done.2.refs_4_), channel_id=1, source_target_pairs={{4,0},{5,1},{8,4},{9,5},{12,8},{13,9},{14,12},{15,13},{10,14},{11,... | collective-permute-start | bytes 2359304 | tf_op jit(solution)/shard_map/ppermute | solution.py:446
  110.4 38.1 %collective-permute-start.28 = (bf16[528,1536]{1,0:T(8,128)(2,1)S(1)}, bf16[528,1536]{1,0:T(8,128)(2,1)S(1)}, u32[]{:S(2)}, u32[]{:S(2)}) collective-permute-start(bf16[528,1536]{1,0:T(8,128)(2,1)S(1)} %pad_maximum_fusion.4), channel_id=1, source_target_pairs={{0,1},{1,0},{2,3},{3,2},{4,5},{5,4},{6,7},{7,6},{8,9},{9,8},{10,11... | collective-permute-start | bytes 4866056 | tf_op jit(solution)/shard_map/ppermute | solution.py:449
  110.4 21.4 %collective-permute-start.25 = (bf16[272,1536]{1,0:T(8,128)(2,1)S(1)}, bf16[272,1536]{1,0:T(8,128)(2,1)S(1)}, u32[]{:S(2)}, u32[]{:S(2)}) collective-permute-start(bf16[272,1536]{1,0:T(8,128)(2,1)S(1)} %copy-done.11), channel_id=1, source_target_pairs={{4,0},{5,1},{8,4},{9,5},{12,8},{13,9},{14,12},{15,13},{10,14},{11,... | collective-permute-start | bytes 2506760 | tf_op jit(solution)/shard_map/ppermute | solution.py:446
  110.9 21.4 %collective-permute-start.24 = (bf16[272,1536]{1,0:T(8,128)(2,1)S(1)}, bf16[272,1536]{1,0:T(8,128)(2,1)S(1)}, u32[]{:S(2)}, u32[]{:S(2)}) collective-permute-start(bf16[272,1536]{1,0:T(8,128)(2,1)S(1)} %copy-done.11), channel_id=1, source_target_pairs={{0,4},{1,5},{4,8},{5,9},{8,12},{9,13},{12,14},{13,15},{14,10},{15,... | collective-permute-start | bytes 2506760 | tf_op jit(solution)/shard_map/ppermute | solution.py:443
  112.4 36.0 %collective-permute-start.26 = (bf16[256,1536]{1,0:T(8,128)(2,1)}, bf16[256,1536]{1,0:T(8,128)(2,1)S(1)}, u32[]{:S(2)}, u32[]{:S(2)}) collective-permute-start(bf16[256,1536]{1,0:T(8,128)(2,1)} %collective-permute-done.21.refs_2_), channel_id=1, source_target_pairs={{0,4},{1,5},{4,8},{5,9},{8,12},{9,13},{12,14},{13,15},{14,10},{15,... | collective-permute-start | bytes 2359304 | tf_op jit(solution)/shard_map/ppermute | solution.py:443
  114.0 34.5 %collective-permute-start.27 = (bf16[256,1536]{1,0:T(8,128)(2,1)}, bf16[256,1536]{1,0:T(8,128)(2,1)S(1)}, u32[]{:S(2)}, u32[]{:S(2)}) collective-permute-start(bf16[256,1536]{1,0:T(8,128)(2,1)} %collective-permute-done.22.refs_4_), channel_id=1, source_target_pairs={{4,0},{5,1},{8,4},{9,5},{12,8},{13,9},{14,12},{15,13},{10,14},{11,... | collective-permute-start | bytes 2359304 | tf_op jit(solution)/shard_map/ppermute | solution.py:446
  148.5 30.7 %collective-permute-start.33 = (bf16[1056,1536]{1,0:T(8,128)(2,1)}, bf16[1056,1536]{1,0:T(8,128)(2,1)S(1)}, u32[]{:S(2)}, u32[]{:S(2)}) collective-permute-start(bf16[1056,1536]{1,0:T(8,128)(2,1)} %pad_maximum_fusion), channel_id=1, source_target_pairs={{0,1},{1,0},{2,3},{3,2},{4,5},{5,4},{6,7},{7,6},{8,9},{9,8},{10,11... | collective-permute-start | bytes 9732104 | tf_op jit(solution)/shard_map/ppermute | solution.py:449
  148.5 21.4 %collective-permute-start.29 = (bf16[272,1536]{1,0:T(8,128)(2,1)S(1)}, bf16[272,1536]{1,0:T(8,128)(2,1)S(1)}, u32[]{:S(2)}, u32[]{:S(2)}) collective-permute-start(bf16[272,1536]{1,0:T(8,128)(2,1)S(1)} %collective-permute-done.24.refs_1_), channel_id=1, source_target_pairs={{0,4},{1,5},{4,8},{5,9},{8,12},{9,13},{12,14},{13,15},{14,10},{15,... | collective-permute-start | bytes 2506760 | tf_op jit(solution)/shard_map/ppermute | solution.py:443
  150.1 21.4 %collective-permute-start.30 = (bf16[272,1536]{1,0:T(8,128)(2,1)S(1)}, bf16[272,1536]{1,0:T(8,128)(2,1)S(1)}, u32[]{:S(2)}, u32[]{:S(2)}) collective-permute-start(bf16[272,1536]{1,0:T(8,128)(2,1)S(1)} %collective-permute-done.25.refs_3_), channel_id=1, source_target_pairs={{4,0},{5,1},{8,4},{9,5},{12,8},{13,9},{14,12},{15,13},{10,14},{11,... | collective-permute-start | bytes 2506760 | tf_op jit(solution)/shard_map/ppermute | solution.py:446
  150.6 28.6 %collective-permute-start.32 = (bf16[128,1536]{1,0:T(8,128)(2,1)S(1)}, bf16[128,1536]{1,0:T(8,128)(2,1)S(1)}, u32[]{:S(2)}, u32[]{:S(2)}) collective-permute-start(bf16[128,1536]{1,0:T(8,128)(2,1)S(1)} %slice.159), channel_id=1, source_target_pairs={{4,0},{5,1},{8,4},{9,5},{12,8},{13,9},{14,12},{15,13},{10,14},{11,... | collective-permute-start | bytes 1179656 | tf_op jit(solution)/shard_map/ppermute | solution.py:446
  152.2 26.9 %collective-permute-start.31 = (bf16[128,1536]{1,0:T(8,128)(2,1)S(1)}, bf16[128,1536]{1,0:T(8,128)(2,1)S(1)}, u32[]{:S(2)}, u32[]{:S(2)}) collective-permute-start(bf16[128,1536]{1,0:T(8,128)(2,1)S(1)} %slice.158), channel_id=1, source_target_pairs={{0,4},{1,5},{4,8},{5,9},{8,12},{9,13},{12,14},{13,15},{14,10},{15,... | collective-permute-start | bytes 1179656 | tf_op jit(solution)/shard_map/ppermute | solution.py:443
  179.2 24.4 %collective-permute-start.36 = (bf16[1056,1536]{1,0:T(8,128)(2,1)}, bf16[1056,1536]{1,0:T(8,128)(2,1)}, u32[]{:S(2)}, u32[]{:S(2)}) collective-permute-start(bf16[1056,1536]{1,0:T(8,128)(2,1)} %pad_maximum_fusion.1), channel_id=1, source_target_pairs={{0,1},{1,0},{2,3},{3,2},{4,5},{5,4},{6,7},{7,6},{8,9},{9,8},{10,11... | collective-permute-start | bytes 9732104 | tf_op jit(solution)/shard_map/ppermute | solution.py:449
  179.3 21.0 %collective-permute-start.34 = (bf16[272,1536]{1,0:T(8,128)(2,1)S(1)}, bf16[272,1536]{1,0:T(8,128)(2,1)S(1)}, u32[]{:S(2)}, u32[]{:S(2)}) collective-permute-start(bf16[272,1536]{1,0:T(8,128)(2,1)S(1)} %collective-permute-done.29.refs_1_), channel_id=1, source_target_pairs={{0,4},{1,5},{4,8},{5,9},{8,12},{9,13},{12,14},{13,15},{14,10},{15,... | collective-permute-start | bytes 2506760 | tf_op jit(solution)/shard_map/ppermute | solution.py:443
  181.0 20.6 %collective-permute-start.35 = (bf16[272,1536]{1,0:T(8,128)(2,1)S(1)}, bf16[272,1536]{1,0:T(8,128)(2,1)S(1)}, u32[]{:S(2)}, u32[]{:S(2)}) collective-permute-start(bf16[272,1536]{1,0:T(8,128)(2,1)S(1)} %collective-permute-done.30.refs_3_), channel_id=1, source_target_pairs={{4,0},{5,1},{8,4},{9,5},{12,8},{13,9},{14,12},{15,13},{10,14},{11,... | collective-permute-start | bytes 2506760 | tf_op jit(solution)/shard_map/ppermute | solution.py:446
  203.6 18.7 %collective-permute-start.39 = (bf16[1056,1536]{1,0:T(8,128)(2,1)}, bf16[1056,1536]{1,0:T(8,128)(2,1)}, u32[]{:S(2)}, u32[]{:S(2)}) collective-permute-start(bf16[1056,1536]{1,0:T(8,128)(2,1)} %pad_maximum_fusion.2), channel_id=1, source_target_pairs={{0,1},{1,0},{2,3},{3,2},{4,5},{5,4},{6,7},{7,6},{8,9},{9,8},{10,11... | collective-permute-start | bytes 9732104 | tf_op jit(solution)/shard_map/ppermute | solution.py:449
  203.7 18.4 %collective-permute-start.38 = (bf16[144,1536]{1,0:T(8,128)(2,1)S(1)}, bf16[144,1536]{1,0:T(8,128)(2,1)S(1)}, u32[]{:S(2)}, u32[]{:S(2)}) collective-permute-start(bf16[144,1536]{1,0:T(8,128)(2,1)S(1)} %slice.161), channel_id=1, source_target_pairs={{4,0},{5,1},{8,4},{9,5},{12,8},{13,9},{14,12},{15,13},{10,14},{11,... | collective-permute-start | bytes 1327112 | tf_op jit(solution)/shard_map/ppermute | solution.py:446
  204.2 17.8 %collective-permute-start.37 = (bf16[128,1536]{1,0:T(8,128)(2,1)S(1)}, bf16[128,1536]{1,0:T(8,128)(2,1)S(1)}, u32[]{:S(2)}, u32[]{:S(2)}) collective-permute-start(bf16[128,1536]{1,0:T(8,128)(2,1)S(1)} %slice.160), channel_id=1, source_target_pairs={{0,4},{1,5},{4,8},{5,9},{8,12},{9,13},{12,14},{13,15},{14,10},{15,... | collective-permute-start | bytes 1179656 | tf_op jit(solution)/shard_map/ppermute | solution.py:443
  257.2 21.5 %collective-permute-start.45 = (bf16[2,272,1536]{2,1,0:T(8,128)(2,1)}, bf16[2,272,1536]{2,1,0:T(8,128)(2,1)S(1)}, u32[]{:S(2)}, u32[]{:S(2)}) collective-permute-start(bf16[2,272,1536]{2,1,0:T(8,128)(2,1)} %copy-done.108), channel_id=1, source_target_pairs={{0,1},{1,0},{2,3},{3,2},{4,5},{5,4},{6,7},{7,6},{8,9},{9,8},{10,11... | collective-permute-start | bytes 5013512 | tf_op jit(solution)/shard_map/ppermute | solution.py:449
  257.4 20.9 %collective-permute-start.47 = (bf16[272,1536]{1,0:T(8,128)(2,1)S(1)}, bf16[272,1536]{1,0:T(8,128)(2,1)S(1)}, u32[]{:S(2)}, u32[]{:S(2)}) collective-permute-start(bf16[272,1536]{1,0:T(8,128)(2,1)S(1)} %get-tuple-element.474), channel_id=1, source_target_pairs={{4,0},{5,1},{8,4},{9,5},{12,8},{13,9},{14,12},{15,13},{10,14},{11,... | collective-permute-start | bytes 2506760 | tf_op jit(solution)/shard_map/ppermute | solution.py:446
  257.9 20.8 %collective-permute-start.46 = (bf16[272,1536]{1,0:T(8,128)(2,1)S(1)}, bf16[272,1536]{1,0:T(8,128)(2,1)S(1)}, u32[]{:S(2)}, u32[]{:S(2)}) collective-permute-start(bf16[272,1536]{1,0:T(8,128)(2,1)S(1)} %get-tuple-element.475), channel_id=1, source_target_pairs={{0,4},{1,5},{4,8},{5,9},{8,12},{9,13},{12,14},{13,15},{14,10},{15,... | collective-permute-start | bytes 2506760 | tf_op jit(solution)/shard_map/ppermute | solution.py:443
  280.1 22.3 %collective-permute-start.48 = (bf16[2,272,1536]{2,1,0:T(8,128)(2,1)S(1)}, bf16[2,272,1536]{2,1,0:T(8,128)(2,1)S(1)}, u32[]{:S(2)}, u32[]{:S(2)}) collective-permute-start(bf16[2,272,1536]{2,1,0:T(8,128)(2,1)S(1)} %copy-done.107), channel_id=1, source_target_pairs={{0,1},{1,0},{2,3},{3,2},{4,5},{5,4},{6,7},{7,6},{8,9},{9,8},{10,11... | collective-permute-start | bytes 5013512 | tf_op jit(solution)/shard_map/ppermute | solution.py:449
  280.1 21.0 %collective-permute-start.49 = (bf16[272,1536]{1,0:T(8,128)(2,1)S(1)}, bf16[272,1536]{1,0:T(8,128)(2,1)S(1)}, u32[]{:S(2)}, u32[]{:S(2)}) collective-permute-start(bf16[272,1536]{1,0:T(8,128)(2,1)S(1)} %get-tuple-element.376), channel_id=1, source_target_pairs={{0,4},{1,5},{4,8},{5,9},{8,12},{9,13},{12,14},{13,15},{14,10},{15,... | collective-permute-start | bytes 2506760 | tf_op jit(solution)/shard_map/ppermute | solution.py:443
  281.6 20.7 %collective-permute-start.50 = (bf16[272,1536]{1,0:T(8,128)(2,1)S(1)}, bf16[272,1536]{1,0:T(8,128)(2,1)S(1)}, u32[]{:S(2)}, u32[]{:S(2)}) collective-permute-start(bf16[272,1536]{1,0:T(8,128)(2,1)S(1)} %get-tuple-element.377), channel_id=1, source_target_pairs={{4,0},{5,1},{8,4},{9,5},{12,8},{13,9},{14,12},{15,13},{10,14},{11,... | collective-permute-start | bytes 2506760 | tf_op jit(solution)/shard_map/ppermute | solution.py:446
  282.1 21.5 %collective-permute-start.51 = (bf16[288,1536]{1,0:T(8,128)(2,1)S(1)}, bf16[288,1536]{1,0:T(8,128)(2,1)S(1)}, u32[]{:S(2)}, u32[]{:S(2)}) collective-permute-start(bf16[288,1536]{1,0:T(8,128)(2,1)S(1)} %get-tuple-element.375), channel_id=1, source_target_pairs={{0,16},{16,0},{1,17},{17,1},{2,18},{18,2},{3,19},{19,3},{4,20},{20... | collective-permute-start | bytes 2654216 | tf_op jit(solution)/shard_map/ppermute | solution.py:554
  303.6 22.1 %collective-permute-start.55 = (bf16[288,1536]{1,0:T(8,128)(2,1)S(1)}, bf16[288,1536]{1,0:T(8,128)(2,1)S(1)}, u32[]{:S(2)}, u32[]{:S(2)}) collective-permute-start(bf16[288,1536]{1,0:T(8,128)(2,1)S(1)} %get-tuple-element.384), channel_id=1, source_target_pairs={{0,16},{16,0},{1,17},{17,1},{2,18},{18,2},{3,19},{19,3},{4,20},{20... | collective-permute-start | bytes 2654216 | tf_op jit(solution)/shard_map/ppermute | solution.py:554
  304.2 22.4 %collective-permute-start.53 = (bf16[272,1536]{1,0:T(8,128)(2,1)S(1)}, bf16[272,1536]{1,0:T(8,128)(2,1)S(1)}, u32[]{:S(2)}, u32[]{:S(2)}) collective-permute-start(bf16[272,1536]{1,0:T(8,128)(2,1)S(1)} %get-tuple-element.380), channel_id=1, source_target_pairs={{0,4},{1,5},{4,8},{5,9},{8,12},{9,13},{12,14},{13,15},{14,10},{15,... | collective-permute-start | bytes 2506760 | tf_op jit(solution)/shard_map/ppermute | solution.py:443
  305.8 20.8 %collective-permute-start.54 = (bf16[272,1536]{1,0:T(8,128)(2,1)S(1)}, bf16[272,1536]{1,0:T(8,128)(2,1)S(1)}, u32[]{:S(2)}, u32[]{:S(2)}) collective-permute-start(bf16[272,1536]{1,0:T(8,128)(2,1)S(1)} %get-tuple-element.381), channel_id=1, source_target_pairs={{4,0},{5,1},{8,4},{9,5},{12,8},{13,9},{14,12},{15,13},{10,14},{11,... | collective-permute-start | bytes 2506760 | tf_op jit(solution)/shard_map/ppermute | solution.py:446
  329.5 17.1 %collective-permute-start.60 = (bf16[224,1536]{1,0:T(8,128)(2,1)}, bf16[224,1536]{1,0:T(8,128)(2,1)S(1)}, u32[]{:S(2)}, u32[]{:S(2)}) collective-permute-start(bf16[224,1536]{1,0:T(8,128)(2,1)} %get-tuple-element.400), channel_id=1, source_target_pairs={{0,16},{16,0},{1,17},{17,1},{2,18},{18,2},{3,19},{19,3},{4,20},{20... | collective-permute-start | bytes 2064392 | tf_op jit(solution)/shard_map/ppermute | solution.py:554
  347.4 28.0 %collective-permute-start.65 = (bf16[2,8,48,1536]{3,2,1,0:T(8,128)(2,1)}, bf16[2,8,48,1536]{3,2,1,0:T(8,128)(2,1)}, u32[]{:S(2)}, u32[]{:S(2)}) collective-permute-start(bf16[2,8,48,1536]{3,2,1,0:T(8,128)(2,1)} %get-tuple-element.418), channel_id=1, source_target_pairs={{0,1},{1,0},{2,3},{3,2},{4,5},{5,4},{6,7},{7,6},{8,9},{9,8},{10,11... | collective-permute-start | bytes 7077896 | tf_op jit(solution)/shard_map/ppermute | solution.py:449
  347.4 21.6 %collective-permute-start.61 = (bf16[2,256,1536]{2,1,0:T(8,128)(2,1)}, bf16[2,256,1536]{2,1,0:T(8,128)(2,1)}, u32[]{:S(2)}, u32[]{:S(2)}) collective-permute-start(bf16[2,256,1536]{2,1,0:T(8,128)(2,1)} %get-tuple-element.403), channel_id=1, source_target_pairs={{0,1},{1,0},{2,3},{3,2},{4,5},{5,4},{6,7},{7,6},{8,9},{9,8},{10,11... | collective-permute-start | bytes 4718600 | tf_op jit(solution)/shard_map/ppermute | solution.py:449
  347.9 19.8 %collective-permute-start.62 = (bf16[256,1536]{1,0:T(8,128)(2,1)}, bf16[256,1536]{1,0:T(8,128)(2,1)}, u32[]{:S(2)}, u32[]{:S(2)}) collective-permute-start(bf16[256,1536]{1,0:T(8,128)(2,1)} %get-tuple-element.401), channel_id=1, source_target_pairs={{0,4},{1,5},{4,8},{5,9},{8,12},{9,13},{12,14},{13,15},{14,10},{15,... | collective-permute-start | bytes 2359304 | tf_op jit(solution)/shard_map/ppermute | solution.py:443
  349.5 19.5 %collective-permute-start.63 = (bf16[256,1536]{1,0:T(8,128)(2,1)}, bf16[256,1536]{1,0:T(8,128)(2,1)}, u32[]{:S(2)}, u32[]{:S(2)}) collective-permute-start(bf16[256,1536]{1,0:T(8,128)(2,1)} %get-tuple-element.402), channel_id=1, source_target_pairs={{4,0},{5,1},{8,4},{9,5},{12,8},{13,9},{14,12},{15,13},{10,14},{11,... | collective-permute-start | bytes 2359304 | tf_op jit(solution)/shard_map/ppermute | solution.py:446
  350.0 25.4 %collective-permute-start.64 = (bf16[352,1536]{1,0:T(8,128)(2,1)}, bf16[352,1536]{1,0:T(8,128)(2,1)S(1)}, u32[]{:S(2)}, u32[]{:S(2)}) collective-permute-start(bf16[352,1536]{1,0:T(8,128)(2,1)} %get-tuple-element.416), channel_id=1, source_target_pairs={{0,16},{16,0},{1,17},{17,1},{2,18},{18,2},{3,19},{19,3},{4,20},{20... | collective-permute-start | bytes 3244040 | tf_op jit(solution)/shard_map/ppermute | solution.py:554
  375.4 34.2 %collective-permute-start.70 = (bf16[2,8,48,2176]{3,2,1,0:T(8,128)(2,1)}, bf16[2,8,48,2176]{3,2,1,0:T(8,128)(2,1)}, u32[]{:S(2)}, u32[]{:S(2)}) collective-permute-start(bf16[2,8,48,2176]{3,2,1,0:T(8,128)(2,1)} %copy-done.105), channel_id=1, source_target_pairs={{0,1},{1,0},{2,3},{3,2},{4,5},{5,4},{6,7},{7,6},{8,9},{9,8},{10,11... | collective-permute-start | bytes 10027016 | tf_op jit(solution)/shard_map/ppermute | solution.py:449
  377.2 28.5 %collective-permute-start.69 = (bf16[8,48,1536]{2,1,0:T(8,128)(2,1)S(1)}, bf16[8,48,1536]{2,1,0:T(8,128)(2,1)}, u32[]{:S(2)}, u32[]{:S(2)}) collective-permute-start(bf16[8,48,1536]{2,1,0:T(8,128)(2,1)S(1)} %fusion.32), channel_id=1, source_target_pairs={{0,16},{16,0},{1,17},{17,1},{2,18},{18,2},{3,19},{19,3},{4,20},{20... | collective-permute-start | bytes 3538952 | tf_op jit(solution)/shard_map/ppermute | solution.py:554
  378.2 29.6 %collective-permute-start.66 = (bf16[2,256,1536]{2,1,0:T(8,128)(2,1)}, bf16[2,256,1536]{2,1,0:T(8,128)(2,1)S(1)}, u32[]{:S(2)}, u32[]{:S(2)}) collective-permute-start(bf16[2,256,1536]{2,1,0:T(8,128)(2,1)} %get-tuple-element.421), channel_id=1, source_target_pairs={{0,1},{1,0},{2,3},{3,2},{4,5},{5,4},{6,7},{7,6},{8,9},{9,8},{10,11... | collective-permute-start | bytes 4718600 | tf_op jit(solution)/shard_map/ppermute | solution.py:449
  378.4 29.4 %collective-permute-start.67 = (bf16[256,1536]{1,0:T(8,128)(2,1)}, bf16[256,1536]{1,0:T(8,128)(2,1)S(1)}, u32[]{:S(2)}, u32[]{:S(2)}) collective-permute-start(bf16[256,1536]{1,0:T(8,128)(2,1)} %get-tuple-element.419), channel_id=1, source_target_pairs={{0,4},{1,5},{4,8},{5,9},{8,12},{9,13},{12,14},{13,15},{14,10},{15,... | collective-permute-start | bytes 2359304 | tf_op jit(solution)/shard_map/ppermute | solution.py:443
  379.9 27.9 %collective-permute-start.68 = (bf16[256,1536]{1,0:T(8,128)(2,1)}, bf16[256,1536]{1,0:T(8,128)(2,1)}, u32[]{:S(2)}, u32[]{:S(2)}) collective-permute-start(bf16[256,1536]{1,0:T(8,128)(2,1)} %get-tuple-element.420), channel_id=1, source_target_pairs={{4,0},{5,1},{8,4},{9,5},{12,8},{13,9},{14,12},{15,13},{10,14},{11,... | collective-permute-start | bytes 2359304 | tf_op jit(solution)/shard_map/ppermute | solution.py:446
  411.5 38.2 %collective-permute-start.74 = (bf16[8,48,2176]{2,1,0:T(8,128)(2,1)S(1)}, bf16[8,48,2176]{2,1,0:T(8,128)(2,1)S(1)}, u32[]{:S(2)}, u32[]{:S(2)}) collective-permute-start(bf16[8,48,2176]{2,1,0:T(8,128)(2,1)S(1)} %fusion.2), channel_id=1, source_target_pairs={{0,16},{16,0},{1,17},{17,1},{2,18},{18,2},{3,19},{19,3},{4,20},{20... | collective-permute-start | bytes 5013512 | tf_op jit(solution)/shard_map/ppermute | solution.py:554
  414.1 40.8 %collective-permute-start.86 = (bf16[48,1536]{1,0:T(8,128)(2,1)S(1)}, bf16[48,1536]{1,0:T(8,128)(2,1)S(1)}, u32[]{:S(2)}, u32[]{:S(2)}) collective-permute-start(bf16[48,1536]{1,0:T(8,128)(2,1)S(1)} %get-tuple-element.486), channel_id=1, source_target_pairs={{4,0},{5,1},{8,4},{9,5},{12,8},{13,9},{14,12},{15,13},{10,14},{11,... | collective-permute-start | bytes 442376 | tf_op jit(solution)/shard_map/ppermute | solution.py:446
  414.7 38.7 %collective-permute-start.72 = (bf16[256,1536]{1,0:T(8,128)(2,1)S(1)}, bf16[256,1536]{1,0:T(8,128)(2,1)S(1)}, u32[]{:S(2)}, u32[]{:S(2)}) collective-permute-start(bf16[256,1536]{1,0:T(8,128)(2,1)S(1)} %get-tuple-element.429), channel_id=1, source_target_pairs={{0,4},{1,5},{4,8},{5,9},{8,12},{9,13},{12,14},{13,15},{14,10},{15,... | collective-permute-start | bytes 2359304 | tf_op jit(solution)/shard_map/ppermute | solution.py:443
  416.1 37.3 %collective-permute-start.73 = (bf16[256,1536]{1,0:T(8,128)(2,1)S(1)}, bf16[256,1536]{1,0:T(8,128)(2,1)S(1)}, u32[]{:S(2)}, u32[]{:S(2)}) collective-permute-start(bf16[256,1536]{1,0:T(8,128)(2,1)S(1)} %get-tuple-element.430), channel_id=1, source_target_pairs={{4,0},{5,1},{8,4},{9,5},{12,8},{13,9},{14,12},{15,13},{10,14},{11,... | collective-permute-start | bytes 2359304 | tf_op jit(solution)/shard_map/ppermute | solution.py:446
  419.4 60.5 %collective-permute-start.71 = (bf16[1,256,1536]{2,1,0:T(8,128)(2,1)S(1)}, bf16[1,256,1536]{2,1,0:T(8,128)(2,1)S(1)}, u32[]{:S(2)}, u32[]{:S(2)}) collective-permute-start(bf16[1,256,1536]{2,1,0:T(8,128)(2,1)S(1)} %copy-done.112), channel_id=1, source_target_pairs={{0,1},{1,0},{2,3},{3,2},{4,5},{5,4},{6,7},{7,6},{8,9},{9,8},{10,11... | collective-permute-start | bytes 2359304 | tf_op jit(solution)/shard_map/ppermute | solution.py:449
  (177 other events, 2155.5 us)

commit v5 on v4

--- a/solution.py
+++ b/solution.py
@@ -435,6 +435,9 @@
             (2 * self.order[p] + lane, 2 * self.order[(p + 1) % n] + lane) for p in range(n) for lane in (0, 1)
         ]
         self.down = [(b, a) for a, b in self.up]
+        self.across = [
+            (2 * self.order[p] + lane, 2 * self.order[(p + self.half) % n] + lane) for p in range(n) for lane in (0, 1)
+        ]
         self.swap = [(d, d ^ 1) for d in range(devices)]
         self.place = np.argsort(np.array(self.order)).astype(np.int32)
         self.offsets = [0] + [s * o for o in range(1, self.half) for s in (-1, 1)] + [self.half]
@@ -806,9 +809,13 @@
         return total(keep[0], got[0], far)
 
     class Blocks:
-        def __init__(self, both):
+        def __init__(self, both, across=()):
             self.term = {o: both[k_] for k_, o in enumerate(ring.offsets)}
             self.up, self.down, self.left = None, None, ring.half
+            self.across = []
+            if across:
+                self.left -= 1
+                self.across = [lax.ppermute(after(self.term[ring.half], *across), "expert", ring.across)]
 
         def hop(self, *events):
             s = self.left
@@ -824,8 +831,11 @@
 
         def result(self):
             while self.left:
-                self.hop()
-            return self.up.astype(f32) + self.down.astype(f32) + self.term[0].astype(f32)
+                self.hop(*(self.across if self.left == 1 else ()))
+            out = self.up.astype(f32) + self.down.astype(f32) + self.term[0].astype(f32)
+            for more_ in self.across:
+                out = out + more_.astype(f32)
+            return out
 
     if apart:
         qkv_got = ring.send_core(after(qkv_part[1], *out_ring.sent))
@@ -833,8 +843,9 @@
         while out_ring.left:
             there = out_ring.step(gate_grad, o_sum, qkv_got)
         qkv_sum = over_y(qkv_part[0], qkv_got, *out_ring.sent)
-        o_blocks, qkv_blocks = Blocks(o_sum), Blocks(qkv_sum)
+        o_blocks = Blocks(o_sum)
         there += o_blocks.hop(*out_ring.sent)
+        qkv_blocks = Blocks(qkv_sum, there)
         qkv_blocks.hop(*there)
         o_grad, qkv_grad = o_blocks.result(), qkv_blocks.result()
     else:

time: 495 us -> 495 us (level)
    ppermute x9, waiting for transfers between devices: 77.7 us -> 70.9 us  [from_dp(): return lax.ppermute(x, 'dp', dp_pairs(shift))]
    ppermute x28 -> x27, waiting for transfers between devices: 102 us -> 98.8 us  [send_up(): return lax.ppermute(x, 'expert', self.up)]
    unnamed x275 -> x277, local copies, waits for them, and re-layouts: 14.3 us -> 15.2 us
    ppermute x28 -> x27, starting transfers between devices: 40.7 us -> 40.1 us  [send_up(): return lax.ppermute(x, 'expert', self.up)]
    convert_element_type x19 -> x18, other arithmetic: 21.4 us -> 21.6 us  [total(): return out.astype(bf16)]
where the time goes in v5:
time: 495 us; the launch traced here: 487 us
  waiting for transfers between devices  245 us (49%)
  Pallas kernels  108 us (22%)
  starting transfers between devices  74.8 us (15%)
  other arithmetic  36 us (7%)
  local copies, waits for them, and re-layouts  21 us (4%)
    pallas_call x10, Pallas kernels, call(): pl.pallas_call(body, out_shape=outs, in_specs=ins, out_specs=vmem(len(out...  108 us
    ppermute x27, waiting for transfers between devices, send_up(): return lax.ppermute(x, 'expert', self.up)  98.8 us
    ppermute x9, waiting for transfers between devices, from_dp(): return lax.ppermute(x, 'dp', dp_pairs(shift))  70.9 us
    ppermute x26, waiting for transfers between devices, send_down(): return lax.ppermute(x, 'expert', self.down)  61.5 us
    ppermute x27, starting transfers between devices, send_up(): return lax.ppermute(x, 'expert', self.up)  40.1 us
    convert_element_type x18, other arithmetic, total(): return out.astype(bf16)  21.6 us
    ppermute x26, starting transfers between devices, send_down(): return lax.ppermute(x, 'expert', self.down)  17.6 us
    unnamed x277, local copies, waits for them, and re-layouts  15.2 us
  transfers between devices with their start and end apart: 89, of which 51 were waited for; matrix products, arithmetic and copies ran while one was open for 7% of the time, Pallas kernels for 21%

profile of v5, /device:TPU:0, one launch (start us, length us, event | category | flops | bytes accessed | tf_op | source)
XLA Modules:
  0.0 487.2 jit_solution(12771387738466106217)
XLA Ops:
  4.1 3.0 collective-permute-start
  10.9 4.5 collective-permute-done
  18.2 8.2 %collective-permute-done.2.refs_4_ = bf16[256,1536]{1,0:T(8,128)(2,1)} collective-permute-done((bf16[256,1536]{1,0:T(8,128)(2,1)}, bf16[256,1536]{1,0:T(8,128)(2,1)}, u32[]{:S(2)}, u32[]{:S(2)}) %collective-permute-start.2) | collective-permute-done | bytes 786464 | tf_op jit(solution)/shard_map/ppermute | solution.py:449
  29.6 14.2 %collective-permute-done.3.refs_2_ = bf16[2,48,3712]{2,1,0:T(8,128)(2,1)S(1)} collective-permute-done((bf16[2,48,3712]{2,1,0:T(8,128)(2,1)S(1)}, bf16[2,48,3712]{2,1,0:T(8,128)(2,1)S(1)}, u32[]{:S(2)}, u32[]{:S(2)}) %collective-permute-start.3) | collective-permute-done | bytes 712736 | tf_op jit(solution)/shard_map/ppermute | solution.py:446
  46.3 14.1 %collective-permute-done.5.refs_6_ = bf16[2,48,3712]{2,1,0:T(8,128)(2,1)S(1)} collective-permute-done((bf16[2,48,3712]{2,1,0:T(8,128)(2,1)S(1)}, bf16[2,48,3712]{2,1,0:T(8,128)(2,1)S(1)}, u32[]{:S(2)}, u32[]{:S(2)}) %collective-permute-start.5) | collective-permute-done | bytes 712736 | tf_op jit(solution)/shard_map/ppermute | solution.py:446
  62.9 5.1 %collective-permute-done.9.refs_6_.refs_8_ = bf16[768,1536]{1,0:T(8,128)(2,1)S(1)} collective-permute-done((bf16[768,1536]{1,0:T(8,128)(2,1)S(1)}, bf16[768,1536]{1,0:T(8,128)(2,1)S(1)}, u32[]{:S(2)}, u32[]{:S(2)}) %collective-permute-start.9) | collective-permute-done | bytes 2359328 | tf_op jit(solution)/shard_map/ppermute | solution.py:557
  68.0 6.7 %collective-permute-done.6.refs_10_ = bf16[2,48,3712]{2,1,0:T(8,128)(2,1)S(1)} collective-permute-done((bf16[2,48,3712]{2,1,0:T(8,128)(2,1)S(1)}, bf16[2,48,3712]{2,1,0:T(8,128)(2,1)S(1)}, u32[]{:S(2)}, u32[]{:S(2)}) %collective-permute-start.6) | collective-permute-done | bytes 712736 | tf_op jit(solution)/shard_map/ppermute | solution.py:446
  79.2 7.6 %collective-permute-done.11.refs_15_ = bf16[1,48,3712]{2,1,0:T(8,128)(2,1)S(1)} collective-permute-done((bf16[1,48,3712]{2,1,0:T(8,128)(2,1)S(1)}, bf16[1,48,3712]{2,1,0:T(8,128)(2,1)S(1)}, u32[]{:S(2)}, u32[]{:S(2)}) %collective-permute-start.11) | collective-permute-done | bytes 356384 | tf_op jit(solution)/shard_map/ppermute | solution.py:449
  92.7 13.3 %forward.1 = (bf16[1536,2048]{1,0:T(8,128)(2,1)}, bf16[1536,1536]{1,0:T(8,128)(2,1)}, bf16[1536,128]{1,0:T(8,128)(2,1)}, f32[8,1536]{1,0:T(8,128)}, bf16[256,153...) custom-call(s32[4]{0:T(128)} %pad_add_fusion.me_ref, ...), custom_call_target="tpu_custom_call" | custom-call | flops 1048576 | bytes 1048576 | tf_op jit(solution)/shard_map/forward/pallas_call | solution.py:45
  114.4 17.3 %collective-permute-done.25.refs_3_ = bf16[272,1536]{1,0:T(8,128)(2,1)S(1)} collective-permute-done((bf16[272,1536]{1,0:T(8,128)(2,1)S(1)}, bf16[272,1536]{1,0:T(8,128)(2,1)S(1)}, u32[]{:S(2)}, u32[]{:S(2)}) %collective-permute-start.25) | collective-permute-done | bytes 835616 | tf_op jit(solution)/shard_map/ppermute | solution.py:449
  132.3 3.3 pad_maximum_fusion
  135.6 12.8 %collective-permute-done.26.refs_2_ = bf16[256,1536]{1,0:T(8,128)(2,1)S(1)} collective-permute-done((bf16[256,1536]{1,0:T(8,128)(2,1)}, bf16[256,1536]{1,0:T(8,128)(2,1)S(1)}, u32[]{:S(2)}, u32[]{:S(2)}) %collective-permute-start.26) | collective-permute-done | bytes 786464 | tf_op jit(solution)/shard_map/ppermute | solution.py:446
  152.9 7.0 %experts.5 = (bf16[256,1536]{1,0:T(8,128)(2,1)S(1)}, bf16[272,1536]{1,0:T(8,128)(2,1)S(1)}, bf16[1,256,1536]{2,1,0:T(8,128)(2,1)S(1)}, bf16[1,272,1536]{2,1,0:T(...) custom-call(s32[4]{0:T(128)S(1)} %copy-done.104, ...), custom_call_target="tpu_custom_call" | custom-call | flops 1048576 | bytes 1048576 | tf_op jit(solution)/shard_map/experts/pallas_call | solution.py:45
  160.9 9.1 %collective-permute-done.29.refs_1_ = bf16[272,1536]{1,0:T(8,128)(2,1)S(1)} collective-permute-done((bf16[272,1536]{1,0:T(8,128)(2,1)S(1)}, bf16[272,1536]{1,0:T(8,128)(2,1)S(1)}, u32[]{:S(2)}, u32[]{:S(2)}) %collective-permute-start.29) | collective-permute-done | bytes 835616 | tf_op jit(solution)/shard_map/ppermute | solution.py:446
  171.5 3.3 pad_maximum_fusion.1
  174.9 4.3 collective-permute-done.32.refs_4_
  181.5 13.7 %experts.6 = (bf16[256,1536]{1,0:T(8,128)(2,1)S(1)}, bf16[256,1536]{1,0:T(8,128)(2,1)S(1)}, bf16[272,1536]{1,0:T(8,128)(2,1)S(1)}, bf16[272,1536]{1,0:T(8,128)(2...) custom-call(s32[4]{0:T(128)S(1)} %copy-done.104, ...), custom_call_target="tpu_custom_call" | custom-call | flops 1048576 | bytes 1048576 | tf_op jit(solution)/shard_map/experts/pallas_call | solution.py:45
  195.2 5.1 %collective-permute-done.34.refs_1_ = bf16[272,1536]{1,0:T(8,128)(2,1)S(1)} collective-permute-done((bf16[272,1536]{1,0:T(8,128)(2,1)S(1)}, bf16[272,1536]{1,0:T(8,128)(2,1)S(1)}, u32[]{:S(2)}, u32[]{:S(2)}) %collective-permute-start.34) | collective-permute-done | bytes 835616 | tf_op jit(solution)/shard_map/ppermute | solution.py:446
  204.1 2.0 collective-permute-start.37
  206.2 13.6 %experts.7 = (bf16[256,1536]{1,0:T(8,128)(2,1)S(1)}, bf16[256,1536]{1,0:T(8,128)(2,1)S(1)}, bf16[272,1536]{1,0:T(8,128)(2,1)S(1)}, bf16[272,1536]{1,0:T(8,128)(2...) custom-call(s32[4]{0:T(128)S(1)} %copy-done.104, ...), custom_call_target="tpu_custom_call" | custom-call | flops 1048576 | bytes 1048576 | tf_op jit(solution)/shard_map/experts/pallas_call | solution.py:45
  223.1 2.6 collective-permute-done.40.refs_0_
  226.7 6.9 %experts.8 = (bf16[256,1536]{1,0:T(8,128)(2,1)S(1)}, bf16[272,1536]{1,0:T(8,128)(2,1)S(1)}, bf16[1,256,1536]{2,1,0:T(8,128)(2,1)S(1)}, bf16[1,272,1536]{2,1,0:T(...) custom-call(s32[4]{0:T(128)S(1)} %copy-done.104, ...), custom_call_target="tpu_custom_call" | custom-call | flops 1048576 | bytes 1048576 | tf_op jit(solution)/shard_map/experts/pallas_call | solution.py:45
  233.9 2.2 collective-permute-done.41
  238.8 13.2 %experts.9 = (bf16[256,1536]{1,0:T(8,128)(2,1)S(1)}, bf16[256,1536]{1,0:T(8,128)(2,1)S(1)}, bf16[272,1536]{1,0:T(8,128)(2,1)S(1)}, bf16[272,1536]{1,0:T(8,128)(2...) custom-call(s32[4]{0:T(128)S(1)} %copy-done.104, ...), custom_call_target="tpu_custom_call" | custom-call | flops 1048576 | bytes 1048576 | tf_op jit(solution)/shard_map/experts/pallas_call | solution.py:45
  252.9 3.5 collective-permute-done.44
  259.7 9.4 %expert_weights.2 = (bf16[288,1536]{1,0:T(8,128)(2,1)S(1)}, bf16[288,1536]{1,0:T(8,128)(2,1)S(1)}, bf16[224,1536]{1,0:T(8,128)(2,1)}, bf16[352,1536]{1,0:T(8,128)(2,1)}) custom-call(s32[4]{0:T(128)S(1)} %copy-done.104, bf16[160,1536]{1,0:T(8,128)(2,1)S(1)} %copy-done.16, bf16[320,1536]{1,0:T(8,128)(2,1)S(1)} %get-tuple-element.355.refs_1_, ...), custom_call_target="tpu_custom_call" | custom-call | flops 1048576 | bytes 1048576 | tf_op jit(solution)/shard_map/expert_weights/pallas_call | solution.py:45
  269.1 9.0 %collective-permute-done.47 = bf16[272,1536]{1,0:T(8,128)(2,1)S(1)} collective-permute-done((bf16[272,1536]{1,0:T(8,128)(2,1)S(1)}, bf16[272,1536]{1,0:T(8,128)(2,1)S(1)}, u32[]{:S(2)}, u32[]{:S(2)}) %collective-permute-start.47) | collective-permute-done | bytes 835616 | tf_op jit(solution)/shard_map/ppermute | solution.py:449
  282.6 18.4 %collective-permute-done.49 = bf16[272,1536]{1,0:T(8,128)(2,1)S(1)} collective-permute-done((bf16[272,1536]{1,0:T(8,128)(2,1)S(1)}, bf16[272,1536]{1,0:T(8,128)(2,1)S(1)}, u32[]{:S(2)}, u32[]{:S(2)}) %collective-permute-start.49) | collective-permute-done | bytes 835616 | tf_op jit(solution)/shard_map/ppermute | solution.py:446
  307.3 18.3 %collective-permute-done.55.refs_26_ = bf16[288,1536]{1,0:T(8,128)(2,1)S(1)} collective-permute-done((bf16[288,1536]{1,0:T(8,128)(2,1)S(1)}, bf16[288,1536]{1,0:T(8,128)(2,1)S(1)}, u32[]{:S(2)}, u32[]{:S(2)}) %collective-permute-start.55) | collective-permute-done | bytes 884768 | tf_op jit(solution)/shard_map/ppermute | solution.py:557
  331.0 8.3 %hidden_back.1 = (f32[256,1536]{1,0:T(8,128)S(1)}, bf16[256,1536]{1,0:T(8,128)(2,1)S(1)}, f32[1536,128]{1,0:T(8,128)S(1)}, f32[8,1536]{1,0:T(8,128)S(1)}, bf16[2...) custom-call(s32[4]{0:T(128)S(1)} %copy-done.104, s32[32,32]{1,0:T(8,128)S(1)} %copy-done.100, ...), custom_call_target="tpu_custom_call" | custom-call | flops 1048576 | bytes 1048576 | tf_op jit(solution)/shard_map/hidden_back/pallas_call | solution.py:45
  340.0 3.9 fusion.28
  343.9 2.6 collective-permute-done.60.refs_27_
  352.3 11.8 %attend_back.1 = (f32[256,1536]{1,0:T(8,128)}, bf16[2,8,48,2176]{3,2,1,0:T(8,128)(2,1)S(1)}, bf16[2,8,48,2176]{3,2,1,0:T(8,128)(2,1)S(1)}) custom-call(s32[4]{0:T(128)S(1)} %copy-done.104, s32[32,32]{1,0:T(8,128)S(1)} %copy-done.100, bf16[256,1536]{1,0:T(8,128)(2,1)S(1)} %bitcast.196, f32[128,128]{1,0:T(8,128)S(1)} %copy-done.98, f32[128,128]{1,0:T(8,128)S(1)} %copy-done.97, ...), custom_call_target="tpu_custom_call" | custom-call | flops 1048576 | bytes 1048576 | tf_op jit(solution)/shard_map/attend_back/pallas_call | solution.py:45
  369.0 4.0 fusion.24
  373.0 2.3 collective-permute-done.64.refs_28_
  380.7 10.9 %expert_weights.3 = (f32[768,768]{1,0:T(8,128)}, f32[768,768]{1,0:T(8,128)}, f32[384,1536]{1,0:T(8,128)}) custom-call(s32[4]{0:T(128)S(1)} %copy-done.104, bf16[160,1536]{1,0:T(8,128)(2,1)S(1)} %copy-done.16, bf16[320,1536]{1,0:T(8,128)(2,1)S(1)} %get-tuple-element.355.refs_1_, bf16[320,1536]{1,0:T(8,128)(2,1)S(1)} %get-tuple-element.356.refs_2_, ...), custom_call_target="tpu_custom_call" | custom-call | flops 1048576 | bytes 1048576 | tf_op jit(solution)/shard_map/expert_weights/pallas_call | solution.py:45
  391.5 14.1 %collective-permute-done.69 = bf16[8,48,1536]{2,1,0:T(8,128)(2,1)} collective-permute-done((bf16[8,48,1536]{2,1,0:T(8,128)(2,1)S(1)}, bf16[8,48,1536]{2,1,0:T(8,128)(2,1)}, u32[]{:S(2)}, u32[]{:S(2)}) %collective-permute-start.69) | collective-permute-done | bytes 1179680 | tf_op jit(solution)/shard_map/ppermute | solution.py:557
  405.6 2.1 fusion.1
  408.7 2.0 fusion.20
  415.7 3.1 collective-permute-done.75
  422.4 3.3 collective-permute-done.83
  427.3 23.5 %collective-permute-done.74 = bf16[8,48,2176]{2,1,0:T(8,128)(2,1)S(1)} collective-permute-done((bf16[8,48,2176]{2,1,0:T(8,128)(2,1)S(1)}, bf16[8,48,2176]{2,1,0:T(8,128)(2,1)S(1)}, u32[]{:S(2)}, u32[]{:S(2)}) %collective-permute-start.74) | collective-permute-done | bytes 1671200 | tf_op jit(solution)/shard_map/ppermute | solution.py:557
  451.6 2.0 fusion
  458.1 2.9 collective-permute-done.76
  466.5 3.5 collective-permute-start.80
  472.0 3.2 collective-permute-done.80
  475.2 3.1 collective-permute-start.81
  481.6 2.5 collective-permute-done.82
  (464 shorter events, 123.8 us)
Async XLA Ops:
  7.1 19.3 %collective-permute-start.2 = (bf16[256,1536]{1,0:T(8,128)(2,1)}, bf16[256,1536]{1,0:T(8,128)(2,1)}, u32[]{:S(2)}, u32[]{:S(2)}) collective-permute-start(bf16[256,1536]{1,0:T(8,128)(2,1)} %bitcast.190), channel_id=1, source_target_pairs={{4,0},{5,1},{8,4},{9,5},{12,8},{13,9},{14,12},{15,13},{10,14},{11,... | collective-permute-start | bytes 2359304 | tf_op jit(solution)/shard_map/ppermute | solution.py:449
  8.6 19.0 %collective-permute-start.1 = (bf16[256,1536]{1,0:T(8,128)(2,1)}, bf16[256,1536]{1,0:T(8,128)(2,1)}, u32[]{:S(2)}, u32[]{:S(2)}) collective-permute-start(bf16[256,1536]{1,0:T(8,128)(2,1)} %bitcast.191), channel_id=1, source_target_pairs={{0,4},{1,5},{4,8},{5,9},{8,12},{9,13},{12,14},{13,15},{14,10},{15,... | collective-permute-start | bytes 2359304 | tf_op jit(solution)/shard_map/ppermute | solution.py:446
  15.4 52.5 %collective-permute-start.9 = (bf16[768,1536]{1,0:T(8,128)(2,1)S(1)}, bf16[768,1536]{1,0:T(8,128)(2,1)S(1)}, u32[]{:S(2)}, u32[]{:S(2)}) collective-permute-start(bf16[768,1536]{1,0:T(8,128)(2,1)S(1)} %pad_maximum_fusion.3), channel_id=1, source_target_pairs={{0,16},{16,0},{1,17},{17,1},{2,18},{18,2},{3,19},{19,3},{4,20},{20... | collective-permute-start | bytes 7077896 | tf_op jit(solution)/shard_map/ppermute | solution.py:557
  78.7 29.0 %collective-permute-start.23 = (bf16[384,1536]{1,0:T(8,128)(2,1)S(1)}, bf16[384,1536]{1,0:T(8,128)(2,1)}, u32[]{:S(2)}, u32[]{:S(2)}) collective-permute-start(bf16[384,1536]{1,0:T(8,128)(2,1)S(1)} %bitcast.184), channel_id=1, source_target_pairs={{0,16},{16,0},{1,17},{17,1},{2,18},{18,2},{3,19},{19,3},{4,20},{20... | collective-permute-start | bytes 3538952 | tf_op jit(solution)/shard_map/ppermute | solution.py:557
  89.2 19.9 %collective-permute-start.21 = (bf16[256,1536]{1,0:T(8,128)(2,1)}, bf16[256,1536]{1,0:T(8,128)(2,1)}, u32[]{:S(2)}, u32[]{:S(2)}) collective-permute-start(bf16[256,1536]{1,0:T(8,128)(2,1)} %collective-permute-done.1.refs_2_), channel_id=1, source_target_pairs={{0,4},{1,5},{4,8},{5,9},{8,12},{9,13},{12,14},{13,15},{14,10},{15,... | collective-permute-start | bytes 2359304 | tf_op jit(solution)/shard_map/ppermute | solution.py:446
  90.8 19.6 %collective-permute-start.22 = (bf16[256,1536]{1,0:T(8,128)(2,1)}, bf16[256,1536]{1,0:T(8,128)(2,1)}, u32[]{:S(2)}, u32[]{:S(2)}) collective-permute-start(bf16[256,1536]{1,0:T(8,128)(2,1)} %collective-permute-done.2.refs_4_), channel_id=1, source_target_pairs={{4,0},{5,1},{8,4},{9,5},{12,8},{13,9},{14,12},{15,13},{10,14},{11,... | collective-permute-start | bytes 2359304 | tf_op jit(solution)/shard_map/ppermute | solution.py:449
  110.4 38.1 %collective-permute-start.28 = (bf16[528,1536]{1,0:T(8,128)(2,1)S(1)}, bf16[528,1536]{1,0:T(8,128)(2,1)S(1)}, u32[]{:S(2)}, u32[]{:S(2)}) collective-permute-start(bf16[528,1536]{1,0:T(8,128)(2,1)S(1)} %pad_maximum_fusion.4), channel_id=1, source_target_pairs={{0,1},{1,0},{2,3},{3,2},{4,5},{5,4},{6,7},{7,6},{8,9},{9,8},{10,11... | collective-permute-start | bytes 4866056 | tf_op jit(solution)/shard_map/ppermute | solution.py:452
  110.4 21.4 %collective-permute-start.25 = (bf16[272,1536]{1,0:T(8,128)(2,1)S(1)}, bf16[272,1536]{1,0:T(8,128)(2,1)S(1)}, u32[]{:S(2)}, u32[]{:S(2)}) collective-permute-start(bf16[272,1536]{1,0:T(8,128)(2,1)S(1)} %copy-done.11), channel_id=1, source_target_pairs={{4,0},{5,1},{8,4},{9,5},{12,8},{13,9},{14,12},{15,13},{10,14},{11,... | collective-permute-start | bytes 2506760 | tf_op jit(solution)/shard_map/ppermute | solution.py:449
  110.9 21.4 %collective-permute-start.24 = (bf16[272,1536]{1,0:T(8,128)(2,1)S(1)}, bf16[272,1536]{1,0:T(8,128)(2,1)S(1)}, u32[]{:S(2)}, u32[]{:S(2)}) collective-permute-start(bf16[272,1536]{1,0:T(8,128)(2,1)S(1)} %copy-done.11), channel_id=1, source_target_pairs={{0,4},{1,5},{4,8},{5,9},{8,12},{9,13},{12,14},{13,15},{14,10},{15,... | collective-permute-start | bytes 2506760 | tf_op jit(solution)/shard_map/ppermute | solution.py:446
  112.4 36.0 %collective-permute-start.26 = (bf16[256,1536]{1,0:T(8,128)(2,1)}, bf16[256,1536]{1,0:T(8,128)(2,1)S(1)}, u32[]{:S(2)}, u32[]{:S(2)}) collective-permute-start(bf16[256,1536]{1,0:T(8,128)(2,1)} %collective-permute-done.21.refs_2_), channel_id=1, source_target_pairs={{0,4},{1,5},{4,8},{5,9},{8,12},{9,13},{12,14},{13,15},{14,10},{15,... | collective-permute-start | bytes 2359304 | tf_op jit(solution)/shard_map/ppermute | solution.py:446
  114.0 34.5 %collective-permute-start.27 = (bf16[256,1536]{1,0:T(8,128)(2,1)}, bf16[256,1536]{1,0:T(8,128)(2,1)S(1)}, u32[]{:S(2)}, u32[]{:S(2)}) collective-permute-start(bf16[256,1536]{1,0:T(8,128)(2,1)} %collective-permute-done.22.refs_4_), channel_id=1, source_target_pairs={{4,0},{5,1},{8,4},{9,5},{12,8},{13,9},{14,12},{15,13},{10,14},{11,... | collective-permute-start | bytes 2359304 | tf_op jit(solution)/shard_map/ppermute | solution.py:449
  148.5 30.7 %collective-permute-start.33 = (bf16[1056,1536]{1,0:T(8,128)(2,1)}, bf16[1056,1536]{1,0:T(8,128)(2,1)S(1)}, u32[]{:S(2)}, u32[]{:S(2)}) collective-permute-start(bf16[1056,1536]{1,0:T(8,128)(2,1)} %pad_maximum_fusion), channel_id=1, source_target_pairs={{0,1},{1,0},{2,3},{3,2},{4,5},{5,4},{6,7},{7,6},{8,9},{9,8},{10,11... | collective-permute-start | bytes 9732104 | tf_op jit(solution)/shard_map/ppermute | solution.py:452
  148.5 21.4 %collective-permute-start.29 = (bf16[272,1536]{1,0:T(8,128)(2,1)S(1)}, bf16[272,1536]{1,0:T(8,128)(2,1)S(1)}, u32[]{:S(2)}, u32[]{:S(2)}) collective-permute-start(bf16[272,1536]{1,0:T(8,128)(2,1)S(1)} %collective-permute-done.24.refs_1_), channel_id=1, source_target_pairs={{0,4},{1,5},{4,8},{5,9},{8,12},{9,13},{12,14},{13,15},{14,10},{15,... | collective-permute-start | bytes 2506760 | tf_op jit(solution)/shard_map/ppermute | solution.py:446
  150.1 21.4 %collective-permute-start.30 = (bf16[272,1536]{1,0:T(8,128)(2,1)S(1)}, bf16[272,1536]{1,0:T(8,128)(2,1)S(1)}, u32[]{:S(2)}, u32[]{:S(2)}) collective-permute-start(bf16[272,1536]{1,0:T(8,128)(2,1)S(1)} %collective-permute-done.25.refs_3_), channel_id=1, source_target_pairs={{4,0},{5,1},{8,4},{9,5},{12,8},{13,9},{14,12},{15,13},{10,14},{11,... | collective-permute-start | bytes 2506760 | tf_op jit(solution)/shard_map/ppermute | solution.py:449
  150.6 28.6 %collective-permute-start.32 = (bf16[128,1536]{1,0:T(8,128)(2,1)S(1)}, bf16[128,1536]{1,0:T(8,128)(2,1)S(1)}, u32[]{:S(2)}, u32[]{:S(2)}) collective-permute-start(bf16[128,1536]{1,0:T(8,128)(2,1)S(1)} %slice.159), channel_id=1, source_target_pairs={{4,0},{5,1},{8,4},{9,5},{12,8},{13,9},{14,12},{15,13},{10,14},{11,... | collective-permute-start | bytes 1179656 | tf_op jit(solution)/shard_map/ppermute | solution.py:449
  152.2 26.9 %collective-permute-start.31 = (bf16[128,1536]{1,0:T(8,128)(2,1)S(1)}, bf16[128,1536]{1,0:T(8,128)(2,1)S(1)}, u32[]{:S(2)}, u32[]{:S(2)}) collective-permute-start(bf16[128,1536]{1,0:T(8,128)(2,1)S(1)} %slice.158), channel_id=1, source_target_pairs={{0,4},{1,5},{4,8},{5,9},{8,12},{9,13},{12,14},{13,15},{14,10},{15,... | collective-permute-start | bytes 1179656 | tf_op jit(solution)/shard_map/ppermute | solution.py:446
  179.2 24.3 %collective-permute-start.36 = (bf16[1056,1536]{1,0:T(8,128)(2,1)}, bf16[1056,1536]{1,0:T(8,128)(2,1)}, u32[]{:S(2)}, u32[]{:S(2)}) collective-permute-start(bf16[1056,1536]{1,0:T(8,128)(2,1)} %pad_maximum_fusion.1), channel_id=1, source_target_pairs={{0,1},{1,0},{2,3},{3,2},{4,5},{5,4},{6,7},{7,6},{8,9},{9,8},{10,11... | collective-permute-start | bytes 9732104 | tf_op jit(solution)/shard_map/ppermute | solution.py:452
  179.3 21.0 %collective-permute-start.34 = (bf16[272,1536]{1,0:T(8,128)(2,1)S(1)}, bf16[272,1536]{1,0:T(8,128)(2,1)S(1)}, u32[]{:S(2)}, u32[]{:S(2)}) collective-permute-start(bf16[272,1536]{1,0:T(8,128)(2,1)S(1)} %collective-permute-done.29.refs_1_), channel_id=1, source_target_pairs={{0,4},{1,5},{4,8},{5,9},{8,12},{9,13},{12,14},{13,15},{14,10},{15,... | collective-permute-start | bytes 2506760 | tf_op jit(solution)/shard_map/ppermute | solution.py:446
  181.0 20.6 %collective-permute-start.35 = (bf16[272,1536]{1,0:T(8,128)(2,1)S(1)}, bf16[272,1536]{1,0:T(8,128)(2,1)S(1)}, u32[]{:S(2)}, u32[]{:S(2)}) collective-permute-start(bf16[272,1536]{1,0:T(8,128)(2,1)S(1)} %collective-permute-done.30.refs_3_), channel_id=1, source_target_pairs={{4,0},{5,1},{8,4},{9,5},{12,8},{13,9},{14,12},{15,13},{10,14},{11,... | collective-permute-start | bytes 2506760 | tf_op jit(solution)/shard_map/ppermute | solution.py:449
  203.5 18.6 %collective-permute-start.39 = (bf16[1056,1536]{1,0:T(8,128)(2,1)}, bf16[1056,1536]{1,0:T(8,128)(2,1)}, u32[]{:S(2)}, u32[]{:S(2)}) collective-permute-start(bf16[1056,1536]{1,0:T(8,128)(2,1)} %pad_maximum_fusion.2), channel_id=1, source_target_pairs={{0,1},{1,0},{2,3},{3,2},{4,5},{5,4},{6,7},{7,6},{8,9},{9,8},{10,11... | collective-permute-start | bytes 9732104 | tf_op jit(solution)/shard_map/ppermute | solution.py:452
  203.6 18.4 %collective-permute-start.38 = (bf16[144,1536]{1,0:T(8,128)(2,1)S(1)}, bf16[144,1536]{1,0:T(8,128)(2,1)S(1)}, u32[]{:S(2)}, u32[]{:S(2)}) collective-permute-start(bf16[144,1536]{1,0:T(8,128)(2,1)S(1)} %slice.161), channel_id=1, source_target_pairs={{4,0},{5,1},{8,4},{9,5},{12,8},{13,9},{14,12},{15,13},{10,14},{11,... | collective-permute-start | bytes 1327112 | tf_op jit(solution)/shard_map/ppermute | solution.py:449
  204.1 17.8 %collective-permute-start.37 = (bf16[128,1536]{1,0:T(8,128)(2,1)S(1)}, bf16[128,1536]{1,0:T(8,128)(2,1)S(1)}, u32[]{:S(2)}, u32[]{:S(2)}) collective-permute-start(bf16[128,1536]{1,0:T(8,128)(2,1)S(1)} %slice.160), channel_id=1, source_target_pairs={{0,4},{1,5},{4,8},{5,9},{8,12},{9,13},{12,14},{13,15},{14,10},{15,... | collective-permute-start | bytes 1179656 | tf_op jit(solution)/shard_map/ppermute | solution.py:446
  257.1 21.4 %collective-permute-start.45 = (bf16[2,272,1536]{2,1,0:T(8,128)(2,1)}, bf16[2,272,1536]{2,1,0:T(8,128)(2,1)S(1)}, u32[]{:S(2)}, u32[]{:S(2)}) collective-permute-start(bf16[2,272,1536]{2,1,0:T(8,128)(2,1)} %copy-done.108), channel_id=1, source_target_pairs={{0,1},{1,0},{2,3},{3,2},{4,5},{5,4},{6,7},{7,6},{8,9},{9,8},{10,11... | collective-permute-start | bytes 5013512 | tf_op jit(solution)/shard_map/ppermute | solution.py:452
  257.3 20.9 %collective-permute-start.47 = (bf16[272,1536]{1,0:T(8,128)(2,1)S(1)}, bf16[272,1536]{1,0:T(8,128)(2,1)S(1)}, u32[]{:S(2)}, u32[]{:S(2)}) collective-permute-start(bf16[272,1536]{1,0:T(8,128)(2,1)S(1)} %get-tuple-element.483), channel_id=1, source_target_pairs={{4,0},{5,1},{8,4},{9,5},{12,8},{13,9},{14,12},{15,13},{10,14},{11,... | collective-permute-start | bytes 2506760 | tf_op jit(solution)/shard_map/ppermute | solution.py:449
  257.8 20.8 %collective-permute-start.46 = (bf16[272,1536]{1,0:T(8,128)(2,1)S(1)}, bf16[272,1536]{1,0:T(8,128)(2,1)S(1)}, u32[]{:S(2)}, u32[]{:S(2)}) collective-permute-start(bf16[272,1536]{1,0:T(8,128)(2,1)S(1)} %get-tuple-element.484), channel_id=1, source_target_pairs={{0,4},{1,5},{4,8},{5,9},{8,12},{9,13},{12,14},{13,15},{14,10},{15,... | collective-permute-start | bytes 2506760 | tf_op jit(solution)/shard_map/ppermute | solution.py:446
  280.0 22.3 %collective-permute-start.48 = (bf16[2,272,1536]{2,1,0:T(8,128)(2,1)S(1)}, bf16[2,272,1536]{2,1,0:T(8,128)(2,1)S(1)}, u32[]{:S(2)}, u32[]{:S(2)}) collective-permute-start(bf16[2,272,1536]{2,1,0:T(8,128)(2,1)S(1)} %copy-done.107), channel_id=1, source_target_pairs={{0,1},{1,0},{2,3},{3,2},{4,5},{5,4},{6,7},{7,6},{8,9},{9,8},{10,11... | collective-permute-start | bytes 5013512 | tf_op jit(solution)/shard_map/ppermute | solution.py:452
  280.0 21.0 %collective-permute-start.49 = (bf16[272,1536]{1,0:T(8,128)(2,1)S(1)}, bf16[272,1536]{1,0:T(8,128)(2,1)S(1)}, u32[]{:S(2)}, u32[]{:S(2)}) collective-permute-start(bf16[272,1536]{1,0:T(8,128)(2,1)S(1)} %get-tuple-element.380), channel_id=1, source_target_pairs={{0,4},{1,5},{4,8},{5,9},{8,12},{9,13},{12,14},{13,15},{14,10},{15,... | collective-permute-start | bytes 2506760 | tf_op jit(solution)/shard_map/ppermute | solution.py:446
  281.6 20.7 %collective-permute-start.50 = (bf16[272,1536]{1,0:T(8,128)(2,1)S(1)}, bf16[272,1536]{1,0:T(8,128)(2,1)S(1)}, u32[]{:S(2)}, u32[]{:S(2)}) collective-permute-start(bf16[272,1536]{1,0:T(8,128)(2,1)S(1)} %get-tuple-element.381), channel_id=1, source_target_pairs={{4,0},{5,1},{8,4},{9,5},{12,8},{13,9},{14,12},{15,13},{10,14},{11,... | collective-permute-start | bytes 2506760 | tf_op jit(solution)/shard_map/ppermute | solution.py:449
  282.0 21.5 %collective-permute-start.51 = (bf16[288,1536]{1,0:T(8,128)(2,1)S(1)}, bf16[288,1536]{1,0:T(8,128)(2,1)S(1)}, u32[]{:S(2)}, u32[]{:S(2)}) collective-permute-start(bf16[288,1536]{1,0:T(8,128)(2,1)S(1)} %get-tuple-element.379), channel_id=1, source_target_pairs={{0,16},{16,0},{1,17},{17,1},{2,18},{18,2},{3,19},{19,3},{4,20},{20... | collective-permute-start | bytes 2654216 | tf_op jit(solution)/shard_map/ppermute | solution.py:557
  303.5 22.1 %collective-permute-start.55 = (bf16[288,1536]{1,0:T(8,128)(2,1)S(1)}, bf16[288,1536]{1,0:T(8,128)(2,1)S(1)}, u32[]{:S(2)}, u32[]{:S(2)}) collective-permute-start(bf16[288,1536]{1,0:T(8,128)(2,1)S(1)} %get-tuple-element.388), channel_id=1, source_target_pairs={{0,16},{16,0},{1,17},{17,1},{2,18},{18,2},{3,19},{19,3},{4,20},{20... | collective-permute-start | bytes 2654216 | tf_op jit(solution)/shard_map/ppermute | solution.py:557
  304.2 22.4 %collective-permute-start.53 = (bf16[272,1536]{1,0:T(8,128)(2,1)S(1)}, bf16[272,1536]{1,0:T(8,128)(2,1)S(1)}, u32[]{:S(2)}, u32[]{:S(2)}) collective-permute-start(bf16[272,1536]{1,0:T(8,128)(2,1)S(1)} %get-tuple-element.384), channel_id=1, source_target_pairs={{0,4},{1,5},{4,8},{5,9},{8,12},{9,13},{12,14},{13,15},{14,10},{15,... | collective-permute-start | bytes 2506760 | tf_op jit(solution)/shard_map/ppermute | solution.py:446
  305.7 20.8 %collective-permute-start.54 = (bf16[272,1536]{1,0:T(8,128)(2,1)S(1)}, bf16[272,1536]{1,0:T(8,128)(2,1)S(1)}, u32[]{:S(2)}, u32[]{:S(2)}) collective-permute-start(bf16[272,1536]{1,0:T(8,128)(2,1)S(1)} %get-tuple-element.385), channel_id=1, source_target_pairs={{4,0},{5,1},{8,4},{9,5},{12,8},{13,9},{14,12},{15,13},{10,14},{11,... | collective-permute-start | bytes 2506760 | tf_op jit(solution)/shard_map/ppermute | solution.py:449
  329.4 17.1 %collective-permute-start.60 = (bf16[224,1536]{1,0:T(8,128)(2,1)}, bf16[224,1536]{1,0:T(8,128)(2,1)S(1)}, u32[]{:S(2)}, u32[]{:S(2)}) collective-permute-start(bf16[224,1536]{1,0:T(8,128)(2,1)} %get-tuple-element.404), channel_id=1, source_target_pairs={{0,16},{16,0},{1,17},{17,1},{2,18},{18,2},{3,19},{19,3},{4,20},{20... | collective-permute-start | bytes 2064392 | tf_op jit(solution)/shard_map/ppermute | solution.py:557
  347.4 28.0 %collective-permute-start.65 = (bf16[2,8,48,1536]{3,2,1,0:T(8,128)(2,1)}, bf16[2,8,48,1536]{3,2,1,0:T(8,128)(2,1)}, u32[]{:S(2)}, u32[]{:S(2)}) collective-permute-start(bf16[2,8,48,1536]{3,2,1,0:T(8,128)(2,1)} %get-tuple-element.422), channel_id=1, source_target_pairs={{0,1},{1,0},{2,3},{3,2},{4,5},{5,4},{6,7},{7,6},{8,9},{9,8},{10,11... | collective-permute-start | bytes 7077896 | tf_op jit(solution)/shard_map/ppermute | solution.py:452
  347.4 21.6 %collective-permute-start.61 = (bf16[2,256,1536]{2,1,0:T(8,128)(2,1)}, bf16[2,256,1536]{2,1,0:T(8,128)(2,1)}, u32[]{:S(2)}, u32[]{:S(2)}) collective-permute-start(bf16[2,256,1536]{2,1,0:T(8,128)(2,1)} %get-tuple-element.407), channel_id=1, source_target_pairs={{0,1},{1,0},{2,3},{3,2},{4,5},{5,4},{6,7},{7,6},{8,9},{9,8},{10,11... | collective-permute-start | bytes 4718600 | tf_op jit(solution)/shard_map/ppermute | solution.py:452
  347.9 19.8 %collective-permute-start.62 = (bf16[256,1536]{1,0:T(8,128)(2,1)}, bf16[256,1536]{1,0:T(8,128)(2,1)}, u32[]{:S(2)}, u32[]{:S(2)}) collective-permute-start(bf16[256,1536]{1,0:T(8,128)(2,1)} %get-tuple-element.405), channel_id=1, source_target_pairs={{0,4},{1,5},{4,8},{5,9},{8,12},{9,13},{12,14},{13,15},{14,10},{15,... | collective-permute-start | bytes 2359304 | tf_op jit(solution)/shard_map/ppermute | solution.py:446
  349.4 19.5 %collective-permute-start.63 = (bf16[256,1536]{1,0:T(8,128)(2,1)}, bf16[256,1536]{1,0:T(8,128)(2,1)}, u32[]{:S(2)}, u32[]{:S(2)}) collective-permute-start(bf16[256,1536]{1,0:T(8,128)(2,1)} %get-tuple-element.406), channel_id=1, source_target_pairs={{4,0},{5,1},{8,4},{9,5},{12,8},{13,9},{14,12},{15,13},{10,14},{11,... | collective-permute-start | bytes 2359304 | tf_op jit(solution)/shard_map/ppermute | solution.py:449
  349.9 25.4 %collective-permute-start.64 = (bf16[352,1536]{1,0:T(8,128)(2,1)}, bf16[352,1536]{1,0:T(8,128)(2,1)S(1)}, u32[]{:S(2)}, u32[]{:S(2)}) collective-permute-start(bf16[352,1536]{1,0:T(8,128)(2,1)} %get-tuple-element.420), channel_id=1, source_target_pairs={{0,16},{16,0},{1,17},{17,1},{2,18},{18,2},{3,19},{19,3},{4,20},{20... | collective-permute-start | bytes 3244040 | tf_op jit(solution)/shard_map/ppermute | solution.py:557
  375.3 35.3 %collective-permute-start.70 = (bf16[2,8,48,2176]{3,2,1,0:T(8,128)(2,1)}, bf16[2,8,48,2176]{3,2,1,0:T(8,128)(2,1)}, u32[]{:S(2)}, u32[]{:S(2)}) collective-permute-start(bf16[2,8,48,2176]{3,2,1,0:T(8,128)(2,1)} %copy-done.105), channel_id=1, source_target_pairs={{0,1},{1,0},{2,3},{3,2},{4,5},{5,4},{6,7},{7,6},{8,9},{9,8},{10,11... | collective-permute-start | bytes 10027016 | tf_op jit(solution)/shard_map/ppermute | solution.py:452
  377.1 28.5 %collective-permute-start.69 = (bf16[8,48,1536]{2,1,0:T(8,128)(2,1)S(1)}, bf16[8,48,1536]{2,1,0:T(8,128)(2,1)}, u32[]{:S(2)}, u32[]{:S(2)}) collective-permute-start(bf16[8,48,1536]{2,1,0:T(8,128)(2,1)S(1)} %fusion.32), channel_id=1, source_target_pairs={{0,16},{16,0},{1,17},{17,1},{2,18},{18,2},{3,19},{19,3},{4,20},{20... | collective-permute-start | bytes 3538952 | tf_op jit(solution)/shard_map/ppermute | solution.py:557
  378.2 29.6 %collective-permute-start.66 = (bf16[2,256,1536]{2,1,0:T(8,128)(2,1)}, bf16[2,256,1536]{2,1,0:T(8,128)(2,1)S(1)}, u32[]{:S(2)}, u32[]{:S(2)}) collective-permute-start(bf16[2,256,1536]{2,1,0:T(8,128)(2,1)} %get-tuple-element.425), channel_id=1, source_target_pairs={{0,1},{1,0},{2,3},{3,2},{4,5},{5,4},{6,7},{7,6},{8,9},{9,8},{10,11... | collective-permute-start | bytes 4718600 | tf_op jit(solution)/shard_map/ppermute | solution.py:452
  378.4 29.3 %collective-permute-start.67 = (bf16[256,1536]{1,0:T(8,128)(2,1)}, bf16[256,1536]{1,0:T(8,128)(2,1)S(1)}, u32[]{:S(2)}, u32[]{:S(2)}) collective-permute-start(bf16[256,1536]{1,0:T(8,128)(2,1)} %get-tuple-element.423), channel_id=1, source_target_pairs={{0,4},{1,5},{4,8},{5,9},{8,12},{9,13},{12,14},{13,15},{14,10},{15,... | collective-permute-start | bytes 2359304 | tf_op jit(solution)/shard_map/ppermute | solution.py:446
  379.8 28.0 %collective-permute-start.68 = (bf16[256,1536]{1,0:T(8,128)(2,1)}, bf16[256,1536]{1,0:T(8,128)(2,1)}, u32[]{:S(2)}, u32[]{:S(2)}) collective-permute-start(bf16[256,1536]{1,0:T(8,128)(2,1)} %get-tuple-element.424), channel_id=1, source_target_pairs={{4,0},{5,1},{8,4},{9,5},{12,8},{13,9},{14,12},{15,13},{10,14},{11,... | collective-permute-start | bytes 2359304 | tf_op jit(solution)/shard_map/ppermute | solution.py:449
  412.5 38.2 %collective-permute-start.74 = (bf16[8,48,2176]{2,1,0:T(8,128)(2,1)S(1)}, bf16[8,48,2176]{2,1,0:T(8,128)(2,1)S(1)}, u32[]{:S(2)}, u32[]{:S(2)}) collective-permute-start(bf16[8,48,2176]{2,1,0:T(8,128)(2,1)S(1)} %fusion.2), channel_id=1, source_target_pairs={{0,16},{16,0},{1,17},{17,1},{2,18},{18,2},{3,19},{19,3},{4,20},{20... | collective-permute-start | bytes 5013512 | tf_op jit(solution)/shard_map/ppermute | solution.py:557
  420.4 33.4 %collective-permute-start.72 = (bf16[256,1536]{1,0:T(8,128)(2,1)S(1)}, bf16[256,1536]{1,0:T(8,128)(2,1)S(1)}, u32[]{:S(2)}, u32[]{:S(2)}) collective-permute-start(bf16[256,1536]{1,0:T(8,128)(2,1)S(1)} %get-tuple-element.433), channel_id=1, source_target_pairs={{0,4},{1,5},{4,8},{5,9},{8,12},{9,13},{12,14},{13,15},{14,10},{15,... | collective-permute-start | bytes 2359304 | tf_op jit(solution)/shard_map/ppermute | solution.py:446
  421.8 32.0 %collective-permute-start.73 = (bf16[256,1536]{1,0:T(8,128)(2,1)S(1)}, bf16[256,1536]{1,0:T(8,128)(2,1)S(1)}, u32[]{:S(2)}, u32[]{:S(2)}) collective-permute-start(bf16[256,1536]{1,0:T(8,128)(2,1)S(1)} %get-tuple-element.434), channel_id=1, source_target_pairs={{4,0},{5,1},{8,4},{9,5},{12,8},{13,9},{14,12},{15,13},{10,14},{11,... | collective-permute-start | bytes 2359304 | tf_op jit(solution)/shard_map/ppermute | solution.py:449
  422.4 55.9 %collective-permute-start.71 = (bf16[1,256,1536]{2,1,0:T(8,128)(2,1)S(1)}, bf16[1,256,1536]{2,1,0:T(8,128)(2,1)S(1)}, u32[]{:S(2)}, u32[]{:S(2)}) collective-permute-start(bf16[1,256,1536]{2,1,0:T(8,128)(2,1)S(1)} %copy-done.112), channel_id=1, source_target_pairs={{0,1},{1,0},{2,3},{3,2},{4,5},{5,4},{6,7},{7,6},{8,9},{9,8},{10,11... | collective-permute-start | bytes 2359304 | tf_op jit(solution)/shard_map/ppermute | solution.py:452
  425.8 30.0 %collective-permute-start.84 = (bf16[48,1536]{1,0:T(8,128)(2,1)S(1)}, bf16[48,1536]{1,0:T(8,128)(2,1)S(1)}, u32[]{:S(2)}, u32[]{:S(2)}) collective-permute-start(bf16[48,1536]{1,0:T(8,128)(2,1)S(1)} %get-tuple-element.493), channel_id=1, source_target_pairs={{0,4},{1,5},{4,8},{5,9},{8,12},{9,13},{12,14},{13,15},{14,10},{15,... | collective-permute-start | bytes 442376 | tf_op jit(solution)/shard_map/ppermute | solution.py:446
  (178 other events, 2168.2 us)
